TPU v7x, 768 devices: a whole 4x8x12 slice. The times are simulated.
768 devices in a mesh: group: 12 (over z), member: 4 (over x), dp: 16 (over y, core).
Axes of the slice: x: 4, y: 8, z: 12, core: 2. Of those that a mesh axis runs over, the one named last changes fastest.
Arguments:
- tokens_in: bfloat16 [4608, 5120], P(('group', 'member')), may hold values from -6 to 6
- out_grad: bfloat16 [4608, 5120], P(('group', 'member')), may hold values from -6 to 6
- scores: bfloat16 [4608, 6], P(('group', 'member')), may hold values from 0.049804688 to 0.5
- expert_ids: int32 [4608, 6], P(('group', 'member')), may hold values from 0 to 95, as said below
- w_in: bfloat16 [192, 2, 384, 5120], P(('group', 'dp'), None, 'member'), may hold values from -0.078125 to 0.078125
- w_down: bfloat16 [192, 384, 5120], P(('group', 'dp'), 'member'), may hold values from -0.21875 to 0.21875
Outputs:
- grad_in: bfloat16 [4608, 5120], P(('group', 'member'), 'dp')
Inputs may be any that keep to these rules, and one draw needn't show every extreme that they name: `expert_ids`: expert E lies in group E // 8. Take the tokens in aligned blocks of 96 (the tokens of one index of group and member). A token's 6 ids name 3 distinct groups, 2 distinct experts in each. Within a block every group is picked by exactly 24 tokens, no expert by more than 6 tokens, and some expert by exactly 6.
All inputs are finite; a program needn't handle non-finite values.
Results may differ from a plain program's by a relative error of at most 0.015.
Values may be sent and summed in bfloat16 or wider, within the bound.
No kernel may reach another device: no remote copies, remote signals or barrier semaphores. Data moves between devices by JAX's collectives and lax.ppermute only.
A program may use at most 32 MiB of HBM per device.

v0:
```python
import jax
import jax.numpy as jnp
from jax import lax
from jax.sharding import PartitionSpec as P

TGROUPS = 3


def per_device(tokens_in, out_grad, scores, expert_ids, w_in, w_down):
    group_count = lax.axis_size("group")
    dp_count = lax.axis_size("dp")
    split_count = max(1, min(2, dp_count // 4))
    per_group = dp_count // split_count
    tok_rows, model_width = tokens_in.shape
    pick_width = expert_ids.shape[1]
    pair_count = pick_width // TGROUPS
    group_rows = TGROUPS * tok_rows // group_count
    capacity = max(2, (pair_count * group_rows + per_group - 1) // per_group)
    slot_total = group_count * capacity
    my_column = lax.axis_index("dp") // split_count
    column_of = expert_ids % per_group
    group_of = expert_ids // per_group
    group_flat = jnp.where(column_of == my_column, group_of, -1).reshape(-1)
    group_hot = (group_flat[:, None] == jnp.arange(group_count, dtype=jnp.int32)[None, :]).astype(
        jnp.int32
    )
    rank_table = jnp.cumsum(group_hot, axis=0) - group_hot
    pick_rank = jnp.sum(rank_table * group_hot, axis=1)
    slot_of = jnp.where(group_flat >= 0, group_flat * capacity + pick_rank, -1)
    slot_hot = (slot_of[:, None] == jnp.arange(slot_total, dtype=jnp.int32)[None, :]).astype(
        jnp.float32
    )
    pick_token = jnp.arange(tok_rows * pick_width, dtype=jnp.int32) // pick_width
    token_hot = (pick_token[:, None] == jnp.arange(tok_rows, dtype=jnp.int32)[None, :]).astype(
        jnp.float32
    )
    contract_first = (((0,), (0,)), ((), ()))
    route = lax.dot_general(slot_hot, token_hot, contract_first, precision=lax.Precision.HIGHEST)
    slot_score = lax.dot_general(
        slot_hot,
        scores.reshape(-1).astype(jnp.float32),
        contract_first,
        precision=lax.Precision.HIGHEST,
    )
    route_bf = route.astype(jnp.bfloat16)
    input_rows = jnp.dot(route_bf, tokens_in, preferred_element_type=jnp.float32).astype(
        jnp.bfloat16
    )
    grad_rows = jnp.dot(route_bf, out_grad, preferred_element_type=jnp.float32)
    scaled_rows = (slot_score[:, None] * grad_rows).astype(jnp.bfloat16)
    packed = jnp.stack([input_rows, scaled_rows])
    arrived = lax.all_to_all(packed, "group", split_axis=1, concat_axis=1, tiled=True)
    w_pair = w_in[0].reshape(-1, model_width)
    w_out = w_down[0]
    hidden_local = w_out.shape[0]
    contract_last = (((1,), (1,)), ((), ()))
    gathered = lax.all_gather(arrived, "member", axis=1, tiled=True)
    gate_up = lax.dot_general(
        gathered[0], w_pair, contract_last, preferred_element_type=jnp.float32
    )
    gate_pre = gate_up[:, :hidden_local]
    up_pre = gate_up[:, hidden_local:]
    act_grad = lax.dot_general(
        gathered[1], w_out, contract_last, preferred_element_type=jnp.float32
    )
    sigmoid_gate = jax.nn.sigmoid(gate_pre)
    gate_grad = act_grad * up_pre * sigmoid_gate * (1.0 + gate_pre * (1.0 - sigmoid_gate))
    up_grad = act_grad * gate_pre * sigmoid_gate
    hidden_grads = jnp.concatenate([gate_grad, up_grad], axis=1).astype(jnp.bfloat16)
    partial_value = jnp.dot(hidden_grads, w_pair, preferred_element_type=jnp.float32)
    summed = lax.psum_scatter(
        partial_value.astype(jnp.bfloat16), "member", scatter_dimension=0, tiled=True
    )
    returned = lax.all_to_all(summed, "group", split_axis=0, concat_axis=0, tiled=True)
    token_sums = lax.dot_general(
        route_bf, returned, contract_first, preferred_element_type=jnp.float32
    )
    grad_local = lax.psum_scatter(token_sums, "dp", scatter_dimension=1, tiled=True)
    return grad_local.astype(jnp.bfloat16)


def solution(mesh):
    in_specs = (
        P(("group", "member"), None),
        P(("group", "member"), None),
        P(("group", "member"), None),
        P(("group", "member"), None),
        P(("group", "dp"), None, "member", None),
        P(("group", "dp"), "member", None),
    )
    out_specs = P(("group", "member"), "dp")
    return jax.shard_map(
        per_device, mesh=mesh, in_specs=in_specs, out_specs=out_specs, check_vma=False
    )
```

profile of v0, /device:TPU:25, one launch (start us, length us, event | category | flops | bytes accessed | tf_op | source)
XLA Modules:
  0.0 324.3 jit_solution(2517259863993379078)
XLA Ops:
  6.5 0.0 copy-start
  6.5 0.0 copy-start.1
  6.5 0.0 all-gather.2.cloned.1.call-start
  6.5 0.9 copy.19
  7.5 0.1 reshape.52
  7.7 0.7 fusion.18
  8.4 0.1 copy.16
  8.5 0.1 reshape.47
  8.7 1.4 reduce-window.6
  10.1 0.3 slice_reduce_fusion
  10.4 0.0 copy-start.2
  10.4 0.1 broadcast_add_fusion
  10.6 0.3 convolution_bitcast_fusion.1
  10.8 0.4 convolution_convert_fusion.2
  11.3 0.0 copy-done.1
  11.3 0.3 fusion.1
  11.6 0.0 copy-done.2
  11.6 0.3 fusion.2
  12.0 0.1 pad_maximum_fusion
  12.1 1.5 copy.20
  13.6 68.4 %all_to_all.17 = bf16[2,72,5120]{2,0,1:T(2,128)(2,1)S(1)} all-to-all(bf16[2,72,5120]{2,0,1:T(2,128)(2,1)S(1)} %copy.20), channel_id=1, replica_groups=mesh['group'=12,'member'=4,'dp'=16] {'group'}, dimensions={1} | all-to-all | bytes 2949120 | tf_op jit(solution)/shard_map/all_to_all | solution.py:52
  82.1 1.4 copy.21
  83.5 0.0 all-gather.2.cloned.1.call-update
  83.5 0.0 reduce-scatter.5.cloned.1.call-start
  83.6 66.5 %all-gather.2.cloned.1.call-done = bf16[2,288,5120]{2,1,0:T(8,128)(2,1)} async-done(((bf16[2,72,5120]{2,1,0:T(8,128)(2,1)}), bf16[2,288,5120]{2,1,0:T(8,128)(2,1)}) %all-gather.2.cloned.1.call-update) | async-done | bytes 5898256 | tf_op jit(solution)/shard_map/all_gather | solution.py:57
  150.1 0.0 copy-done
  150.1 0.0 copy-start.3
  150.1 0.0 copy-start.4
  150.1 3.4 %fusion.3 = f32[288,192]{0,1:T(8,128)S(1)} fusion(bf16[192,5120]{1,0:T(8,128)(2,1)S(1)} %bitcast.38, bf16[2,288,5120]{2,1,0:T(8,128)(2,1)} %all-gather.2.cloned.1.call-done), kind=kOutput, calls=%fused_computation.8 | convolution fusion | flops 566231040 | bytes 5136384 | tf_op jit(solution)/shard_map/dot_general | solution.py:58
  153.5 0.1 copy-done.3
  153.7 0.2 copy-done.4
  153.9 1.2 fusion.8
  155.1 2.6 convolution_convert_fusion
  157.7 0.0 reduce-scatter.5.cloned.1.call-update
  157.7 0.0 reduce-scatter.7.cloned.1.call-start
  157.8 45.6 %reduce-scatter.5.cloned.1.call-done = bf16[72,5120]{1,0:T(8,128)(2,1)} async-done(((bf16[288,5120]{1,0:T(8,128)(2,1)}), bf16[72,5120]{1,0:T(8,128)(2,1)}) %reduce-scatter.5.cloned.1.call-update) | async-done | bytes 737296 | tf_op jit(solution)/shard_map/reduce_scatter | solution.py:71
  203.3 1.3 all_to_all.12
  204.7 47.8 %all_to_all.18 = bf16[12,6,5120]{2,1,0:T(8,128)(2,1)} all-to-all(bf16[12,6,5120]{2,1,0:T(8,128)(2,1)S(1)} %all_to_all.12), channel_id=1, replica_groups=mesh['group'=12,'member'=4,'dp'=16] {'group'}, dimensions={0} | all-to-all | bytes 1474560 | tf_op jit(solution)/shard_map/all_to_all | solution.py:74
  252.5 1.4 all_to_all.14
  253.9 2.1 convolution_bitcast_fusion
  256.0 0.0 reduce-scatter.7.cloned.1.call-update
  256.0 60.1 %reduce-scatter.7.cloned.1.call-done = f32[320,96]{1,0:T(8,128)} async-done(((f32[5120,96]{1,0:T(8,128)}), f32[320,96]{1,0:T(8,128)}) %reduce-scatter.7.cloned.1.call-update) | async-done | bytes 122896
  316.1 1.6 copy.23
  (10 shorter events, 0.1 us)
Async XLA Ops:
  6.5 143.6 %copy-start = (bf16[1,2,96,5120]{3,2,1,0:T(8,128)(2,1)S(1)}, bf16[1,2,96,5120]{3,2,1,0:T(8,128)(2,1)}, u32[]{:S(2)}) copy-start(bf16[1,2,96,5120]{3,2,1,0:T(8,128)(2,1)} %param.10) | copy-start | bytes 5898244
  6.5 4.7 %copy-start.1 = (bf16[96,5120]{1,0:T(8,128)(2,1)S(1)}, bf16[96,5120]{1,0:T(8,128)(2,1)}, u32[]{:S(2)}) copy-start(bf16[96,5120]{1,0:T(8,128)(2,1)} %param.6) | copy-start | bytes 2949124
  6.5 143.6 %all-gather.2.cloned.1.call-start = ((), (), s32[]{:S(2)}) async-start(), calls=%async_computation.4 | async-start | bytes 7372800 | tf_op jit(solution)/shard_map/all_gather | solution.py:57
  10.4 1.2 copy-start.2
  83.5 119.8 %reduce-scatter.5.cloned.1.call-start = ((), (), s32[]{:S(2)}) async-start(), calls=%async_computation.5 | async-start | bytes 3686400 | tf_op jit(solution)/shard_map/reduce_scatter | solution.py:71
  150.1 3.6 %copy-start.3 = (bf16[2,288,5120]{2,1,0:T(8,128)(2,1)S(1)}, bf16[2,288,5120]{2,1,0:T(8,128)(2,1)}, u32[]{:S(2)}) copy-start(bf16[2,288,5120]{2,1,0:T(8,128)(2,1)} %all-gather.2.cloned.1.call-done) | copy-start | bytes 17694724
  150.1 3.8 %copy-start.4 = (bf16[1,96,5120]{2,1,0:T(8,128)(2,1)S(1)}, bf16[1,96,5120]{2,1,0:T(8,128)(2,1)}, u32[]{:S(2)}) copy-start(bf16[1,96,5120]{2,1,0:T(8,128)(2,1)} %param.11) | copy-start | bytes 2949124
  157.7 158.4 %reduce-scatter.7.cloned.1.call-start = ((), (), s32[]{:S(2)}) async-start(), calls=%async_computation.6 | async-start | bytes 2785280
Sparse Core Ops, SparseCore 0:
  83.7 66.3 all-gather.1
  157.8 45.4 reduce-scatter.4
  256.2 59.9 reduce-scatter.6
where the time goes:
time: 325 us; the launch traced here: 324 us
  waiting for transfers between devices  172 us (53%)
  blocking collectives  116 us (36%)
  between operations  13.3 us (4%)
  matrix products  10.7 us (3%)
  local copies, waits for them, and re-layouts  9.34 us (3%)
    all_to_all x1, blocking collectives, per_device(): lax.all_to_all(packed, 'group', split_axis=1, concat_axis=1, tiled=True)  68.4 us
    all_gather x1, waiting for transfers between devices, per_device(): gathered = lax.all_gather(arrived, 'member', axis=1, tiled=True)  66.5 us
    unnamed x4, waiting for transfers between devices  60.1 us
    all_to_all x1, blocking collectives, per_device(): lax.all_to_all(summed, 'group', split_axis=0, concat_axis=0, tiled=True)  47.8 us
    reduce_scatter x1, waiting for transfers between devices, per_device(): lax.psum_scatter(partial_value.astype(jnp.bfloat16), 'member', scatter_di...  45.6 us
  transfers between devices with their start and end apart: 3, of which 3 were waited for; matrix products, arithmetic and copies ran while one was open for 0% of the time, Pallas kernels for 0%

commit v1 on v0

v1 whole, which is shorter than its diff:
```python
import jax
import jax.numpy as jnp
from jax import lax
from jax.experimental import pallas as pl
from jax.experimental.pallas import tpu as pltpu
from jax.sharding import Mesh, PartitionSpec as P

TGROUPS = 3
QUARTERS = 4
LANES = 128
INTERPRET = False
F32 = jnp.float32
BF16 = jnp.bfloat16


def iota(shape, dim):
    return lax.broadcasted_iota(jnp.int32, shape, dim)


def call(body, out_shape, *args, scratch=(), smem=0, flops=0):
    specs = [
        pl.BlockSpec(memory_space=pltpu.SMEM if i < smem else pltpu.VMEM) for i in range(len(args))
    ]
    moved = sum(a.size * a.dtype.itemsize for a in args)
    return pl.pallas_call(
        body,
        out_shape=out_shape,
        in_specs=specs,
        out_specs=jax.tree.map(lambda s: pl.BlockSpec(memory_space=pltpu.VMEM), out_shape),
        scratch_shapes=list(scratch),
        compiler_params=pltpu.CompilerParams(vmem_limit_bytes=40 * 1024 * 1024),
        cost_estimate=pl.CostEstimate(flops=flops, bytes_accessed=moved, transcendentals=0),
        interpret=INTERPRET,
    )(*args)


def dot(a, b):
    return jnp.dot(a, b, preferred_element_type=F32)


def dot_last(a, b):
    return lax.dot_general(a, b, (((1,), (1,)), ((), ())), preferred_element_type=F32)


def picked(ids, target):
    hit = jnp.zeros(target.shape, F32)
    for e in range(ids.shape[0]):
        hit += (ids[e : e + 1, :] == target).astype(F32)
    return hit


def before(tokens, lanes):
    return (iota((tokens, lanes), 0) < iota((tokens, lanes), 1) % tokens).astype(BF16)


def slot_matrix(ids, y, groups, per_group, slots):
    tokens = ids.shape[1]
    lanes = QUARTERS * tokens
    rows_each = QUARTERS * slots
    rows = groups * rows_each
    hit = picked(ids, iota((groups, tokens), 0) * per_group + y).astype(BF16)
    same = (iota((tokens, lanes), 0) == iota((tokens, lanes), 1) % tokens).astype(BF16)
    rank = dot(hit, before(tokens, lanes))
    hit4 = dot(hit, same)
    code = jnp.where(hit4 > 0.5, rank, -1.0).astype(BF16)
    expand = (iota((rows, groups), 0) // rows_each == iota((rows, groups), 1)).astype(BF16)
    row = iota((rows, lanes), 0) % rows_each
    spread = dot(expand, code).astype(jnp.int32)
    mark = (spread == row % slots) & (row // slots == iota((rows, lanes), 1) // tokens)
    return mark, expand, same


def stacked_quarters(ref, core, half):
    quarter = half // QUARTERS
    return jnp.concatenate(
        [
            ref[:, pl.ds(pl.multiple_of(core * half + f * quarter, LANES), quarter)]
            for f in range(QUARTERS)
        ],
        axis=0,
    )


def pack_inputs(groups, per_group, slots, info, ids, tokens, out):
    mark, _, _ = slot_matrix(ids[...], info[0], groups, per_group, slots)
    rows = stacked_quarters(tokens, info[1], tokens.shape[1] // 2)
    out[...] = dot(mark.astype(BF16), rows).astype(BF16)


def pack_grads(groups, per_group, slots, info, ids, scores, grads, out):
    ids_now = ids[...]
    mark, expand, same = slot_matrix(ids_now, info[0], groups, per_group, slots)
    tokens = ids_now.shape[1]
    target = iota((groups, tokens), 0) * per_group + info[0]
    score = jnp.zeros((groups, tokens), F32)
    for e in range(ids_now.shape[0]):
        score += jnp.where(ids_now[e : e + 1, :] == target, scores[e : e + 1, :].astype(F32), 0.0)
    wide = dot(expand, dot(score.astype(BF16), same).astype(BF16))
    slot_score = jnp.sum(jnp.where(mark, wide, 0.0), axis=1, keepdims=True)
    rows = stacked_quarters(grads, info[1], grads.shape[1] // 2)
    out[...] = (slot_score * dot(mark.astype(BF16), rows)).astype(BF16)


def group_codes(ids, per_group, groups):
    tokens = ids.shape[1]
    hit = picked(ids // per_group, iota((groups, tokens), 0)) > 0.5
    rank = dot(hit.astype(BF16), before(tokens, tokens))
    return jnp.where(hit, rank, -1.0)


def describe(groups, per_group, slots, rows_group, ids, ranks, gather):
    ids_now = ids[...]
    tokens = ids_now.shape[1]
    experts = groups * per_group
    codes = group_codes(ids_now, per_group, groups).astype(BF16)
    hit = picked(ids_now, iota((experts, tokens), 0)) > 0.5
    order = dot(hit.astype(BF16), before(tokens, tokens))
    widen = (iota((experts, groups), 0) // per_group == iota((experts, groups), 1)).astype(BF16)
    rank = dot(widen, codes)
    lane = iota((experts, LANES), 1)
    result = jnp.zeros((experts, LANES), F32)
    for r in range(slots):
        value = jnp.sum(jnp.where(hit & (order == r), rank, 0.0), axis=1, keepdims=True)
        result += jnp.where(lane == r, value, 0.0)
    ranks[...] = result.astype(jnp.int32)
    rows = groups * rows_group
    expand = (iota((rows, groups), 0) // rows_group == iota((rows, groups), 1)).astype(BF16)
    spread = dot(expand, codes).astype(jnp.int32)
    gather[...] = (spread == iota((rows, tokens), 0) % rows_group).astype(BF16)


def unpack(slots, x, rows):
    piece = 8 * QUARTERS * slots
    each = 8 * slots
    at = iota((piece, piece), 0)
    source = (at % each) // slots * (QUARTERS * slots) + at // each * slots + at % slots
    order = (source == iota((piece, piece), 1)).astype(BF16)
    for i in range(x.shape[0] // piece):
        moved = dot(order, x[i * piece : (i + 1) * piece, :]).astype(BF16)
        for f in range(QUARTERS):
            rows[f, i * each : (i + 1) * each, :] = moved[f * each : (f + 1) * each, :]


def project(slots, info, x, own, other, out, rows):
    unpack(slots, x, rows)
    half = other.shape[1]
    quarter = half // QUARTERS
    width = other.shape[0]
    mine = jnp.zeros((rows.shape[1], width), F32)
    theirs = jnp.zeros((rows.shape[1], width), F32)
    for f in range(QUARTERS):
        begin = pl.multiple_of(info[1] * half + f * quarter, LANES)
        mine += dot_last(rows[f], own[:, pl.ds(begin, quarter)])
        theirs += dot_last(rows[f], other[:, f * quarter : (f + 1) * quarter])
    out[0] = mine
    out[1] = theirs


def backward(pre, pre_far, act, act_far, own, other, out):
    hidden = act.shape[2]
    grads = []
    for s in range(2):
        both = pre[s] + pre_far[1 - s]
        gate, up = both[:, :hidden], both[:, hidden:]
        slope = act[s] + act_far[1 - s]
        sig = jax.nn.sigmoid(gate)
        gate_grad = slope * up * sig * (1.0 + gate * (1.0 - sig))
        up_grad = slope * gate * sig
        grads.append((gate_grad.astype(BF16), up_grad.astype(BF16)))
    step = 640 if out.shape[1] % 640 == 0 else out.shape[1]
    for j in range(out.shape[1] // step):
        at = slice(j * step, (j + 1) * step)
        total = dot(grads[0][0], own[:hidden, at]) + dot(grads[0][1], own[hidden:, at])
        total += dot(grads[1][0], other[:hidden, at]) + dot(grads[1][1], other[hidden:, at])
        out[:, at] = total.astype(BF16)


def windows(chunk, count):
    starts = [chunk * k // LANES * LANES for k in range(count)]
    ends = [-(-(chunk * (k + 1)) // LANES) * LANES for k in range(count)]
    return starts, max(e - s for s, e in zip(starts, ends))


def add_members(starts, width, x, out):
    for k, begin in enumerate(starts):
        at = slice(begin, begin + width)
        total = x[0, :, at].astype(F32)
        for m in range(1, x.shape[0]):
            total += x[m, :, at].astype(F32)
        out[k] = total.astype(BF16)


def merge(codes, x, out):
    mark = (codes[...] == iota((out.shape[0], x.shape[0]), 0)).astype(BF16)
    out[...] = dot(mark, x[...]).astype(BF16)


def finish(gather, x, out):
    out[...] = lax.dot_general(
        gather[...], x[...], (((0,), (0,)), ((), ())), preferred_element_type=F32
    ).astype(BF16)


def per_device(tokens_in, out_grad, scores, expert_ids, w_in, w_down):
    groups, members = lax.axis_size("group"), lax.axis_size("member")
    columns = lax.axis_size("y")
    y, core = lax.axis_index("y"), lax.axis_index("core")
    tokens, width = tokens_in.shape
    picks = expert_ids.shape[1]
    pairs = picks // TGROUPS
    per_group = columns
    rows_group = TGROUPS * tokens // groups
    slots = pairs * rows_group // per_group
    half = width // 2
    quarter = half // QUARTERS
    chunk = width // (2 * columns)
    hidden = w_down.shape[1]
    packed_rows = groups * QUARTERS * slots
    all_rows = members * groups * slots
    swap = [(0, 1), (1, 0)]

    def struct(shape, kind):
        return jax.ShapeDtypeStruct(shape, kind)

    def exchange(x, axis):
        return lax.all_to_all(x, axis, split_axis=0, concat_axis=0, tiled=True)

    def to_group(x):
        return exchange(x.reshape(groups, -1, x.shape[1]), "group").reshape(x.shape)

    def to_members(x):
        copies = jnp.broadcast_to(x[None], (members,) + x.shape)
        return exchange(copies, "member").reshape(members * x.shape[0], x.shape[1])

    info = jnp.stack([y, core]).astype(jnp.int32)
    ids = expert_ids.T
    sizes = (groups, per_group, slots)

    def bind(body, *front):
        return lambda *refs: body(*front, *refs)

    packed = struct((packed_rows, quarter), BF16)
    sent_in = call(bind(pack_inputs, *sizes), packed, info, ids, tokens_in, smem=1)
    near_in = to_group(sent_in)
    sent_grad = call(bind(pack_grads, *sizes), packed, info, ids, scores.T, out_grad, smem=1)
    near_grad = to_group(sent_grad)
    ranks, gather = call(
        bind(describe, *sizes, rows_group),
        (
            struct((groups * per_group, LANES), jnp.int32),
            struct((groups * rows_group, tokens), BF16),
        ),
        ids,
    )
    ranks = to_group(ranks).reshape(groups, per_group, LANES)[:, :, :slots]
    ranks += rows_group * jnp.arange(groups, dtype=jnp.int32)[:, None, None]
    codes = ranks.transpose(1, 0, 2).reshape(1, -1)

    w_pair = w_in[0].reshape(2 * hidden, width)
    w_out = w_down[0]

    def far(x):
        return lax.ppermute(x, "core", swap)

    pair_far = far(lax.dynamic_slice_in_dim(w_pair, (1 - core) * half, half, axis=1))
    out_far = far(lax.dynamic_slice_in_dim(w_out, (1 - core) * half, half, axis=1))
    by_chunk = w_pair.reshape(2 * hidden, columns, 2, chunk)
    back_own = lax.dynamic_index_in_dim(by_chunk, core, 2, keepdims=False)
    back_own = back_own.reshape(2 * hidden, half)
    back_far = lax.dynamic_index_in_dim(by_chunk, 1 - core, 2, keepdims=False)
    back_far = far(back_far.reshape(2 * hidden, half))

    scratch = (pltpu.VMEM((QUARTERS, all_rows, quarter), BF16),)
    rows_in = to_members(near_in)
    pre = call(
        bind(project, slots),
        struct((2, all_rows, 2 * hidden), F32),
        info, rows_in, w_pair, pair_far,
        scratch=scratch, smem=1,
    )
    pre_far = far(pre)
    rows_grad = to_members(near_grad)
    act = call(
        bind(project, slots),
        struct((2, all_rows, hidden), F32),
        info, rows_grad, w_out, out_far,
        scratch=scratch, smem=1,
    )
    act_far = far(act)
    partial = call(
        backward, struct((all_rows, half), BF16), pre, pre_far, act, act_far, back_own, back_far
    )

    arrived = exchange(partial.reshape(members, groups * slots, half), "member")
    starts, window = windows(chunk, columns)
    summed = call(
        bind(add_members, starts, window),
        struct((columns, groups * slots, window), BF16),
        arrived,
    )
    summed = exchange(summed, "y").reshape(columns * groups * slots, window)
    merged = call(merge, struct((groups * rows_group, window), BF16), codes, summed)
    returned = to_group(merged)
    result = call(finish, struct((tokens, window), BF16), gather, returned)
    begin = y * chunk % LANES
    return lax.dynamic_slice_in_dim(result, begin, chunk, axis=1)


def solution(mesh):
    shape = mesh.devices.shape
    split = Mesh(
        mesh.devices.reshape(shape[0], shape[1], shape[2] // 2, 2),
        ("group", "member", "y", "core"),
    )
    in_specs = (
        P(("group", "member"), None),
        P(("group", "member"), None),
        P(("group", "member"), None),
        P(("group", "member"), None),
        P(("group", "y", "core"), None, "member", None),
        P(("group", "y", "core"), "member", None),
    )
    out_specs = P(("group", "member"), ("y", "core"))
    return jax.shard_map(
        per_device, mesh=split, in_specs=in_specs, out_specs=out_specs, check_vma=False
    )
```

time: 325 us -> 217 us (0.67)
  the two profiles are of different devices: /device:TPU:25 before, /device:TPU:2 now
where the time goes in v1:
time: 217 us; the launch traced here: 216 us
  waiting for transfers between devices  82.7 us (38%)
  starting transfers between devices  56.6 us (26%)
  local copies, waits for them, and re-layouts  36.2 us (17%)
  blocking collectives  22.4 us (10%)
  Pallas kernels  17.6 us (8%)
    all_to_all x7, waiting for transfers between devices, exchange(): return lax.all_to_all(x, axis, split_axis=0, concat_axis=0, tiled=True)  82.5 us
    all_to_all x7, starting transfers between devices, exchange(): return lax.all_to_all(x, axis, split_axis=0, concat_axis=0, tiled=True)  45.9 us
    all_to_all x1, blocking collectives, exchange(): return lax.all_to_all(x, axis, split_axis=0, concat_axis=0, tiled=True)  22.4 us
    dynamic_slice x1, local copies, waits for them, and re-layouts, per_device(): back_far = lax.dynamic_index_in_dim(by_chunk, 1 - core, 2, keepdims=False)  17.7 us
    pallas_call x9, Pallas kernels, call(): pl.pallas_call(body, out_shape=out_shape, in_specs=specs, out_specs=jax.t...  17.6 us
    ppermute x5, starting transfers between devices, far(): return lax.ppermute(x, 'core', swap)  10.7 us
    unnamed x20, local copies, waits for them, and re-layouts  4.93 us
  transfers between devices with their start and end apart: 12, of which 7 were waited for; matrix products, arithmetic and copies ran while one was open for 14% of the time, Pallas kernels for 5%

profile of v1, /device:TPU:2, one launch (start us, length us, event | category | flops | bytes accessed | tf_op | source)
XLA Modules:
  0.0 215.9 jit_solution(9917848396401305031)
XLA Ops:
  0.0 0.0 copy-start.7
  0.0 0.0 copy-start.8
  0.0 0.1 pad_add_fusion.refs_0_
  0.1 0.0 copy-start.2
  0.1 1.2 copy-done.2
  1.3 0.0 copy-start.6
  1.3 0.7 copy-done.6
  2.0 0.0 copy-start.3
  2.0 2.0 shard_map.65
  4.0 15.2 %all-to-all-start.1 = ((bf16[12,24,640]{2,1,0:T(8,128)(2,1)}), bf16[12,24,640]{2,1,0:T(8,128)(2,1)S(1)}, u32[]{:S(2)}, u32[]{:S(2)}) async-start(bf16[12,24,640]{2,1,0:T(8,128)(2,1)} %bitcast.5), calls=%async_computation.1 | async-start | bytes 737280 | tf_op jit(solution)/shard_map/all_to_all | solution.py:226
  19.1 0.0 copy-done.7
  19.1 0.0 copy-done.8
  19.2 0.0 copy-done.3
  19.2 1.4 shard_map.67
  20.5 17.7 %all-to-all-done.1 = bf16[12,24,640]{2,1,0:T(8,128)(2,1)S(1)} async-done(((bf16[12,24,640]{2,1,0:T(8,128)(2,1)}), bf16[12,24,640]{2,1,0:T(8,128)(2,1)S(1)}, u32[]{:S(2)}, u32[]{:S(2)}) %all-to-all-start.1) | async-done | bytes 368672 | tf_op jit(solution)/shard_map/all_to_all | solution.py:226
  38.3 22.4 %all_to_all.40 = bf16[12,24,640]{2,1,0:T(8,128)(2,1)} all-to-all(bf16[12,24,640]{2,1,0:T(8,128)(2,1)S(1)} %bitcast.28), channel_id=1, replica_groups=mesh['group'=12,'member'=4,'y'=8,'core'=2] {'group'}, dimensions={0} | all-to-all | bytes 737280 | tf_op jit(solution)/shard_map/all_to_all | solution.py:226
  60.6 1.2 broadcast_in_dim.16
  61.9 0.0 copy-start
  61.9 5.0 %all-to-all-start.2 = ((bf16[4,288,640]{2,1,0:T(8,128)(2,1)}), bf16[4,288,640]{2,1,0:T(8,128)(2,1)S(1)}, u32[]{:S(2)}, u32[]{:S(2)}) async-start(bf16[4,288,640]{2,1,0:T(8,128)(2,1)} %broadcast_in_dim.16), calls=%async_computation.2 | async-start | bytes 2949120 | tf_op jit(solution)/shard_map/all_to_all | solution.py:226
  66.8 0.0 copy-done
  66.8 1.0 constant_dynamic-slice_fusion.1
  67.9 1.9 collective-permute-start
  69.8 3.6 %reshape_reshape_squeeze.3 = bf16[192,8,2,320]{3,2,1,0:T(2,128)(2,1)} reshape(bf16[1,2,96,5120]{3,2,1,0:T(8,128)(2,1)S(1)} %copy-done) | data formatting | bytes 3932160 | tf_op jit(solution)/shard_map/reshape;reshape;squeeze | solution.py:267
  73.4 10.3 %all-to-all-done.2 = bf16[4,288,640]{2,1,0:T(8,128)(2,1)S(1)} async-done(((bf16[4,288,640]{2,1,0:T(8,128)(2,1)}), bf16[4,288,640]{2,1,0:T(8,128)(2,1)S(1)}, u32[]{:S(2)}, u32[]{:S(2)}) %all-to-all-start.2) | async-done | bytes 1474592 | tf_op jit(solution)/shard_map/all_to_all | solution.py:226
  83.7 2.2 %broadcast_in_dim.18 = bf16[4,288,640]{2,1,0:T(8,128)(2,1)} broadcast(bf16[288,640]{1,0:T(8,128)(2,1)} %bitcast.34), dimensions={1,2} | broadcast | bytes 1843200 | tf_op jit(solution)/shard_map/broadcast_in_dim | solution.py:232
  86.0 5.8 %all-to-all-start.4 = ((bf16[4,288,640]{2,1,0:T(8,128)(2,1)}), bf16[4,288,640]{2,1,0:T(8,128)(2,1)}, u32[]{:S(2)}, u32[]{:S(2)}) async-start(bf16[4,288,640]{2,1,0:T(8,128)(2,1)} %broadcast_in_dim.18), calls=%async_computation.4 | async-start | bytes 2949120 | tf_op jit(solution)/shard_map/all_to_all | solution.py:226
  91.7 17.7 %dynamic-slice_reduce_fusion = (bf16[192,8,320]{2,1,0:T(8,128)(2,1)}, bf16[192,8,320]{2,1,0:T(8,128)(2,1)}) fusion(bf16[192,8,2,320]{3,2,1,0:T(2,128)(2,1)} %reshape_reshape_squeeze.3, s32[]{:T(128)S(6)} %select_n.23, s32[]{:T(128)S(6)} %select_n.22), kind=kLoop, calls=%fused_computation | loop fusion | bytes 3932168 | tf_op jit(solution)/shard_map/jit(dynamic_index_in_dim)/dynamic_slice | solution.py:270
  109.4 2.7 %reshape.53 = bf16[192,2560]{1,0:T(8,128)(2,1)} reshape(bf16[192,8,320]{2,1,0:T(8,128)(2,1)} %get-tuple-element.9) | data formatting | bytes 1966080 | tf_op jit(solution)/shard_map/reshape | solution.py:271
  112.1 1.9 collective-permute-start.4
  114.0 1.1 dynamic-slice_bitcast_fusion
  115.1 2.4 %collective-permute-start.2 = (bf16[96,2560]{1,0:T(8,128)(2,1)S(1)}, bf16[96,2560]{1,0:T(8,128)(2,1)S(1)}, u32[]{:S(2)}, u32[]{:S(2)}) collective-permute-start(bf16[96,2560]{1,0:T(8,128)(2,1)S(1)} %dynamic-slice_bitcast_fusion), channel_id=1, source_target_pairs={{0,1},{1,0},{2,3},{3,2},{4,5},{5,4},{6,7},{7,6},{8,9},{9,8},{10,11... | collective-permute-start | bytes 1474568 | tf_op jit(solution)/shard_map/ppermute | solution.py:263
  117.5 0.0 collective-permute-done.refs_3_
  117.5 3.7 %shard_map.66.pre = f32[2,288,192]{2,1,0:T(8,128)} custom-call(s32[2]{0:T(128)S(1)} %pad_add_fusion.refs_0_, bf16[1152,640]{1,0:T(8,128)(2,1)S(1)} %bitcast.25, bf16[192,5120]{1,0:T(8,128)(2,1)S(1)} %bitcast.24, bf16[192,2560]{1,0:T(8,128)(2,1)} %collective-permute-done.refs_3_), custom_call_target="tpu_custom_call" | custom-call | bytes 4423688 | tf_op jit(solution)/shard_map/pallas_call | solution.py:25
  121.2 1.9 collective-permute-start.1
  123.1 0.0 collective-permute-done.2.refs_3_
  123.1 0.0 copy-start.4
  123.1 0.8 copy-done.4
  123.9 0.0 all-to-all-done.4
  123.9 0.0 copy-start.1
  123.9 1.2 copy-done.1
  125.1 1.0 copy-done.5
  126.2 3.0 %shard_map.68.act = f32[2,288,96]{2,1,0:T(8,128)S(1)} custom-call(s32[2]{0:T(128)S(1)} %pad_add_fusion.refs_0_, bf16[1152,640]{1,0:T(8,128)(2,1)} %bitcast.12.refs_1_, bf16[96,5120]{1,0:T(8,128)(2,1)S(1)} %bitcast.26, bf16[96,2560]{1,0:T(8,128)(2,1)S(1)} %copy-done.5), custom_call_target="tpu_custom_call" | custom-call | bytes 2949128 | tf_op jit(solution)/shard_map/pallas_call | solution.py:25
  129.2 2.6 %collective-permute-start.3 = (f32[2,288,96]{2,1,0:T(8,128)S(1)}, f32[2,288,96]{2,1,0:T(8,128)S(1)}, u32[]{:S(2)}, u32[]{:S(2)}) collective-permute-start(f32[2,288,96]{2,1,0:T(8,128)S(1)} %shard_map.68.act), channel_id=1, source_target_pairs={{0,1},{1,0},{2,3},{3,2},{4,5},{5,4},{6,7},{7,6},{8,9},{9,8},{10,11... | collective-permute-start | bytes 663560 | tf_op jit(solution)/shard_map/ppermute | solution.py:263
  131.8 0.0 copy-done.9
  131.8 0.8 reshape.52.own
  132.6 0.0 collective-permute-done.4.other
  132.6 0.2 collective-permute-done.3.act_far
  132.8 0.0 collective-permute-done.1.pre_far
  132.8 4.2 %shard_map.69 = bf16[288,2560]{1,0:T(8,128)(2,1)} custom-call(f32[2,288,192]{2,1,0:T(8,128)} %shard_map.66.pre, f32[2,288,192]{2,1,0:T(8,128)S(1)} %collective-permute-done.1.pre_far, f32[2,288,96]{2,1,0:T(8,128)S(1)} %shard_map.68.act, f32[2,288,96]{2,1,0:T(8,128)S(1)} %collective-permute-done.3.act_far, bf16[192,2560]{1,0:T(8,128)(2,1)S(1)} %reshape.52.own, ...), custom_call_target="tpu_custom_call" | custom-call | bytes 3293184 | tf_op jit(solution)/shard_map/pallas_call | solution.py:25
  137.0 4.8 %all-to-all-start.5 = ((bf16[4,72,2560]{2,1,0:T(8,128)(2,1)}), bf16[4,72,2560]{2,1,0:T(8,128)(2,1)S(1)}, u32[]{:S(2)}, u32[]{:S(2)}) async-start(bf16[4,72,2560]{2,1,0:T(8,128)(2,1)} %bitcast.15), calls=%async_computation.5 | async-start | bytes 2949120 | tf_op jit(solution)/shard_map/all_to_all | solution.py:226
  141.8 1.0 shard_map.64
  142.9 17.7 %all-to-all-done.5.refs_0_ = bf16[4,72,2560]{2,1,0:T(8,128)(2,1)S(1)} async-done(((bf16[4,72,2560]{2,1,0:T(8,128)(2,1)}), bf16[4,72,2560]{2,1,0:T(8,128)(2,1)S(1)}, u32[]{:S(2)}, u32[]{:S(2)}) %all-to-all-start.5) | async-done | bytes 1474592 | tf_op jit(solution)/shard_map/all_to_all | solution.py:226
  160.6 4.6 %all-to-all-start = ((s32[12,8,128]{2,1,0:T(8,128)}), s32[12,8,128]{2,1,0:T(8,128)S(1)}, u32[]{:S(2)}, u32[]{:S(2)}) async-start(s32[12,8,128]{2,1,0:T(8,128)} %bitcast.1), calls=%async_computation | async-start | bytes 98304 | tf_op jit(solution)/shard_map/all_to_all | solution.py:226
  165.1 1.0 shard_map.70
  166.1 9.8 %all-to-all-done = s32[12,8,128]{2,1,0:T(8,128)S(1)} async-done(((s32[12,8,128]{2,1,0:T(8,128)}), s32[12,8,128]{2,1,0:T(8,128)S(1)}, u32[]{:S(2)}, u32[]{:S(2)}) %all-to-all-start) | async-done | bytes 49184 | tf_op jit(solution)/shard_map/all_to_all | solution.py:226
  176.0 7.1 %all-to-all-start.6 = ((bf16[8,72,384]{2,1,0:T(8,128)(2,1)}), bf16[8,72,384]{2,1,0:T(8,128)(2,1)S(1)}, u32[]{:S(2)}, u32[]{:S(2)}) async-start(bf16[8,72,384]{2,1,0:T(8,128)(2,1)} %shard_map.70), calls=%async_computation.6 | async-start | bytes 884736 | tf_op jit(solution)/shard_map/all_to_all | solution.py:226
  183.1 0.1 fusion
  183.2 0.1 reshape.47.codes
  183.3 13.5 %all-to-all-done.6 = bf16[8,72,384]{2,1,0:T(8,128)(2,1)S(1)} async-done(((bf16[8,72,384]{2,1,0:T(8,128)(2,1)}), bf16[8,72,384]{2,1,0:T(8,128)(2,1)S(1)}, u32[]{:S(2)}, u32[]{:S(2)}) %all-to-all-start.6) | async-done | bytes 442400 | tf_op jit(solution)/shard_map/all_to_all | solution.py:226
  196.8 1.1 shard_map.71
  197.9 3.5 %all-to-all-start.7 = ((bf16[12,24,384]{2,1,0:T(8,128)(2,1)}), bf16[12,24,384]{2,1,0:T(8,128)(2,1)S(1)}, u32[]{:S(2)}, u32[]{:S(2)}) async-start(bf16[12,24,384]{2,1,0:T(8,128)(2,1)} %bitcast.17), calls=%async_computation.7 | async-start | bytes 442368 | tf_op jit(solution)/shard_map/all_to_all | solution.py:226
  201.4 13.5 %all-to-all-done.7 = bf16[12,24,384]{2,1,0:T(8,128)(2,1)S(1)} async-done(((bf16[12,24,384]{2,1,0:T(8,128)(2,1)}), bf16[12,24,384]{2,1,0:T(8,128)(2,1)S(1)}, u32[]{:S(2)}, u32[]{:S(2)}) %all-to-all-start.7) | async-done | bytes 221216 | tf_op jit(solution)/shard_map/all_to_all | solution.py:226
  214.9 0.2 shard_map.72
  215.2 0.7 constant_dynamic-slice_fusion
  (4 shorter events, 0.0 us)
Async XLA Ops:
  0.0 19.1 %copy-start.7 = (s32[96,6]{0,1:T(8,128)S(1)}, s32[96,6]{0,1:T(8,128)}, u32[]{:S(2)}) copy-start(s32[96,6]{0,1:T(8,128)} %param.9) | copy-start | bytes 6916
  0.0 19.1 %copy-start.8 = (bf16[96,6]{0,1:T(8,128)(2,1)S(1)}, bf16[96,6]{0,1:T(8,128)(2,1)}, u32[]{:S(2)}) copy-start(bf16[96,6]{0,1:T(8,128)(2,1)} %param.8) | copy-start | bytes 3460
  0.1 1.2 copy-start.2
  1.3 0.7 copy-start.6
  2.0 17.2 %copy-start.3 = (bf16[96,5120]{1,0:T(8,128)(2,1)S(1)}, bf16[96,5120]{1,0:T(8,128)(2,1)}, u32[]{:S(2)}) copy-start(bf16[96,5120]{1,0:T(8,128)(2,1)} %refs_3_.1) | copy-start | bytes 2949124
  4.0 34.3 %all-to-all-start.1 = ((bf16[12,24,640]{2,1,0:T(8,128)(2,1)}), bf16[12,24,640]{2,1,0:T(8,128)(2,1)S(1)}, u32[]{:S(2)}, u32[]{:S(2)}) async-start(bf16[12,24,640]{2,1,0:T(8,128)(2,1)} %bitcast.5), calls=%async_computation.1 | async-start | bytes 737280 | tf_op jit(solution)/shard_map/all_to_all | solution.py:226
  61.9 5.0 %copy-start = (bf16[1,2,96,5120]{3,2,1,0:T(8,128)(2,1)S(1)}, bf16[1,2,96,5120]{3,2,1,0:T(8,128)(2,1)}, u32[]{:S(2)}) copy-start(bf16[1,2,96,5120]{3,2,1,0:T(8,128)(2,1)} %param.10) | copy-start | bytes 5898244
  61.9 21.9 %all-to-all-start.2 = ((bf16[4,288,640]{2,1,0:T(8,128)(2,1)}), bf16[4,288,640]{2,1,0:T(8,128)(2,1)S(1)}, u32[]{:S(2)}, u32[]{:S(2)}) async-start(bf16[4,288,640]{2,1,0:T(8,128)(2,1)} %broadcast_in_dim.16), calls=%async_computation.2 | async-start | bytes 2949120 | tf_op jit(solution)/shard_map/all_to_all | solution.py:226
  67.9 49.7 %collective-permute-start = (bf16[192,2560]{1,0:T(8,128)(2,1)}, bf16[192,2560]{1,0:T(8,128)(2,1)}, u32[]{:S(2)}, u32[]{:S(2)}) collective-permute-start(bf16[192,2560]{1,0:T(8,128)(2,1)} %constant_dynamic-slice_fusion.1), channel_id=1, source_target_pairs={{0,1},{1,0},{2,3},{3,2},{4,5},{5,4},{6,7},{7,6},{8,9},{9,8},{10,11... | collective-permute-start | bytes 2949128 | tf_op jit(solution)/shard_map/ppermute | solution.py:263
  86.0 38.0 %all-to-all-start.4 = ((bf16[4,288,640]{2,1,0:T(8,128)(2,1)}), bf16[4,288,640]{2,1,0:T(8,128)(2,1)}, u32[]{:S(2)}, u32[]{:S(2)}) async-start(bf16[4,288,640]{2,1,0:T(8,128)(2,1)} %broadcast_in_dim.18), calls=%async_computation.4 | async-start | bytes 2949120 | tf_op jit(solution)/shard_map/all_to_all | solution.py:226
  112.1 20.5 %collective-permute-start.4 = (bf16[192,2560]{1,0:T(8,128)(2,1)}, bf16[192,2560]{1,0:T(8,128)(2,1)}, u32[]{:S(2)}, u32[]{:S(2)}) collective-permute-start(bf16[192,2560]{1,0:T(8,128)(2,1)} %reshape.53), channel_id=1, source_target_pairs={{0,1},{1,0},{2,3},{3,2},{4,5},{5,4},{6,7},{7,6},{8,9},{9,8},{10,11... | collective-permute-start | bytes 2949128 | tf_op jit(solution)/shard_map/ppermute | solution.py:263
  115.1 8.0 %collective-permute-start.2 = (bf16[96,2560]{1,0:T(8,128)(2,1)S(1)}, bf16[96,2560]{1,0:T(8,128)(2,1)S(1)}, u32[]{:S(2)}, u32[]{:S(2)}) collective-permute-start(bf16[96,2560]{1,0:T(8,128)(2,1)S(1)} %dynamic-slice_bitcast_fusion), channel_id=1, source_target_pairs={{0,1},{1,0},{2,3},{3,2},{4,5},{5,4},{6,7},{7,6},{8,9},{9,8},{10,11... | collective-permute-start | bytes 1474568 | tf_op jit(solution)/shard_map/ppermute | solution.py:263
  121.2 11.6 %collective-permute-start.1 = (f32[2,288,192]{2,1,0:T(8,128)}, f32[2,288,192]{2,1,0:T(8,128)S(1)}, u32[]{:S(2)}, u32[]{:S(2)}) collective-permute-start(f32[2,288,192]{2,1,0:T(8,128)} %shard_map.66.pre), channel_id=1, source_target_pairs={{0,1},{1,0},{2,3},{3,2},{4,5},{5,4},{6,7},{7,6},{8,9},{9,8},{10,11... | collective-permute-start | bytes 1327112 | tf_op jit(solution)/shard_map/ppermute | solution.py:263
  123.1 0.8 copy-start.4
  123.9 1.2 copy-start.1
  125.1 1.0 copy-start.5
  126.2 5.6 %copy-start.9 = (bf16[192,8,320]{2,1,0:T(8,128)(2,1)S(1)}, bf16[192,8,320]{2,1,0:T(8,128)(2,1)}, u32[]{:S(2)}) copy-start(bf16[192,8,320]{2,1,0:T(8,128)(2,1)} %get-tuple-element.10) | copy-start | bytes 2949124
  129.2 3.6 %collective-permute-start.3 = (f32[2,288,96]{2,1,0:T(8,128)S(1)}, f32[2,288,96]{2,1,0:T(8,128)S(1)}, u32[]{:S(2)}, u32[]{:S(2)}) collective-permute-start(f32[2,288,96]{2,1,0:T(8,128)S(1)} %shard_map.68.act), channel_id=1, source_target_pairs={{0,1},{1,0},{2,3},{3,2},{4,5},{5,4},{6,7},{7,6},{8,9},{9,8},{10,11... | collective-permute-start | bytes 663560 | tf_op jit(solution)/shard_map/ppermute | solution.py:263
  137.0 23.5 %all-to-all-start.5 = ((bf16[4,72,2560]{2,1,0:T(8,128)(2,1)}), bf16[4,72,2560]{2,1,0:T(8,128)(2,1)S(1)}, u32[]{:S(2)}, u32[]{:S(2)}) async-start(bf16[4,72,2560]{2,1,0:T(8,128)(2,1)} %bitcast.15), calls=%async_computation.5 | async-start | bytes 2949120 | tf_op jit(solution)/shard_map/all_to_all | solution.py:226
  160.6 15.4 %all-to-all-start = ((s32[12,8,128]{2,1,0:T(8,128)}), s32[12,8,128]{2,1,0:T(8,128)S(1)}, u32[]{:S(2)}, u32[]{:S(2)}) async-start(s32[12,8,128]{2,1,0:T(8,128)} %bitcast.1), calls=%async_computation | async-start | bytes 98304 | tf_op jit(solution)/shard_map/all_to_all | solution.py:226
  176.0 20.8 %all-to-all-start.6 = ((bf16[8,72,384]{2,1,0:T(8,128)(2,1)}), bf16[8,72,384]{2,1,0:T(8,128)(2,1)S(1)}, u32[]{:S(2)}, u32[]{:S(2)}) async-start(bf16[8,72,384]{2,1,0:T(8,128)(2,1)} %shard_map.70), calls=%async_computation.6 | async-start | bytes 884736 | tf_op jit(solution)/shard_map/all_to_all | solution.py:226
  197.9 17.0 %all-to-all-start.7 = ((bf16[12,24,384]{2,1,0:T(8,128)(2,1)}), bf16[12,24,384]{2,1,0:T(8,128)(2,1)S(1)}, u32[]{:S(2)}, u32[]{:S(2)}) async-start(bf16[12,24,384]{2,1,0:T(8,128)(2,1)} %bitcast.17), calls=%async_computation.7 | async-start | bytes 442368 | tf_op jit(solution)/shard_map/all_to_all | solution.py:226

commit v2 on v0

v2 whole, which is shorter than its diff:
```python
import jax
import jax.numpy as jnp
from jax import lax
from jax.experimental import pallas as pl
from jax.experimental.pallas import tpu as pltpu
from jax.sharding import Mesh, PartitionSpec as P

TGROUPS = 3
QUARTERS = 4
LANES = 128
INTERPRET = False
F32 = jnp.float32
BF16 = jnp.bfloat16


def iota(shape, dim):
    return lax.broadcasted_iota(jnp.int32, shape, dim)


def call(body, out_shape, *args, scratch=(), smem=0, far=(), flops=0, room=40):
    def place(i):
        if i < smem:
            return pl.BlockSpec(memory_space=pltpu.SMEM)
        return pl.BlockSpec(memory_space=pltpu.HBM if i in far else pltpu.VMEM)

    moved = sum(a.size * a.dtype.itemsize for a in args)
    return pl.pallas_call(
        body,
        out_shape=out_shape,
        in_specs=[place(i) for i in range(len(args))],
        out_specs=jax.tree.map(lambda s: pl.BlockSpec(memory_space=pltpu.VMEM), out_shape),
        scratch_shapes=list(scratch),
        compiler_params=pltpu.CompilerParams(vmem_limit_bytes=room * 1024 * 1024),
        cost_estimate=pl.CostEstimate(flops=flops, bytes_accessed=moved, transcendentals=0),
        interpret=INTERPRET,
    )(*args)


def dot(a, b):
    return jnp.dot(a, b, preferred_element_type=F32)


def dot_last(a, b):
    return lax.dot_general(a, b, (((1,), (1,)), ((), ())), preferred_element_type=F32)


def dot_first(a, b):
    return lax.dot_general(a, b, (((0,), (0,)), ((), ())), preferred_element_type=F32)


def picked(ids, target):
    hit = jnp.zeros(target.shape, F32)
    for e in range(ids.shape[0]):
        hit += (ids[e : e + 1, :] == target).astype(F32)
    return hit


def before(tokens, lanes):
    return (iota((tokens, lanes), 0) < iota((tokens, lanes), 1) % tokens).astype(BF16)


def slot_matrix(ids, y, groups, per_group, slots):
    tokens = ids.shape[1]
    lanes = QUARTERS * tokens
    rows_each = QUARTERS * slots
    rows = groups * rows_each
    hit = picked(ids, iota((groups, tokens), 0) * per_group + y).astype(BF16)
    same = (iota((tokens, lanes), 0) == iota((tokens, lanes), 1) % tokens).astype(BF16)
    rank = dot(hit, before(tokens, lanes))
    hit4 = dot(hit, same)
    code = jnp.where(hit4 > 0.5, rank, -1.0).astype(BF16)
    expand = (iota((rows, groups), 0) // rows_each == iota((rows, groups), 1)).astype(BF16)
    row = iota((rows, lanes), 0) % rows_each
    spread = dot(expand, code).astype(jnp.int32)
    mark = (spread == row % slots) & (row // slots == iota((rows, lanes), 1) // tokens)
    return mark, expand, same


def stacked_quarters(ref):
    quarter = ref.shape[1] // QUARTERS
    return jnp.concatenate(
        [ref[:, f * quarter : (f + 1) * quarter] for f in range(QUARTERS)], axis=0
    )


def pack(groups, per_group, slots, info, *refs):
    sources, out, held, done = refs[:4], refs[4], refs[5:9], refs[9]
    ids, scores, near_tokens, near_grads = held
    half = near_tokens.shape[1]
    lanes = pl.ds(pl.multiple_of(info[1] * half, LANES), half)
    copies = []
    for n, (source, target) in enumerate(zip(sources, held)):
        source = source.at[:, lanes] if n >= 2 else source
        copies.append(pltpu.make_async_copy(source, target, done.at[n]))
    for copy in copies:
        copy.start()
    copies[0].wait()
    copies[1].wait()
    ids_now = ids[...]
    mark, expand, same = slot_matrix(ids_now, info[0], groups, per_group, slots)
    target = iota((groups, ids_now.shape[1]), 0) * per_group + info[0]
    score = jnp.zeros(target.shape, F32)
    for e in range(ids_now.shape[0]):
        score += jnp.where(ids_now[e : e + 1, :] == target, scores[e : e + 1, :].astype(F32), 0.0)
    wide = dot(expand, dot(score.astype(BF16), same).astype(BF16))
    slot_score = jnp.sum(jnp.where(mark, wide, 0.0), axis=1, keepdims=True)
    mark = mark.astype(BF16)
    quarter = half // QUARTERS
    copies[2].wait()
    out[:, :quarter] = dot(mark, stacked_quarters(near_tokens)).astype(BF16)
    copies[3].wait()
    out[:, quarter:] = (slot_score * dot(mark, stacked_quarters(near_grads))).astype(BF16)


ENTRIES = ((0, 0), (0, 1), (0, 2), (1, 2), (1, 3), (1, 4))
PIECE = 16


def describe(groups, per_group, slots, pad, ids, gather, place, order):
    ids_now = ids[...]
    tokens = ids_now.shape[1]
    experts = groups * per_group
    hit = picked(ids_now, iota((experts, tokens), 0)) > 0.5
    rank = dot(hit.astype(BF16), before(tokens, tokens))
    code = jnp.where(hit, rank, -1.0).astype(BF16)
    lanes = experts * PIECE
    widen = (iota((experts, lanes), 1) // PIECE == iota((experts, lanes), 0)).astype(BF16)
    spread = dot_first(code, widen).astype(jnp.int32)
    row = iota((tokens, lanes), 1) % PIECE
    for n, (odd, part) in enumerate(ENTRIES):
        mark = (spread == 2 * (row % 3) + odd) & (row // 3 == part)
        gather[n * tokens : (n + 1) * tokens, :] = mark.astype(BF16)

    rows = groups * slots
    at, col = iota(place.shape, 0), iota(place.shape, 1)
    row, source = at % PIECE, col % rows
    mark = jnp.zeros(place.shape, jnp.bool_)
    for n, (odd, part) in enumerate(ENTRIES):
        mark |= (col // rows == n) & (row // 3 == part) & (source % slots == 2 * (row % 3) + odd)
    place[...] = (mark & (at // PIECE == source // slots)).astype(BF16)

    at = iota(order.shape[1:], 0)
    inner = at % pad
    source = inner // slots * (QUARTERS * slots) + at // pad * slots + inner % slots
    for h in range(2):
        here = iota(order.shape[1:], 1) + h * order.shape[2]
        order[h] = ((source == here) & (inner < rows)).astype(BF16)


def round_up(n, k):
    return -(-n // k) * k


def project(blocks, whole, info, order, *refs):
    parts, (pair, pair_far, down, down_far, out, ins, grads) = refs[:-7], refs[-7:]
    quarter = ins.shape[2]
    pad = ins.shape[1] // blocks
    middle = order.shape[2]
    halves = []
    if whole:
        halves += [parts[0][:middle, :], parts[0][middle:, :]]
    halves += [p[...] for p in parts[whole:]]
    for k in range(blocks):
        moved = dot(order[0], halves[2 * k]) + dot(order[1], halves[2 * k + 1])
        moved = moved.astype(BF16)
        for f in range(QUARTERS):
            at = slice(f * pad, (f + 1) * pad)
            ins[f, k * pad : (k + 1) * pad, :] = moved[at, :quarter]
            grads[f, k * pad : (k + 1) * pad, :] = moved[at, quarter:]
    half = QUARTERS * quarter
    hidden = down.shape[0]
    for rows, own, far, begin in ((ins, pair, pair_far, 0), (grads, down, down_far, 2 * LANES)):
        for s, weight in enumerate((own, far)):
            total = jnp.zeros((ins.shape[1], weight.shape[0]), F32)
            for f in range(QUARTERS):
                lanes = pl.ds(pl.multiple_of(info[1] * half + f * quarter, LANES), quarter)
                total += dot_last(rows[f], weight[:, lanes])
            out[s, :, begin : begin + weight.shape[0]] = total


def backward(info, pre_a, got_a, pre_b, got_b, own, far, out):
    hidden = own.shape[0] // 2
    grads = []
    for s in range(2):
        total = jnp.concatenate([pre_a[s] + got_a[1 - s], pre_b[s] + got_b[1 - s]], axis=0)
        gate, up = total[:, :hidden], total[:, hidden : 2 * hidden]
        slope = total[:, 2 * LANES : 2 * LANES + hidden]
        sig = jax.nn.sigmoid(gate)
        gate_grad = slope * up * sig * (1.0 + gate * (1.0 - sig))
        up_grad = slope * gate * sig
        grads.append(jnp.concatenate([gate_grad, up_grad], axis=1).astype(BF16))
    first_core = info[1] == 0
    members = out.shape[0]
    count = grads[0].shape[0]
    pad = count // members
    window = 3 * LANES
    chunk = own.shape[1] // 16
    block_rows = out.shape[1] * LANES // (8 * chunk)
    low = iota((count, LANES), 1) < LANES // 2
    for f in range(4):
        pair = []
        for y in (2 * f, 2 * f + 1):
            lanes = pl.ds(pl.multiple_of(2 * chunk * y + 2 * LANES * info[1], LANES), window)
            pair.append(dot(grads[0], own[:, lanes]) + dot(grads[1], far[:, lanes]))
        turned = jnp.where(first_core, pair[1], pair[0])
        turned = pltpu.roll(turned, jnp.where(first_core, LANES // 2, window - LANES // 2), 1)
        even = jnp.where(first_core, pair[0], turned)
        odd = jnp.where(first_core, turned, pair[1])
        seam = jnp.where(low, even[:, 2 * LANES :], odd[:, :LANES])
        tiles = [even[:, :LANES], even[:, LANES : 2 * LANES], seam]
        tiles += [odd[:, LANES : 2 * LANES], odd[:, 2 * LANES :]]
        for t, tile in enumerate(tiles):
            begin = (5 * f + t) * block_rows
            for k, shift in enumerate((0, members - 1, 1, 2)):
                home = lax.rem(info[2] + shift, members)
                out[home, begin : begin + block_rows, :] = tile[
                    k * pad : k * pad + block_rows
                ].astype(BF16)


def total_pieces(groups, columns, place, x, out):
    rows = place.shape[1] // len(ENTRIES)
    low = iota((rows, LANES), 1) < LANES // 2
    for y in range(columns):
        tiles, turned = [], []
        for t in range(3):
            at = (5 * y // 2 + t) * rows
            tile = x[0, at : at + rows, :].astype(F32)
            for m in range(1, x.shape[0]):
                tile += x[m, at : at + rows, :].astype(F32)
            tiles.append(tile)
            turned.append(pltpu.roll(tile, LANES // 2, 1))
        first = [
            jnp.where(low, turned[0], turned[1]),
            jnp.where(low, turned[1], turned[2]),
        ]
        if y % 2 == 0:
            entries = tiles[:2] + [jnp.where(low, tiles[2], 0.0), jnp.where(low, 0.0, turned[0])] + first
        else:
            entries = first + [jnp.where(low, turned[2], 0.0), jnp.where(low, 0.0, tiles[0])] + tiles[1:]
        stack = jnp.concatenate(entries, axis=0).astype(BF16)
        moved = dot(place[...], stack).astype(BF16)
        for g in range(groups):
            out[g * columns + y] = moved[g * PIECE : (g + 1) * PIECE]


def finish(gather, x, out):
    tokens, chunk = out.shape
    found = dot(gather[...], x[...])
    part = [found[n * tokens : (n + 1) * tokens] for n in range(len(ENTRIES))]
    turned = [pltpu.roll(p, LANES // 2, 1) for p in part[3:]]
    low = iota((tokens, LANES), 1) < LANES // 2
    out[:, :LANES] = (part[0] + jnp.where(low, turned[0], turned[1])).astype(BF16)
    out[:, LANES : 2 * LANES] = (part[1] + jnp.where(low, turned[1], turned[2])).astype(BF16)
    last = (part[2] + turned[2]).astype(BF16)
    out[:, 2 * LANES :] = last[:, : chunk - 2 * LANES]


def per_device(tokens_in, out_grad, scores, expert_ids, w_in, w_down):
    groups, members = lax.axis_size("group"), lax.axis_size("member")
    columns = lax.axis_size("y")
    tokens, width = tokens_in.shape
    picks = expert_ids.shape[1]
    pairs = picks // TGROUPS
    slots = pairs * (TGROUPS * tokens // groups) // columns
    half = width // 2
    quarter = half // QUARTERS
    chunk = width // (2 * columns)
    hidden = w_down.shape[1]
    block_rows = groups * slots
    pad = round_up(block_rows, 16)
    packed_rows = block_rows * QUARTERS
    middle = packed_rows // 2

    def struct(shape, kind):
        return jax.ShapeDtypeStruct(shape, kind)

    def exchange(x, axis):
        return lax.all_to_all(x, axis, split_axis=0, concat_axis=0, tiled=True)

    def up(x):
        return lax.ppermute(x, "member", [(i, (i + 1) % members) for i in range(members)])

    def down(x):
        return lax.ppermute(x, "member", [(i, (i - 1) % members) for i in range(members)])

    def far(x):
        return lax.ppermute(x, "core", [(0, 1), (1, 0)])

    def bind(body, *front):
        return lambda *refs: body(*front, *refs)

    places = [lax.axis_index(name) for name in ("y", "core", "member")]
    info = jnp.stack(places).astype(jnp.int32)
    ids = expert_ids.T
    sent = call(
        bind(pack, groups, columns, slots),
        struct((packed_rows, 2 * quarter), BF16),
        info, ids, scores.T, tokens_in, out_grad,
        smem=1, far=(1, 2, 3, 4), room=60,
        scratch=(
            pltpu.VMEM(ids.shape, ids.dtype),
            pltpu.VMEM(ids.shape, BF16),
            pltpu.VMEM((tokens, half), BF16),
            pltpu.VMEM((tokens, half), BF16),
            pltpu.SemaphoreType.DMA((4,)),
        ),
    )
    w_pair = w_in[0].reshape(2 * hidden, width)
    w_out = w_down[0]
    sent, ids, pair_late, out_late = lax.optimization_barrier((sent, ids, w_pair, w_out))
    near = exchange(sent.reshape(groups, -1, 2 * quarter), "group").reshape(sent.shape)
    pair_far, out_far = far(pair_late), far(out_late)
    gather, place, order = call(
        bind(describe, groups, columns, slots, pad),
        (
            struct((len(ENTRIES) * tokens, groups * columns * PIECE), BF16),
            struct((groups * PIECE, len(ENTRIES) * block_rows), BF16),
            struct((2, QUARTERS * pad, middle), BF16),
        ),
        ids,
    )
    near, order, pair_far, out_far = lax.optimization_barrier((near, order, pair_far, out_far))
    weights = (w_pair, pair_far, w_out, out_far)

    top, bottom = near[:middle], near[middle:]
    below_top, above_bottom = up(top), down(bottom)
    below_bottom, above_top = up(bottom), down(top)
    opposite = (up(below_top), down(above_bottom))

    def step(blocks, *parts):
        count = blocks * pad
        return call(
            bind(project, blocks, blocks == 3),
            struct((2, count, 3 * LANES), F32),
            info, order, *parts, *weights,
            smem=1, flops=12 * count * half * hidden,
            scratch=(
                pltpu.VMEM((QUARTERS, count, quarter), BF16),
                pltpu.VMEM((QUARTERS, count, quarter), BF16),
            ),
        )

    pre_a = step(3, near, below_top, below_bottom, above_top, above_bottom)
    pre_late, *opposite = lax.optimization_barrier((pre_a, *opposite))
    got_a = far(pre_late)
    pre_b = step(1, *opposite)
    got_b = far(pre_b)
    partial = call(
        backward,
        struct((members, block_rows * half // LANES, LANES), BF16),
        info, pre_a, got_a, pre_b, got_b, w_pair, pair_far,
        smem=1, flops=8 * members * pad * hidden * half,
    )
    pieces = call(
        bind(total_pieces, groups, columns),
        struct((groups * columns, PIECE, LANES), BF16),
        place, exchange(partial, "member"),
    )
    arrived = exchange(pieces, ("group", "y")).reshape(-1, LANES)
    return call(finish, struct((tokens, chunk), BF16), gather, arrived)


def solution(mesh):
    shape = mesh.devices.shape
    split = Mesh(
        mesh.devices.reshape(shape[0], shape[1], shape[2] // 2, 2),
        ("group", "member", "y", "core"),
    )
    in_specs = (
        P(("group", "member"), None),
        P(("group", "member"), None),
        P(("group", "member"), None),
        P(("group", "member"), None),
        P(("group", "y", "core"), None, "member", None),
        P(("group", "y", "core"), "member", None),
    )
    out_specs = P(("group", "member"), ("y", "core"))
    return jax.shard_map(
        per_device, mesh=split, in_specs=in_specs, out_specs=out_specs, check_vma=False
    )
```

time: 325 us -> 151 us (0.46)
  the two profiles are of different devices: /device:TPU:25 before, /device:TPU:2 now
where the time goes in v2:
time: 151 us; the launch traced here: 150 us
  blocking collectives  58.2 us (39%)
  starting transfers between devices  41.4 us (27%)
  waiting for transfers between devices  27.9 us (18%)
  Pallas kernels  15.9 us (11%)
  local copies, waits for them, and re-layouts  6.26 us (4%)
    all_to_all x2, blocking collectives, exchange(): return lax.all_to_all(x, axis, split_axis=0, concat_axis=0, tiled=True)  58.2 us
    all_to_all x1, waiting for transfers between devices, exchange(): return lax.all_to_all(x, axis, split_axis=0, concat_axis=0, tiled=True)  20.2 us
    pallas_call x7, Pallas kernels, call(): pl.pallas_call(body, out_shape=out_shape, in_specs=[place(i) for i in ran...  15.9 us
    all_to_all x1, starting transfers between devices, exchange(): return lax.all_to_all(x, axis, split_axis=0, concat_axis=0, tiled=True)  15.2 us
    ppermute x3, starting transfers between devices, up(): lax.ppermute(x, 'member', [(i, (i + 1) % members) for i in range(members)])  10.3 us
    ppermute x4, starting transfers between devices, far(): return lax.ppermute(x, 'core', [(0, 1), (1, 0)])  8.6 us
    ppermute x3, starting transfers between devices, down(): lax.ppermute(x, 'member', [(i, (i - 1) % members) for i in range(members)])  7.29 us
    unnamed x24, local copies, waits for them, and re-layouts  6.22 us
  transfers between devices with their start and end apart: 11, of which 6 were waited for; matrix products, arithmetic and copies ran while one was open for 0% of the time, Pallas kernels for 5%

profile of v2, /device:TPU:2, one launch (start us, length us, event | category | flops | bytes accessed | tf_op | source)
XLA Modules:
  0.0 150.4 jit_solution(13635592334891728491)
XLA Ops:
  0.0 0.6 pad_add_fusion.refs_0_.info
  0.6 0.0 copy-start
  0.6 0.0 copy-start.10
  0.6 3.9 %shard_map.64 = bf16[288,1280]{1,0:T(8,128)(2,1)} custom-call(s32[3]{0:T(128)} %pad_add_fusion.refs_0_.info, s32[6,96]{1,0:T(8,128)} %bitcast.20, bf16[6,96]{1,0:T(8,128)(2,1)} %bitcast.23, bf16[96,5120]{1,0:T(8,128)(2,1)} %refs_3_.1, bf16[96,5120]{1,0:T(8,128)(2,1)} %refs_4_.1), custom_call_target="tpu_custom_call" | custom-call | bytes 1969548 | tf_op jit(solution)/shard_map/pallas_call | solution.py:27
  4.4 0.0 copy-start.11
  4.5 15.2 %all-to-all-start = ((bf16[12,24,1280]{2,1,0:T(8,128)(2,1)}), bf16[12,24,1280]{2,1,0:T(8,128)(2,1)S(1)}, u32[]{:S(2)}, u32[]{:S(2)}) async-start(bf16[12,24,1280]{2,1,0:T(8,128)(2,1)} %bitcast.22), calls=%async_computation | async-start | bytes 1474560 | tf_op jit(solution)/shard_map/all_to_all | solution.py:279
  19.6 0.0 copy-done
  19.6 1.9 %collective-permute-start = (bf16[192,5120]{1,0:T(8,128)(2,1)S(1)}, bf16[192,5120]{1,0:T(8,128)(2,1)S(1)}, u32[]{:S(2)}, u32[]{:S(2)}) collective-permute-start(bf16[192,5120]{1,0:T(8,128)(2,1)S(1)} %bitcast.10), channel_id=1, source_target_pairs={{0,1},{1,0},{2,3},{3,2},{4,5},{5,4},{6,7},{7,6},{8,9},{9,8},{10,11... | collective-permute-start | bytes 5898248 | tf_op jit(solution)/shard_map/ppermute | solution.py:288
  21.6 2.4 %collective-permute-start.1 = (bf16[96,5120]{1,0:T(8,128)(2,1)}, bf16[96,5120]{1,0:T(8,128)(2,1)S(1)}, u32[]{:S(2)}, u32[]{:S(2)}) collective-permute-start(bf16[96,5120]{1,0:T(8,128)(2,1)} %bitcast.16), channel_id=1, source_target_pairs={{0,1},{1,0},{2,3},{3,2},{4,5},{5,4},{6,7},{7,6},{8,9},{9,8},{10,11... | collective-permute-start | bytes 2949128 | tf_op jit(solution)/shard_map/ppermute | solution.py:288
  24.0 0.0 copy-done.10
  24.0 1.9 %shard_map.65 = (bf16[576,1536]{1,0:T(8,128)(2,1)S(1)}, bf16[192,432]{1,0:T(8,128)(2,1)S(1)}, bf16[2,320,144]{2,1,0:T(8,128)(2,1)S(1)}) custom-call(s32[6,96]{1,0:T(8,128)S(1)} %bitcast.21), custom_call_target="tpu_custom_call" | custom-call | bytes 2304 | tf_op jit(solution)/shard_map/pallas_call | solution.py:27
  25.9 0.0 copy-start.8
  25.9 1.2 copy-done.8
  27.1 0.0 collective-permute-done.1.refs_10_.refs_7_
  27.1 0.0 copy-start.5
  27.1 0.9 copy-done.5
  28.1 0.0 collective-permute-done.refs_8_.refs_5_.far
  28.1 0.0 copy-start.1
  28.1 1.3 copy-done.1
  29.4 20.2 %all-to-all-done = bf16[12,24,1280]{2,1,0:T(8,128)(2,1)S(1)} async-done(((bf16[12,24,1280]{2,1,0:T(8,128)(2,1)}), bf16[12,24,1280]{2,1,0:T(8,128)(2,1)S(1)}, u32[]{:S(2)}, u32[]{:S(2)}) %all-to-all-start) | async-done | bytes 737312 | tf_op jit(solution)/shard_map/all_to_all | solution.py:279
  49.5 0.0 copy-start.4
  49.6 3.5 %collective-permute-start.2 = (bf16[144,1280]{1,0:T(8,128)(2,1)S(1)}, bf16[144,1280]{1,0:T(8,128)(2,1)S(1)}, u32[]{:S(2)}, u32[]{:S(2)}) collective-permute-start(bf16[144,1280]{1,0:T(8,128)(2,1)S(1)} %get-tuple-element.34), channel_id=1, source_target_pairs={{0,16},{16,32},{32,48},{48,0},{1,17},{17,33},{33,49},{49,1},{2,18}... | collective-permute-start | bytes 1105928 | tf_op jit(solution)/shard_map/ppermute | solution.py:282
  53.1 2.4 %collective-permute-start.5 = (bf16[144,1280]{1,0:T(8,128)(2,1)S(1)}, bf16[144,1280]{1,0:T(8,128)(2,1)S(1)}, u32[]{:S(2)}, u32[]{:S(2)}) collective-permute-start(bf16[144,1280]{1,0:T(8,128)(2,1)S(1)} %get-tuple-element.33), channel_id=1, source_target_pairs={{0,48},{16,0},{32,16},{48,32},{1,49},{17,1},{33,17},{49,33},{2,50}... | collective-permute-start | bytes 1105928 | tf_op jit(solution)/shard_map/ppermute | solution.py:285
  55.6 3.4 %collective-permute-start.3 = (bf16[144,1280]{1,0:T(8,128)(2,1)S(1)}, bf16[144,1280]{1,0:T(8,128)(2,1)S(1)}, u32[]{:S(2)}, u32[]{:S(2)}) collective-permute-start(bf16[144,1280]{1,0:T(8,128)(2,1)S(1)} %get-tuple-element.33), channel_id=1, source_target_pairs={{0,16},{16,32},{32,48},{48,0},{1,17},{17,33},{33,49},{49,1},{2,18}... | collective-permute-start | bytes 1105928 | tf_op jit(solution)/shard_map/ppermute | solution.py:282
  59.0 2.4 %collective-permute-start.4 = (bf16[144,1280]{1,0:T(8,128)(2,1)S(1)}, bf16[144,1280]{1,0:T(8,128)(2,1)S(1)}, u32[]{:S(2)}, u32[]{:S(2)}) collective-permute-start(bf16[144,1280]{1,0:T(8,128)(2,1)S(1)} %get-tuple-element.34), channel_id=1, source_target_pairs={{0,48},{16,0},{32,16},{48,32},{1,49},{17,1},{33,17},{49,33},{2,50}... | collective-permute-start | bytes 1105928 | tf_op jit(solution)/shard_map/ppermute | solution.py:285
  61.4 0.8 collective-permute-done.2.refs_3_
  62.2 3.4 %collective-permute-start.6 = (bf16[144,1280]{1,0:T(8,128)(2,1)S(1)}, bf16[144,1280]{1,0:T(8,128)(2,1)S(1)}, u32[]{:S(2)}, u32[]{:S(2)}) collective-permute-start(bf16[144,1280]{1,0:T(8,128)(2,1)S(1)} %collective-permute-done.2.refs_3_), channel_id=1, source_target_pairs={{0,16},{16,32},{32,48},{48,0},{1,17},{17,33},{33,49},{49,1},{2,18}... | collective-permute-start | bytes 1105928 | tf_op jit(solution)/shard_map/ppermute | solution.py:282
  65.7 0.3 collective-permute-done.5.refs_6_
  66.0 2.4 %collective-permute-start.7 = (bf16[144,1280]{1,0:T(8,128)(2,1)S(1)}, bf16[144,1280]{1,0:T(8,128)(2,1)S(1)}, u32[]{:S(2)}, u32[]{:S(2)}) collective-permute-start(bf16[144,1280]{1,0:T(8,128)(2,1)S(1)} %collective-permute-done.5.refs_6_), channel_id=1, source_target_pairs={{0,48},{16,0},{32,16},{48,32},{1,49},{17,1},{33,17},{49,33},{2,50}... | collective-permute-start | bytes 1105928 | tf_op jit(solution)/shard_map/ppermute | solution.py:285
  68.4 1.7 %collective-permute-done.3.refs_4_ = bf16[144,1280]{1,0:T(8,128)(2,1)S(1)} collective-permute-done((bf16[144,1280]{1,0:T(8,128)(2,1)S(1)}, bf16[144,1280]{1,0:T(8,128)(2,1)S(1)}, u32[]{:S(2)}, u32[]{:S(2)}) %collective-permute-start.3) | collective-permute-done | bytes 368672 | tf_op jit(solution)/shard_map/ppermute | solution.py:282
  70.1 3.8 %collective-permute-done.4.refs_5_ = bf16[144,1280]{1,0:T(8,128)(2,1)S(1)} collective-permute-done((bf16[144,1280]{1,0:T(8,128)(2,1)S(1)}, bf16[144,1280]{1,0:T(8,128)(2,1)S(1)}, u32[]{:S(2)}, u32[]{:S(2)}) %collective-permute-start.4) | collective-permute-done | bytes 368672 | tf_op jit(solution)/shard_map/ppermute | solution.py:285
  73.9 0.0 copy-done.11
  73.9 0.0 copy-done.4
  73.9 0.0 copy-start.2
  73.9 1.5 %copy-done.2 = bf16[192,5120]{1,0:T(8,128)(2,1)S(1)} copy-done((bf16[192,5120]{1,0:T(8,128)(2,1)S(1)}, bf16[192,5120]{1,0:T(8,128)(2,1)}, u32[]{:S(2)}) %copy-start.2) | copy-done | bytes 1966104
  75.5 0.0 copy-start.6
  75.5 1.2 copy-done.6
  76.7 0.0 copy-start.3
  76.7 0.0 copy-start.7
  76.7 3.5 %shard_map.66.pre_a = f32[2,240,384]{2,1,0:T(8,128)S(1)} custom-call(s32[3]{0:T(128)S(1)} %copy-done.11, bf16[2,320,144]{2,1,0:T(8,128)(2,1)S(1)} %get-tuple-element.26.refs_1_, bf16[288,1280]{1,0:T(8,128)(2,1)S(1)} %bitcast.15, bf16[144,1280]{1,0:T(8,128)(2,1)S(1)} %collective-permute-done.2.refs_3_, bf16[144,1280]{1,0:T(8,128)(2,1)S(1)} %collective-permute-done.3.refs_4_, ...), custom_call_target="tpu_custom_call" | custom-call | flops 707788800 | bytes 8294412 | tf_op jit(solution)/shard_map/pallas_call | solution.py:27
  80.2 0.0 collective-permute-done.6.refs_2_
  80.2 0.0 collective-permute-done.7.refs_3_
  80.2 1.9 %collective-permute-start.8 = (f32[2,240,384]{2,1,0:T(8,128)S(1)}, f32[2,240,384]{2,1,0:T(8,128)S(1)}, u32[]{:S(2)}, u32[]{:S(2)}) collective-permute-start(f32[2,240,384]{2,1,0:T(8,128)S(1)} %shard_map.66.pre_a), channel_id=1, source_target_pairs={{0,1},{1,0},{2,3},{3,2},{4,5},{5,4},{6,7},{7,6},{8,9},{9,8},{10,11... | collective-permute-start | bytes 2211848 | tf_op jit(solution)/shard_map/ppermute | solution.py:288
  82.1 0.0 copy-done.3
  82.1 0.0 copy-done.7
  82.1 2.2 %shard_map.67.pre_b = f32[2,80,384]{2,1,0:T(8,128)S(1)} custom-call(s32[3]{0:T(128)S(1)} %copy-done.11, bf16[2,320,144]{2,1,0:T(8,128)(2,1)S(1)} %get-tuple-element.26.refs_1_, bf16[144,1280]{1,0:T(8,128)(2,1)S(1)} %collective-permute-done.6.refs_2_, bf16[144,1280]{1,0:T(8,128)(2,1)S(1)} %collective-permute-done.7.refs_3_, bf16[192,5120]{1,0:T(8,128)(2,1)S(1)} %bitcast.12, ...), custom_call_target="tpu_custom_call" | custom-call | flops 235929600 | bytes 6819852 | tf_op jit(solution)/shard_map/pallas_call | solution.py:27
  84.3 2.3 %collective-permute-start.9 = (f32[2,80,384]{2,1,0:T(8,128)S(1)}, f32[2,80,384]{2,1,0:T(8,128)S(1)}, u32[]{:S(2)}, u32[]{:S(2)}) collective-permute-start(f32[2,80,384]{2,1,0:T(8,128)S(1)} %shard_map.67.pre_b), channel_id=1, source_target_pairs={{0,1},{1,0},{2,3},{3,2},{4,5},{5,4},{6,7},{7,6},{8,9},{9,8},{10,11... | collective-permute-start | bytes 737288 | tf_op jit(solution)/shard_map/ppermute | solution.py:288
  86.7 1.1 collective-permute-done.9.got_b
  87.8 0.0 collective-permute-done.8.got_a
  87.8 2.5 %shard_map.68 = bf16[4,1440,128]{2,1,0:T(8,128)(2,1)S(1)} custom-call(s32[3]{0:T(128)S(1)} %copy-done.11, f32[2,240,384]{2,1,0:T(8,128)S(1)} %shard_map.66.pre_a, f32[2,240,384]{2,1,0:T(8,128)S(1)} %collective-permute-done.8.got_a, f32[2,80,384]{2,1,0:T(8,128)S(1)} %shard_map.67.pre_b, f32[2,80,384]{2,1,0:T(8,128)S(1)} %collective-permute-done.9.got_b, ...), custom_call_target="tpu_custom_call" | custom-call | flops 629145600 | bytes 5898252 | tf_op jit(solution)/shard_map/pallas_call | solution.py:27
  90.3 23.2 %all_to_all.15.refs_1_ = bf16[4,1440,128]{2,1,0:T(8,128)(2,1)S(1)} all-to-all(bf16[4,1440,128]{2,1,0:T(8,128)(2,1)S(1)} %shard_map.68), channel_id=1, replica_groups=mesh['group'=12,'member'=4,'y'=8,'core'=2] {'member'}, dimensions={0} | all-to-all | bytes 2949120 | tf_op jit(solution)/shard_map/all_to_all | solution.py:279
  113.5 0.0 copy-start.9
  113.5 0.7 shard_map.69
  114.1 35.0 %all_to_all.16 = bf16[96,16,128]{2,1,0:T(8,128)(2,1)S(1)} all-to-all(bf16[96,16,128]{2,1,0:T(8,128)(2,1)S(1)} %shard_map.69), channel_id=1, replica_groups=mesh['group'=12,'member'=4,'y'=8,'core'=2] {'group','y'}, dimensions={0} | all-to-all | bytes 786432 | tf_op jit(solution)/shard_map/all_to_all | solution.py:279
  149.1 0.0 copy-done.9
  149.1 1.3 shard_map.70
  (1 shorter events, 0.0 us)
Async XLA Ops:
  0.6 19.1 %copy-start = (bf16[1,2,96,5120]{3,2,1,0:T(8,128)(2,1)S(1)}, bf16[1,2,96,5120]{3,2,1,0:T(8,128)(2,1)}, u32[]{:S(2)}) copy-start(bf16[1,2,96,5120]{3,2,1,0:T(8,128)(2,1)} %param.10) | copy-start | bytes 5898244
  0.6 23.4 %copy-start.10 = (s32[96,6]{0,1:T(8,128)S(1)}, s32[96,6]{0,1:T(8,128)}, u32[]{:S(2)}) copy-start(s32[96,6]{0,1:T(8,128)} %param.9) | copy-start | bytes 6916
  4.4 69.5 %copy-start.11 = (s32[3]{0:T(128)S(1)}, s32[3]{0:T(128)}, u32[]{:S(2)}) copy-start(s32[3]{0:T(128)} %pad_add_fusion.refs_0_.info) | copy-start | bytes 40
  4.5 45.1 %all-to-all-start = ((bf16[12,24,1280]{2,1,0:T(8,128)(2,1)}), bf16[12,24,1280]{2,1,0:T(8,128)(2,1)S(1)}, u32[]{:S(2)}, u32[]{:S(2)}) async-start(bf16[12,24,1280]{2,1,0:T(8,128)(2,1)} %bitcast.22), calls=%async_computation | async-start | bytes 1474560 | tf_op jit(solution)/shard_map/all_to_all | solution.py:279
  19.6 8.4 %collective-permute-start = (bf16[192,5120]{1,0:T(8,128)(2,1)S(1)}, bf16[192,5120]{1,0:T(8,128)(2,1)S(1)}, u32[]{:S(2)}, u32[]{:S(2)}) collective-permute-start(bf16[192,5120]{1,0:T(8,128)(2,1)S(1)} %bitcast.10), channel_id=1, source_target_pairs={{0,1},{1,0},{2,3},{3,2},{4,5},{5,4},{6,7},{7,6},{8,9},{9,8},{10,11... | collective-permute-start | bytes 5898248 | tf_op jit(solution)/shard_map/ppermute | solution.py:288
  21.6 5.6 %collective-permute-start.1 = (bf16[96,5120]{1,0:T(8,128)(2,1)}, bf16[96,5120]{1,0:T(8,128)(2,1)S(1)}, u32[]{:S(2)}, u32[]{:S(2)}) collective-permute-start(bf16[96,5120]{1,0:T(8,128)(2,1)} %bitcast.16), channel_id=1, source_target_pairs={{0,1},{1,0},{2,3},{3,2},{4,5},{5,4},{6,7},{7,6},{8,9},{9,8},{10,11... | collective-permute-start | bytes 2949128 | tf_op jit(solution)/shard_map/ppermute | solution.py:288
  25.9 1.2 copy-start.8
  27.1 0.9 copy-start.5
  28.1 1.3 copy-start.1
  49.5 24.4 %copy-start.4 = (bf16[1,96,5120]{2,1,0:T(8,128)(2,1)S(1)}, bf16[1,96,5120]{2,1,0:T(8,128)(2,1)}, u32[]{:S(2)}) copy-start(bf16[1,96,5120]{2,1,0:T(8,128)(2,1)} %param.11) | copy-start | bytes 2949124
  49.6 12.6 %collective-permute-start.2 = (bf16[144,1280]{1,0:T(8,128)(2,1)S(1)}, bf16[144,1280]{1,0:T(8,128)(2,1)S(1)}, u32[]{:S(2)}, u32[]{:S(2)}) collective-permute-start(bf16[144,1280]{1,0:T(8,128)(2,1)S(1)} %get-tuple-element.34), channel_id=1, source_target_pairs={{0,16},{16,32},{32,48},{48,0},{1,17},{17,33},{33,49},{49,1},{2,18}... | collective-permute-start | bytes 1105928 | tf_op jit(solution)/shard_map/ppermute | solution.py:282
  53.1 12.9 %collective-permute-start.5 = (bf16[144,1280]{1,0:T(8,128)(2,1)S(1)}, bf16[144,1280]{1,0:T(8,128)(2,1)S(1)}, u32[]{:S(2)}, u32[]{:S(2)}) collective-permute-start(bf16[144,1280]{1,0:T(8,128)(2,1)S(1)} %get-tuple-element.33), channel_id=1, source_target_pairs={{0,48},{16,0},{32,16},{48,32},{1,49},{17,1},{33,17},{49,33},{2,50}... | collective-permute-start | bytes 1105928 | tf_op jit(solution)/shard_map/ppermute | solution.py:285
  55.6 14.6 %collective-permute-start.3 = (bf16[144,1280]{1,0:T(8,128)(2,1)S(1)}, bf16[144,1280]{1,0:T(8,128)(2,1)S(1)}, u32[]{:S(2)}, u32[]{:S(2)}) collective-permute-start(bf16[144,1280]{1,0:T(8,128)(2,1)S(1)} %get-tuple-element.33), channel_id=1, source_target_pairs={{0,16},{16,32},{32,48},{48,0},{1,17},{17,33},{33,49},{49,1},{2,18}... | collective-permute-start | bytes 1105928 | tf_op jit(solution)/shard_map/ppermute | solution.py:282
  59.0 14.9 %collective-permute-start.4 = (bf16[144,1280]{1,0:T(8,128)(2,1)S(1)}, bf16[144,1280]{1,0:T(8,128)(2,1)S(1)}, u32[]{:S(2)}, u32[]{:S(2)}) collective-permute-start(bf16[144,1280]{1,0:T(8,128)(2,1)S(1)} %get-tuple-element.34), channel_id=1, source_target_pairs={{0,48},{16,0},{32,16},{48,32},{1,49},{17,1},{33,17},{49,33},{2,50}... | collective-permute-start | bytes 1105928 | tf_op jit(solution)/shard_map/ppermute | solution.py:285
  62.2 17.9 %collective-permute-start.6 = (bf16[144,1280]{1,0:T(8,128)(2,1)S(1)}, bf16[144,1280]{1,0:T(8,128)(2,1)S(1)}, u32[]{:S(2)}, u32[]{:S(2)}) collective-permute-start(bf16[144,1280]{1,0:T(8,128)(2,1)S(1)} %collective-permute-done.2.refs_3_), channel_id=1, source_target_pairs={{0,16},{16,32},{32,48},{48,0},{1,17},{17,33},{33,49},{49,1},{2,18}... | collective-permute-start | bytes 1105928 | tf_op jit(solution)/shard_map/ppermute | solution.py:282
  66.0 14.2 %collective-permute-start.7 = (bf16[144,1280]{1,0:T(8,128)(2,1)S(1)}, bf16[144,1280]{1,0:T(8,128)(2,1)S(1)}, u32[]{:S(2)}, u32[]{:S(2)}) collective-permute-start(bf16[144,1280]{1,0:T(8,128)(2,1)S(1)} %collective-permute-done.5.refs_6_), channel_id=1, source_target_pairs={{0,48},{16,0},{32,16},{48,32},{1,49},{17,1},{33,17},{49,33},{2,50}... | collective-permute-start | bytes 1105928 | tf_op jit(solution)/shard_map/ppermute | solution.py:285
  73.9 1.5 %copy-start.2 = (bf16[192,5120]{1,0:T(8,128)(2,1)S(1)}, bf16[192,5120]{1,0:T(8,128)(2,1)}, u32[]{:S(2)}) copy-start(bf16[192,5120]{1,0:T(8,128)(2,1)} %copy-done.1) | copy-start | bytes 5898244
  75.5 1.2 copy-start.6
  76.7 5.5 %copy-start.3 = (bf16[192,5120]{1,0:T(8,128)(2,1)S(1)}, bf16[192,5120]{1,0:T(8,128)(2,1)}, u32[]{:S(2)}) copy-start(bf16[192,5120]{1,0:T(8,128)(2,1)} %copy-done.1) | copy-start | bytes 5898244
  76.7 5.5 %copy-start.7 = (bf16[96,5120]{1,0:T(8,128)(2,1)S(1)}, bf16[96,5120]{1,0:T(8,128)(2,1)}, u32[]{:S(2)}) copy-start(bf16[96,5120]{1,0:T(8,128)(2,1)} %copy-done.5) | copy-start | bytes 2949124
  80.2 7.6 %collective-permute-start.8 = (f32[2,240,384]{2,1,0:T(8,128)S(1)}, f32[2,240,384]{2,1,0:T(8,128)S(1)}, u32[]{:S(2)}, u32[]{:S(2)}) collective-permute-start(f32[2,240,384]{2,1,0:T(8,128)S(1)} %shard_map.66.pre_a), channel_id=1, source_target_pairs={{0,1},{1,0},{2,3},{3,2},{4,5},{5,4},{6,7},{7,6},{8,9},{9,8},{10,11... | collective-permute-start | bytes 2211848 | tf_op jit(solution)/shard_map/ppermute | solution.py:288
  84.3 3.5 %collective-permute-start.9 = (f32[2,80,384]{2,1,0:T(8,128)S(1)}, f32[2,80,384]{2,1,0:T(8,128)S(1)}, u32[]{:S(2)}, u32[]{:S(2)}) collective-permute-start(f32[2,80,384]{2,1,0:T(8,128)S(1)} %shard_map.67.pre_b), channel_id=1, source_target_pairs={{0,1},{1,0},{2,3},{3,2},{4,5},{5,4},{6,7},{7,6},{8,9},{9,8},{10,11... | collective-permute-start | bytes 737288 | tf_op jit(solution)/shard_map/ppermute | solution.py:288
  113.5 35.6 %copy-start.9 = (bf16[576,1536]{1,0:T(8,128)(2,1)S(1)}, bf16[576,1536]{1,0:T(8,128)(2,1)}, u32[]{:S(2)}) copy-start(bf16[576,1536]{1,0:T(8,128)(2,1)} %copy-done.8) | copy-start | bytes 5308420

commit v3 on v2

v3 whole, which is shorter than its diff:
```python
from types import MappingProxyType

import jax
import jax.numpy as jnp
from jax import lax
from jax.experimental import pallas as pl
from jax.experimental.pallas import tpu as pltpu
from jax.sharding import Mesh, PartitionSpec as P

TGROUPS = 3
PARTS = 8
CORES = 2
LATE = 128
LANES = 128
INTERPRET = False
F32 = jnp.float32
BF16 = jnp.bfloat16


def iota(shape, dim):
    return lax.broadcasted_iota(jnp.int32, shape, dim)


def call(body, out_shape, *args, scratch=(), far=MappingProxyType({}), far_out=False, alias=None, flops=0, room=20):
    moved = sum(a.size * a.dtype.itemsize for a in args)
    target = pl.ANY if far_out else pltpu.VMEM
    return pl.pallas_call(
        body,
        out_shape=out_shape,
        in_specs=[pl.BlockSpec(memory_space=far.get(i, pltpu.VMEM)) for i in range(len(args))],
        out_specs=jax.tree.map(lambda s: pl.BlockSpec(memory_space=target), out_shape),
        scratch_shapes=list(scratch),
        input_output_aliases={} if alias is None else {alias: 0},
        compiler_params=pltpu.CompilerParams(vmem_limit_bytes=room * 1024 * 1024),
        cost_estimate=pl.CostEstimate(flops=flops, bytes_accessed=moved, transcendentals=0),
        interpret=INTERPRET,
    )(*args)


def dot(a, b):
    return jnp.dot(a, b, preferred_element_type=F32)


def dot_last(a, b):
    return lax.dot_general(a, b, (((1,), (1,)), ((), ())), preferred_element_type=F32)


def dot_first(a, b):
    return lax.dot_general(a, b, (((0,), (0,)), ((), ())), preferred_element_type=F32)


def picked(ids, target):
    hit = jnp.zeros(target.shape, F32)
    for e in range(ids.shape[0]):
        hit += (ids[e : e + 1, :] == target).astype(F32)
    return hit


def before(tokens, lanes):
    return (iota((tokens, lanes), 0) < iota((tokens, lanes), 1) % tokens).astype(BF16)


def stacked_parts(ref):
    part = ref.shape[1] // PARTS
    return jnp.concatenate([ref[:, f * part : (f + 1) * part] for f in range(PARTS)], axis=0)


def pack(groups, per_group, slots, ids_far, scores_far, tokens_far, grads_far, out, ids, scores, tokens, grads, done):
    sources, targets = (ids_far, scores_far, tokens_far, grads_far), (ids, scores, tokens, grads)
    copies = [
        pltpu.make_async_copy(source, target, done.at[n])
        for n, (source, target) in enumerate(zip(sources, targets))
    ]
    for copy in copies:
        copy.start()
    count = ids.shape[1]
    lanes = PARTS * count
    own_slots = slots // CORES
    each = PARTS * own_slots
    rows = groups * each
    expert = iota((rows, count), 0) // each * per_group + lax.axis_index("y")
    wide = iota((count, lanes), 1) % count
    at = iota((count, lanes), 0)
    ranker = jnp.where(at < wide, 1.0, jnp.where(at == wide, float(LATE), 0.0)).astype(BF16)
    row = iota((rows, lanes), 0) % each
    here = row // own_slots == iota((rows, lanes), 1) // count
    wanted = (row % own_slots + (LATE + own_slots * lax.axis_index("core"))).astype(F32)
    copies[0].wait()
    copies[1].wait()
    hit = jnp.zeros((rows, count), F32)
    score = jnp.zeros((rows, count), F32)
    for e in range(ids.shape[0]):
        same = ids[e : e + 1, :] == expert
        hit = jnp.where(same, 1.0, hit)
        score = jnp.where(same, scores[e : e + 1, :].astype(F32), score)
    rank = dot(hit.astype(BF16), ranker)
    found = rank == wanted
    mark = jnp.where(found & here, 1.0, 0.0).astype(BF16)
    slot_score = jnp.sum(jnp.where(found[:, :count], score, 0.0), axis=1, keepdims=True)
    part = tokens.shape[1] // PARTS
    copies[2].wait()
    out[:, :part] = dot(mark, stacked_parts(tokens)).astype(BF16)
    copies[3].wait()
    out[:, part:] = (slot_score * dot(mark, stacked_parts(grads))).astype(BF16)


ENTRIES = ((0, 0), (0, 1), (0, 2), (1, 2), (1, 3), (1, 4))
PIECE = 16


def describe(groups, per_group, slots, pad, ids, gather, place, order):
    ids_now = ids[...]
    tokens = ids_now.shape[1]
    experts = groups * per_group
    hit = picked(ids_now, iota((experts, tokens), 0)) > 0.5
    rank = dot(hit.astype(BF16), before(tokens, tokens))
    code = jnp.where(hit, rank, -1.0).astype(BF16)
    lanes = experts * PIECE
    widen = (iota((experts, lanes), 1) // PIECE == iota((experts, lanes), 0)).astype(BF16)
    spread = dot_first(code, widen).astype(jnp.int32)
    row = iota((tokens, lanes), 1) % PIECE
    for n, (odd, part) in enumerate(ENTRIES):
        mark = (spread == 2 * (row % 3) + odd) & (row // 3 == part)
        gather[n * tokens : (n + 1) * tokens, :] = mark.astype(BF16)

    own_slots = slots // CORES
    rows = groups * own_slots
    at, col = iota(place.shape, 0), iota(place.shape, 1)
    tall = place.shape[1] // (len(ENTRIES) * CORES)
    row, source = at % PIECE, col % tall
    slot = source % own_slots + col // tall % CORES * own_slots
    mark = jnp.zeros(place.shape, jnp.bool_)
    for n, (odd, part) in enumerate(ENTRIES):
        mark |= (col // (CORES * tall) == n) & (row // 3 == part) & (slot == 2 * (row % 3) + odd)
    place[...] = (mark & (at // PIECE == source // own_slots) & (source < rows)).astype(BF16)

    at = iota(order.shape[1:], 0)
    inner = at % pad
    source = inner // own_slots * (PARTS * own_slots) + at // pad * own_slots + inner % own_slots
    for h in range(2):
        here = iota(order.shape[1:], 1) + h * order.shape[2]
        order[h] = ((source == here) & (inner < rows)).astype(BF16)


def round_up(n, k):
    return -(-n // k) * k


def backward(homes, order, parts, pair, pair_far, down, down_far, write, ins, grads):
    blocks = len(homes)
    pad, part = ins.shape[1] // blocks, ins.shape[2]
    for k in range(blocks):
        moved = dot(order[0], parts[2 * k]) + dot(order[1], parts[2 * k + 1])
        moved = moved.astype(BF16)
        for f in range(PARTS):
            at = slice(f * pad, (f + 1) * pad)
            ins[f, k * pad : (k + 1) * pad, :] = moved[at, :part]
            grads[f, k * pad : (k + 1) * pad, :] = moved[at, part:]
    hidden = down.shape[0]
    count = blocks * pad
    pre = [jnp.zeros((count, 2 * hidden), F32) for _ in range(2)]
    act = [jnp.zeros((count, hidden), F32) for _ in range(2)]
    for f in range(PARTS):
        lanes = slice(f * part, (f + 1) * part)
        for s, weight in enumerate((pair, pair_far)):
            pre[s] += dot_last(ins[f], weight[:, lanes])
        for s, weight in enumerate((down, down_far)):
            act[s] += dot_last(grads[f], weight[:, lanes])
    hid = []
    for s in range(2):
        gate, up = pre[s][:, :hidden], pre[s][:, hidden:]
        sig = jax.nn.sigmoid(gate)
        gate_grad = act[s] * up * sig * (1.0 + gate * (1.0 - sig))
        up_grad = act[s] * gate * sig
        hid.append(jnp.concatenate([gate_grad, up_grad], axis=1).astype(BF16))
    low = iota((count, LANES), 1) < LANES // 2

    def join(left, right):
        return jnp.where(low, left, right)

    def turn(x):
        return pltpu.roll(x, LANES // 2, 1)

    for f in range(pair.shape[1] // (10 * LANES)):
        tiles = []
        for y in (2 * f, 2 * f + 1):
            lanes = slice(5 * LANES * y, 5 * LANES * (y + 1))
            total = dot(hid[0], pair[:, lanes]) + dot(hid[1], pair_far[:, lanes])
            tiles.append([total[:, t * LANES : (t + 1) * LANES] for t in range(5)])
        a, b = tiles
        at = [turn(a[t]) for t in (2, 3, 4)]
        bt = [turn(b[t]) for t in (0, 1, 2)]
        first = [a[0], a[1], join(a[2], bt[0]), join(bt[0], bt[1]), join(bt[1], bt[2])]
        second = [join(at[0], at[1]), join(at[1], at[2]), join(at[2], b[2]), b[3], b[4]]
        for core, group in enumerate((first, second)):
            for t, tile in enumerate(group):
                for k, home in enumerate(homes):
                    write(home, core, 5 * f + t, tile[k * pad : (k + 1) * pad])


def home_of(shift, members):
    return lax.rem(lax.axis_index("member") + shift, members)


def backward_near(members, tall, order, near, *refs):
    parts, (pair, pair_far, down, down_far, out, ins, grads) = refs[:-7], refs[-7:]
    middle = order.shape[2]
    halves = [near[:middle, :], near[middle:, :]] + [p[...] for p in parts]

    def write(home, core, t, rows):
        out[home * CORES + core, t * tall : (t + 1) * tall, :] = rows[:tall].astype(BF16)

    homes = [home_of(shift, members) for shift in (0, members - 1, 1)]
    backward(homes, order, halves, pair, pair_far, down, down_far, write, ins, grads)


def backward_opposite(members, tall, order, top, bottom, pair, pair_far, down, down_far, before_out, out, ins, grads, held, done):
    del before_out

    def write(home, core, t, rows):
        held[core, t * tall : (t + 1) * tall, :] = rows[:tall].astype(BF16)

    halves = [top[...], bottom[...]]
    backward([None], order, halves, pair, pair_far, down, down_far, write, ins, grads)
    home = home_of(members // 2, members)
    copies = [
        pltpu.make_async_copy(held.at[core], out.at[home * CORES + core], done.at[core])
        for core in range(CORES)
    ]
    for copy in copies:
        copy.start()
    for copy in copies:
        copy.wait()


def total_pieces(groups, columns, tall, place, x, out):
    low = iota((tall, LANES), 1) < LANES // 2
    members = x.shape[0] // CORES
    for y in range(columns):
        sorted_entries = [[] for _ in ENTRIES]
        for c in range(CORES):
            tiles, turned = [], []
            for t in range(3):
                at = (5 * y // 2 + t) * tall
                tile = x[c, at : at + tall, :].astype(F32)
                for m in range(1, members):
                    tile += x[m * CORES + c, at : at + tall, :].astype(F32)
                tiles.append(tile)
                turned.append(pltpu.roll(tile, LANES // 2, 1))
            first = [
                jnp.where(low, turned[0], turned[1]),
                jnp.where(low, turned[1], turned[2]),
            ]
            if y % 2 == 0:
                seam = [jnp.where(low, tiles[2], 0.0), jnp.where(low, 0.0, turned[0])]
                entries = tiles[:2] + seam + first
            else:
                seam = [jnp.where(low, turned[2], 0.0), jnp.where(low, 0.0, tiles[0])]
                entries = first + seam + tiles[1:]
            for n, entry in enumerate(entries):
                sorted_entries[n].append(entry)
        stack = jnp.concatenate([e for pair in sorted_entries for e in pair], axis=0)
        moved = dot(place[...], stack.astype(BF16)).astype(BF16)
        for g in range(groups):
            out[g * columns + y] = moved[g * PIECE : (g + 1) * PIECE]


def finish(gather, x, out):
    tokens, chunk = out.shape
    found = dot(gather[...], x[...])
    part = [found[n * tokens : (n + 1) * tokens] for n in range(len(ENTRIES))]
    turned = [pltpu.roll(p, LANES // 2, 1) for p in part[3:]]
    low = iota((tokens, LANES), 1) < LANES // 2
    out[:, :LANES] = (part[0] + jnp.where(low, turned[0], turned[1])).astype(BF16)
    out[:, LANES : 2 * LANES] = (part[1] + jnp.where(low, turned[1], turned[2])).astype(BF16)
    last = (part[2] + turned[2]).astype(BF16)
    out[:, 2 * LANES :] = last[:, : chunk - 2 * LANES]


def per_device(tokens_in, out_grad, scores, expert_ids, w_in, w_down):
    groups, members = lax.axis_size("group"), lax.axis_size("member")
    columns = lax.axis_size("y")
    tokens, width = tokens_in.shape
    picks = expert_ids.shape[1]
    pairs = picks // TGROUPS
    slots = pairs * (TGROUPS * tokens // groups) // columns
    part = width // PARTS
    chunk = width // (CORES * columns)
    hidden = w_down.shape[1]
    block_rows = groups * slots // CORES
    pad, tall = round_up(block_rows, 16), round_up(block_rows, 8)
    packed_rows = block_rows * PARTS
    middle = packed_rows // 2

    def struct(shape, kind):
        return jax.ShapeDtypeStruct(shape, kind)

    def exchange(x, axis):
        return lax.all_to_all(x, axis, split_axis=0, concat_axis=0, tiled=True)

    def up(x):
        return lax.ppermute(x, "member", [(i, (i + 1) % members) for i in range(members)])

    def down(x):
        return lax.ppermute(x, "member", [(i, (i - 1) % members) for i in range(members)])

    def far(x):
        return lax.ppermute(x, "core", [(0, 1), (1, 0)])

    def bind(body, *front):
        return lambda *refs: body(*front, *refs)

    ids = expert_ids.T
    sent = call(
        bind(pack, groups, columns, slots),
        struct((packed_rows, 2 * part), BF16),
        ids, scores.T, tokens_in, out_grad,
        far={i: pltpu.HBM for i in range(4)}, room=60,
        scratch=(
            pltpu.VMEM(ids.shape, ids.dtype),
            pltpu.VMEM(ids.shape, BF16),
            pltpu.VMEM((tokens, width), BF16),
            pltpu.VMEM((tokens, width), BF16),
            pltpu.SemaphoreType.DMA((4,)),
        ),
    )
    w_pair = w_in[0].reshape(2 * hidden, width)
    w_out = w_down[0]
    sent, ids, pair_late, out_late = lax.optimization_barrier((sent, ids, w_pair, w_out))
    near = exchange(sent.reshape(groups, -1, 2 * part), "group").reshape(sent.shape)
    pair_far, out_far = far(pair_late), far(out_late)
    gather, place, order = call(
        bind(describe, groups, columns, slots, pad),
        (
            struct((len(ENTRIES) * tokens, groups * columns * PIECE), BF16),
            struct((groups * PIECE, len(ENTRIES) * CORES * tall), BF16),
            struct((2, PARTS * pad, middle), BF16),
        ),
        ids,
    )
    near, order, pair_far, out_far = lax.optimization_barrier((near, order, pair_far, out_far))
    weights = (w_pair, pair_far, w_out, out_far)

    top, bottom = near[:middle], near[middle:]
    below_top, above_bottom = up(top), down(bottom)
    below_bottom, above_top = up(bottom), down(top)
    opposite = (up(below_top), down(above_bottom))

    lane_tiles = width // (CORES * LANES)
    result = struct((members * CORES, lane_tiles * tall, LANES), BF16)

    def rows(blocks):
        return pltpu.VMEM((PARTS, blocks * pad, part), BF16)

    partial = call(
        bind(backward_near, members, tall),
        result,
        order, near, below_top, below_bottom, above_top, above_bottom, *weights,
        flops=2 * 3 * pad * width * 10 * hidden, scratch=(rows(3), rows(3)),
    )
    partial = call(
        bind(backward_opposite, members, tall),
        result,
        order, *opposite, *weights, partial,
        far={7: pl.ANY}, far_out=True, alias=7,
        flops=2 * pad * width * 10 * hidden,
        scratch=(
            rows(1),
            rows(1),
            pltpu.VMEM((CORES,) + result.shape[1:], BF16),
            pltpu.SemaphoreType.DMA((CORES,)),
        ),
    )
    pieces = call(
        bind(total_pieces, groups, columns, tall),
        struct((groups * columns, PIECE, LANES), BF16),
        place, exchange(partial, ("member", "core")),
    )
    arrived = exchange(pieces, ("group", "y")).reshape(-1, LANES)
    return call(finish, struct((tokens, chunk), BF16), gather, arrived)


def solution(mesh):
    shape = mesh.devices.shape
    split = Mesh(
        mesh.devices.reshape(shape[0], shape[1], shape[2] // 2, 2),
        ("group", "member", "y", "core"),
    )
    in_specs = (
        P(("group", "member"), None),
        P(("group", "member"), None),
        P(("group", "member"), None),
        P(("group", "member"), None),
        P(("group", "y", "core"), None, "member", None),
        P(("group", "y", "core"), "member", None),
    )
    out_specs = P(("group", "member"), ("y", "core"))
    return jax.shard_map(
        per_device, mesh=split, in_specs=in_specs, out_specs=out_specs, check_vma=False
    )
```

time: 151 us -> 149 us (0.987)
  starting transfers between devices: 41.4 us -> 37.1 us
  blocking collectives: 58.2 us -> 60.7 us
  Pallas kernels: 15.9 us -> 17.6 us
    ppermute x4 -> x2, starting transfers between devices: 8.6 us -> 4.33 us  [far(): return lax.ppermute(x, 'core', [(0, 1), (1, 0)])]
    all_to_all x2, blocking collectives: 58.2 us -> 60.7 us  [exchange(): return lax.all_to_all(x, axis, split_axis=0, concat_axis=0, tiled=True)]
    pallas_call x7 -> x6, Pallas kernels: 15.9 us -> 17.6 us  [call(): pl.pallas_call(body, out_shape=out_shape, in_specs=[pl.BlockSpec(memory_s...]
    unnamed x24 -> x22, local copies, waits for them, and re-layouts: 6.22 us -> 6.2 us
  transfers between devices with their start and end apart: 11 -> 9, of which waited for: 6 -> 5; matrix products, arithmetic and copies ran while one was open for 0% -> 0% of each run, Pallas kernels for 5% -> 5%
where the time goes in v3:
time: 149 us
  blocking collectives  60.7 us (41%)
  starting transfers between devices  37.1 us (25%)
  waiting for transfers between devices  26.7 us (18%)
  Pallas kernels  17.6 us (12%)
  local copies, waits for them, and re-layouts  6.25 us (4%)
    all_to_all x2, blocking collectives, exchange(): return lax.all_to_all(x, axis, split_axis=0, concat_axis=0, tiled=True)  60.7 us
    all_to_all x1, waiting for transfers between devices, exchange(): return lax.all_to_all(x, axis, split_axis=0, concat_axis=0, tiled=True)  20.1 us
    pallas_call x6, Pallas kernels, call(): pl.pallas_call(body, out_shape=out_shape, in_specs=[pl.BlockSpec(memory_s...  17.6 us
    all_to_all x1, starting transfers between devices, exchange(): return lax.all_to_all(x, axis, split_axis=0, concat_axis=0, tiled=True)  15.2 us
    ppermute x3, starting transfers between devices, up(): lax.ppermute(x, 'member', [(i, (i + 1) % members) for i in range(members)])  10.4 us
    ppermute x3, starting transfers between devices, down(): lax.ppermute(x, 'member', [(i, (i - 1) % members) for i in range(members)])  7.26 us
    unnamed x22, local copies, waits for them, and re-layouts  6.2 us
    ppermute x2, starting transfers between devices, far(): return lax.ppermute(x, 'core', [(0, 1), (1, 0)])  4.33 us
  transfers between devices with their start and end apart: 9, of which 5 were waited for; matrix products, arithmetic and copies ran while one was open for 0% of the time, Pallas kernels for 5%

profile of v3, /device:TPU:2, one launch (start us, length us, event | category | flops | bytes accessed | tf_op | source)
XLA Modules:
  0.0 148.6 jit_solution(14096722073962037171)
XLA Ops:
  0.0 0.0 copy-start
  0.0 0.0 copy-start.10
  0.0 3.6 %shard_map.64 = bf16[288,1280]{1,0:T(8,128)(2,1)} custom-call(s32[6,96]{1,0:T(8,128)} %bitcast.16, bf16[6,96]{1,0:T(8,128)(2,1)} %bitcast.19, bf16[96,5120]{1,0:T(8,128)(2,1)} %refs_2_.1, bf16[96,5120]{1,0:T(8,128)(2,1)} %refs_3_.1), custom_call_target="tpu_custom_call" | custom-call | bytes 1969536 | tf_op jit(solution)/shard_map/pallas_call | solution.py:27
  3.6 15.2 %all-to-all-start = ((bf16[12,24,1280]{2,1,0:T(8,128)(2,1)}), bf16[12,24,1280]{2,1,0:T(8,128)(2,1)S(1)}, u32[]{:S(2)}, u32[]{:S(2)}) async-start(bf16[12,24,1280]{2,1,0:T(8,128)(2,1)} %bitcast.18), calls=%async_computation | async-start | bytes 1474560 | tf_op jit(solution)/shard_map/all_to_all | solution.py:299
  18.7 0.0 copy-done
  18.8 1.9 %collective-permute-start = (bf16[192,5120]{1,0:T(8,128)(2,1)S(1)}, bf16[192,5120]{1,0:T(8,128)(2,1)S(1)}, u32[]{:S(2)}, u32[]{:S(2)}) collective-permute-start(bf16[192,5120]{1,0:T(8,128)(2,1)S(1)} %bitcast.7), channel_id=1, source_target_pairs={{0,1},{1,0},{2,3},{3,2},{4,5},{5,4},{6,7},{7,6},{8,9},{9,8},{10,11... | collective-permute-start | bytes 5898248 | tf_op jit(solution)/shard_map/ppermute | solution.py:308
  20.7 2.4 %collective-permute-start.1 = (bf16[96,5120]{1,0:T(8,128)(2,1)}, bf16[96,5120]{1,0:T(8,128)(2,1)S(1)}, u32[]{:S(2)}, u32[]{:S(2)}) collective-permute-start(bf16[96,5120]{1,0:T(8,128)(2,1)} %bitcast.12), channel_id=1, source_target_pairs={{0,1},{1,0},{2,3},{3,2},{4,5},{5,4},{6,7},{7,6},{8,9},{9,8},{10,11... | collective-permute-start | bytes 2949128 | tf_op jit(solution)/shard_map/ppermute | solution.py:308
  23.1 0.0 copy-done.10
  23.1 2.0 %shard_map.65 = (bf16[576,1536]{1,0:T(8,128)(2,1)S(1)}, bf16[192,480]{1,0:T(8,128)(2,1)S(1)}, bf16[2,384,144]{2,1,0:T(8,128)(2,1)S(1)}) custom-call(s32[6,96]{1,0:T(8,128)S(1)} %bitcast.17), custom_call_target="tpu_custom_call" | custom-call | bytes 2304 | tf_op jit(solution)/shard_map/pallas_call | solution.py:27
  25.1 0.0 copy-start.8
  25.1 1.2 copy-done.8
  26.3 0.0 collective-permute-done.1.refs_9_.refs_6_
  26.3 0.0 copy-start.5
  26.3 0.9 copy-done.5
  27.2 0.0 collective-permute-done.refs_7_.refs_4_
  27.2 0.0 copy-start.1
  27.3 1.3 copy-done.1
  28.6 20.1 %all-to-all-done = bf16[12,24,1280]{2,1,0:T(8,128)(2,1)S(1)} async-done(((bf16[12,24,1280]{2,1,0:T(8,128)(2,1)}), bf16[12,24,1280]{2,1,0:T(8,128)(2,1)S(1)}, u32[]{:S(2)}, u32[]{:S(2)}) %all-to-all-start) | async-done | bytes 737312 | tf_op jit(solution)/shard_map/all_to_all | solution.py:299
  48.6 0.0 copy-start.4
  48.7 3.5 %collective-permute-start.2 = (bf16[144,1280]{1,0:T(8,128)(2,1)S(1)}, bf16[144,1280]{1,0:T(8,128)(2,1)S(1)}, u32[]{:S(2)}, u32[]{:S(2)}) collective-permute-start(bf16[144,1280]{1,0:T(8,128)(2,1)S(1)} %get-tuple-element.28), channel_id=1, source_target_pairs={{0,16},{16,32},{32,48},{48,0},{1,17},{17,33},{33,49},{49,1},{2,18}... | collective-permute-start | bytes 1105928 | tf_op jit(solution)/shard_map/ppermute | solution.py:302
  52.2 2.4 %collective-permute-start.4 = (bf16[144,1280]{1,0:T(8,128)(2,1)S(1)}, bf16[144,1280]{1,0:T(8,128)(2,1)S(1)}, u32[]{:S(2)}, u32[]{:S(2)}) collective-permute-start(bf16[144,1280]{1,0:T(8,128)(2,1)S(1)} %get-tuple-element.27), channel_id=1, source_target_pairs={{0,48},{16,0},{32,16},{48,32},{1,49},{17,1},{33,17},{49,33},{2,50}... | collective-permute-start | bytes 1105928 | tf_op jit(solution)/shard_map/ppermute | solution.py:305
  54.7 3.4 %collective-permute-start.6 = (bf16[144,1280]{1,0:T(8,128)(2,1)S(1)}, bf16[144,1280]{1,0:T(8,128)(2,1)S(1)}, u32[]{:S(2)}, u32[]{:S(2)}) collective-permute-start(bf16[144,1280]{1,0:T(8,128)(2,1)S(1)} %get-tuple-element.27), channel_id=1, source_target_pairs={{0,16},{16,32},{32,48},{48,0},{1,17},{17,33},{33,49},{49,1},{2,18}... | collective-permute-start | bytes 1105928 | tf_op jit(solution)/shard_map/ppermute | solution.py:302
  58.1 2.4 %collective-permute-start.7 = (bf16[144,1280]{1,0:T(8,128)(2,1)S(1)}, bf16[144,1280]{1,0:T(8,128)(2,1)S(1)}, u32[]{:S(2)}, u32[]{:S(2)}) collective-permute-start(bf16[144,1280]{1,0:T(8,128)(2,1)S(1)} %get-tuple-element.28), channel_id=1, source_target_pairs={{0,48},{16,0},{32,16},{48,32},{1,49},{17,1},{33,17},{49,33},{2,50}... | collective-permute-start | bytes 1105928 | tf_op jit(solution)/shard_map/ppermute | solution.py:305
  60.5 0.8 collective-permute-done.2.refs_2_
  61.4 3.4 %collective-permute-start.3 = (bf16[144,1280]{1,0:T(8,128)(2,1)S(1)}, bf16[144,1280]{1,0:T(8,128)(2,1)S(1)}, u32[]{:S(2)}, u32[]{:S(2)}) collective-permute-start(bf16[144,1280]{1,0:T(8,128)(2,1)S(1)} %collective-permute-done.2.refs_2_), channel_id=1, source_target_pairs={{0,16},{16,32},{32,48},{48,0},{1,17},{17,33},{33,49},{49,1},{2,18}... | collective-permute-start | bytes 1105928 | tf_op jit(solution)/shard_map/ppermute | solution.py:302
  64.8 0.3 collective-permute-done.4.refs_5_
  65.1 2.4 %collective-permute-start.5 = (bf16[144,1280]{1,0:T(8,128)(2,1)S(1)}, bf16[144,1280]{1,0:T(8,128)(2,1)S(1)}, u32[]{:S(2)}, u32[]{:S(2)}) collective-permute-start(bf16[144,1280]{1,0:T(8,128)(2,1)S(1)} %collective-permute-done.4.refs_5_), channel_id=1, source_target_pairs={{0,48},{16,0},{32,16},{48,32},{1,49},{17,1},{33,17},{49,33},{2,50}... | collective-permute-start | bytes 1105928 | tf_op jit(solution)/shard_map/ppermute | solution.py:305
  67.5 1.7 %collective-permute-done.6.refs_3_ = bf16[144,1280]{1,0:T(8,128)(2,1)S(1)} collective-permute-done((bf16[144,1280]{1,0:T(8,128)(2,1)S(1)}, bf16[144,1280]{1,0:T(8,128)(2,1)S(1)}, u32[]{:S(2)}, u32[]{:S(2)}) %collective-permute-start.6) | collective-permute-done | bytes 368672 | tf_op jit(solution)/shard_map/ppermute | solution.py:302
  69.3 3.8 %collective-permute-done.7.refs_4_ = bf16[144,1280]{1,0:T(8,128)(2,1)S(1)} collective-permute-done((bf16[144,1280]{1,0:T(8,128)(2,1)S(1)}, bf16[144,1280]{1,0:T(8,128)(2,1)S(1)}, u32[]{:S(2)}, u32[]{:S(2)}) %collective-permute-start.7) | collective-permute-done | bytes 368672 | tf_op jit(solution)/shard_map/ppermute | solution.py:305
  73.0 0.0 copy-done.4
  73.0 0.0 copy-start.2
  73.0 1.5 %copy-done.2 = bf16[192,5120]{1,0:T(8,128)(2,1)S(1)} copy-done((bf16[192,5120]{1,0:T(8,128)(2,1)S(1)}, bf16[192,5120]{1,0:T(8,128)(2,1)}, u32[]{:S(2)}) %copy-start.2) | copy-done | bytes 1966104
  74.6 0.0 copy-start.6
  74.6 1.2 copy-done.6
  75.8 0.0 copy-start.3
  75.8 0.0 copy-start.7
  75.8 5.2 %shard_map.66.refs_7_ = bf16[8,800,128]{2,1,0:T(8,128)(2,1)S(1)} custom-call(bf16[2,384,144]{2,1,0:T(8,128)(2,1)S(1)} %get-tuple-element.23.refs_0_, bf16[288,1280]{1,0:T(8,128)(2,1)S(1)} %bitcast.11, bf16[144,1280]{1,0:T(8,128)(2,1)S(1)} %collective-permute-done.2.refs_2_, bf16[144,1280]{1,0:T(8,128)(2,1)S(1)} %collective-permute-done.6.refs_3_, ...), custom_call_target="tpu_custom_call" | custom-call | flops 1415577600 | bytes 8331264 | tf_op jit(solution)/shard_map/pallas_call | solution.py:27
  81.0 0.0 collective-permute-done.3.refs_1_
  81.0 0.0 collective-permute-done.5.refs_2_
  81.0 0.0 copy-done.3
  81.0 0.0 copy-done.7
  81.0 4.9 %shard_map.67 = bf16[8,800,128]{2,1,0:T(8,128)(2,1)S(1)} custom-call(bf16[2,384,144]{2,1,0:T(8,128)(2,1)S(1)} %get-tuple-element.23.refs_0_, bf16[144,1280]{1,0:T(8,128)(2,1)S(1)} %collective-permute-done.3.refs_1_, bf16[144,1280]{1,0:T(8,128)(2,1)S(1)} %collective-permute-done.5.refs_2_, ...), custom_call_target="tpu_custom_call", output_to_operand_aliasing={{}: (7, {})} | custom-call | flops 471859200 | bytes 8495104 | tf_op jit(solution)/shard_map/pallas_call | solution.py:27
  85.9 25.4 %all_to_all.15.refs_1_ = bf16[8,800,128]{2,1,0:T(8,128)(2,1)S(1)} all-to-all(bf16[8,800,128]{2,1,0:T(8,128)(2,1)S(1)} %shard_map.67), channel_id=1, replica_groups=mesh['group'=12,'member'=4,'y'=8,'core'=2] {'member','core'}, dimensions={0} | all-to-all | bytes 3276800 | tf_op jit(solution)/shard_map/all_to_all | solution.py:299
  111.3 0.0 copy-start.9
  111.3 0.7 shard_map.68
  111.9 35.4 %all_to_all.16 = bf16[96,16,128]{2,1,0:T(8,128)(2,1)S(1)} all-to-all(bf16[96,16,128]{2,1,0:T(8,128)(2,1)S(1)} %shard_map.68), channel_id=1, replica_groups=mesh['group'=12,'member'=4,'y'=8,'core'=2] {'group','y'}, dimensions={0} | all-to-all | bytes 786432 | tf_op jit(solution)/shard_map/all_to_all | solution.py:299
  147.3 0.0 copy-done.9
  147.3 1.3 shard_map.69
  (1 shorter events, 0.0 us)
Async XLA Ops:
  0.0 18.7 %copy-start = (bf16[1,2,96,5120]{3,2,1,0:T(8,128)(2,1)S(1)}, bf16[1,2,96,5120]{3,2,1,0:T(8,128)(2,1)}, u32[]{:S(2)}) copy-start(bf16[1,2,96,5120]{3,2,1,0:T(8,128)(2,1)} %param.10) | copy-start | bytes 5898244
  0.0 23.1 %copy-start.10 = (s32[96,6]{0,1:T(8,128)S(1)}, s32[96,6]{0,1:T(8,128)}, u32[]{:S(2)}) copy-start(s32[96,6]{0,1:T(8,128)} %param.9) | copy-start | bytes 6916
  3.6 45.1 %all-to-all-start = ((bf16[12,24,1280]{2,1,0:T(8,128)(2,1)}), bf16[12,24,1280]{2,1,0:T(8,128)(2,1)S(1)}, u32[]{:S(2)}, u32[]{:S(2)}) async-start(bf16[12,24,1280]{2,1,0:T(8,128)(2,1)} %bitcast.18), calls=%async_computation | async-start | bytes 1474560 | tf_op jit(solution)/shard_map/all_to_all | solution.py:299
  18.8 8.5 %collective-permute-start = (bf16[192,5120]{1,0:T(8,128)(2,1)S(1)}, bf16[192,5120]{1,0:T(8,128)(2,1)S(1)}, u32[]{:S(2)}, u32[]{:S(2)}) collective-permute-start(bf16[192,5120]{1,0:T(8,128)(2,1)S(1)} %bitcast.7), channel_id=1, source_target_pairs={{0,1},{1,0},{2,3},{3,2},{4,5},{5,4},{6,7},{7,6},{8,9},{9,8},{10,11... | collective-permute-start | bytes 5898248 | tf_op jit(solution)/shard_map/ppermute | solution.py:308
  20.7 5.6 %collective-permute-start.1 = (bf16[96,5120]{1,0:T(8,128)(2,1)}, bf16[96,5120]{1,0:T(8,128)(2,1)S(1)}, u32[]{:S(2)}, u32[]{:S(2)}) collective-permute-start(bf16[96,5120]{1,0:T(8,128)(2,1)} %bitcast.12), channel_id=1, source_target_pairs={{0,1},{1,0},{2,3},{3,2},{4,5},{5,4},{6,7},{7,6},{8,9},{9,8},{10,11... | collective-permute-start | bytes 2949128 | tf_op jit(solution)/shard_map/ppermute | solution.py:308
  25.1 1.2 copy-start.8
  26.3 0.9 copy-start.5
  27.2 1.3 copy-start.1
  48.6 24.4 %copy-start.4 = (bf16[1,96,5120]{2,1,0:T(8,128)(2,1)S(1)}, bf16[1,96,5120]{2,1,0:T(8,128)(2,1)}, u32[]{:S(2)}) copy-start(bf16[1,96,5120]{2,1,0:T(8,128)(2,1)} %param.11) | copy-start | bytes 2949124
  48.7 12.7 %collective-permute-start.2 = (bf16[144,1280]{1,0:T(8,128)(2,1)S(1)}, bf16[144,1280]{1,0:T(8,128)(2,1)S(1)}, u32[]{:S(2)}, u32[]{:S(2)}) collective-permute-start(bf16[144,1280]{1,0:T(8,128)(2,1)S(1)} %get-tuple-element.28), channel_id=1, source_target_pairs={{0,16},{16,32},{32,48},{48,0},{1,17},{17,33},{33,49},{49,1},{2,18}... | collective-permute-start | bytes 1105928 | tf_op jit(solution)/shard_map/ppermute | solution.py:302
  52.2 12.9 %collective-permute-start.4 = (bf16[144,1280]{1,0:T(8,128)(2,1)S(1)}, bf16[144,1280]{1,0:T(8,128)(2,1)S(1)}, u32[]{:S(2)}, u32[]{:S(2)}) collective-permute-start(bf16[144,1280]{1,0:T(8,128)(2,1)S(1)} %get-tuple-element.27), channel_id=1, source_target_pairs={{0,48},{16,0},{32,16},{48,32},{1,49},{17,1},{33,17},{49,33},{2,50}... | collective-permute-start | bytes 1105928 | tf_op jit(solution)/shard_map/ppermute | solution.py:305
  54.7 14.6 %collective-permute-start.6 = (bf16[144,1280]{1,0:T(8,128)(2,1)S(1)}, bf16[144,1280]{1,0:T(8,128)(2,1)S(1)}, u32[]{:S(2)}, u32[]{:S(2)}) collective-permute-start(bf16[144,1280]{1,0:T(8,128)(2,1)S(1)} %get-tuple-element.27), channel_id=1, source_target_pairs={{0,16},{16,32},{32,48},{48,0},{1,17},{17,33},{33,49},{49,1},{2,18}... | collective-permute-start | bytes 1105928 | tf_op jit(solution)/shard_map/ppermute | solution.py:302
  58.1 14.9 %collective-permute-start.7 = (bf16[144,1280]{1,0:T(8,128)(2,1)S(1)}, bf16[144,1280]{1,0:T(8,128)(2,1)S(1)}, u32[]{:S(2)}, u32[]{:S(2)}) collective-permute-start(bf16[144,1280]{1,0:T(8,128)(2,1)S(1)} %get-tuple-element.28), channel_id=1, source_target_pairs={{0,48},{16,0},{32,16},{48,32},{1,49},{17,1},{33,17},{49,33},{2,50}... | collective-permute-start | bytes 1105928 | tf_op jit(solution)/shard_map/ppermute | solution.py:305
  61.4 19.6 %collective-permute-start.3 = (bf16[144,1280]{1,0:T(8,128)(2,1)S(1)}, bf16[144,1280]{1,0:T(8,128)(2,1)S(1)}, u32[]{:S(2)}, u32[]{:S(2)}) collective-permute-start(bf16[144,1280]{1,0:T(8,128)(2,1)S(1)} %collective-permute-done.2.refs_2_), channel_id=1, source_target_pairs={{0,16},{16,32},{32,48},{48,0},{1,17},{17,33},{33,49},{49,1},{2,18}... | collective-permute-start | bytes 1105928 | tf_op jit(solution)/shard_map/ppermute | solution.py:302
  65.1 15.9 %collective-permute-start.5 = (bf16[144,1280]{1,0:T(8,128)(2,1)S(1)}, bf16[144,1280]{1,0:T(8,128)(2,1)S(1)}, u32[]{:S(2)}, u32[]{:S(2)}) collective-permute-start(bf16[144,1280]{1,0:T(8,128)(2,1)S(1)} %collective-permute-done.4.refs_5_), channel_id=1, source_target_pairs={{0,48},{16,0},{32,16},{48,32},{1,49},{17,1},{33,17},{49,33},{2,50}... | collective-permute-start | bytes 1105928 | tf_op jit(solution)/shard_map/ppermute | solution.py:305
  73.0 1.5 %copy-start.2 = (bf16[192,5120]{1,0:T(8,128)(2,1)S(1)}, bf16[192,5120]{1,0:T(8,128)(2,1)}, u32[]{:S(2)}) copy-start(bf16[192,5120]{1,0:T(8,128)(2,1)} %copy-done.1) | copy-start | bytes 5898244
  74.6 1.2 copy-start.6
  75.8 5.2 %copy-start.3 = (bf16[192,5120]{1,0:T(8,128)(2,1)S(1)}, bf16[192,5120]{1,0:T(8,128)(2,1)}, u32[]{:S(2)}) copy-start(bf16[192,5120]{1,0:T(8,128)(2,1)} %copy-done.1) | copy-start | bytes 5898244
  75.8 5.2 %copy-start.7 = (bf16[96,5120]{1,0:T(8,128)(2,1)S(1)}, bf16[96,5120]{1,0:T(8,128)(2,1)}, u32[]{:S(2)}) copy-start(bf16[96,5120]{1,0:T(8,128)(2,1)} %copy-done.5) | copy-start | bytes 2949124
  111.3 36.0 %copy-start.9 = (bf16[576,1536]{1,0:T(8,128)(2,1)S(1)}, bf16[576,1536]{1,0:T(8,128)(2,1)}, u32[]{:S(2)}) copy-start(bf16[576,1536]{1,0:T(8,128)(2,1)} %copy-done.8) | copy-start | bytes 5308420

commit v4 on v3

--- a/solution.py
+++ b/solution.py
@@ -108,7 +108,7 @@
 PIECE = 16
 
 
-def describe(groups, per_group, slots, pad, ids, gather, place, order):
+def describe(groups, per_group, slots, ids, gather, place, order):
     ids_now = ids[...]
     tokens = ids_now.shape[1]
     experts = groups * per_group
@@ -134,45 +134,51 @@
         mark |= (col // (CORES * tall) == n) & (row // 3 == part) & (slot == 2 * (row % 3) + odd)
     place[...] = (mark & (at // PIECE == source // own_slots) & (source < rows)).astype(BF16)
 
-    at = iota(order.shape[1:], 0)
-    inner = at % pad
-    source = inner // own_slots * (PARTS * own_slots) + at // pad * own_slots + inner % own_slots
+    span = order.shape[1] // PARTS
+    at, here = iota(order.shape[1:], 0), iota(order.shape[1:], 1)
     for h in range(2):
-        here = iota(order.shape[1:], 1) + h * order.shape[2]
-        order[h] = ((source == here) & (inner < rows)).astype(BF16)
+        inner = at % span + h * (tall - span - rows // 2)
+        source = inner // own_slots * (PARTS * own_slots) + at // span * own_slots + inner % own_slots
+        order[h] = ((source == here) & (inner >= 0) & (inner < rows // 2)).astype(BF16)
 
 
 def round_up(n, k):
     return -(-n // k) * k
 
 
-def backward(homes, order, parts, pair, pair_far, down, down_far, write, ins, grads):
-    blocks = len(homes)
-    pad, part = ins.shape[1] // blocks, ins.shape[2]
-    for k in range(blocks):
-        moved = dot(order[0], parts[2 * k]) + dot(order[1], parts[2 * k + 1])
-        moved = moved.astype(BF16)
+def backward(homes, tall, order, halves, ready, pairs, downs, write, ins, grads):
+    span = order.shape[1] // PARTS
+    apart = tall - span
+    wide = ins.shape[2]
+    part = wide // 2
+    for k in range(len(homes)):
+        a, b = dot(order[0], halves[2 * k]), dot(order[1], halves[2 * k + 1])
         for f in range(PARTS):
-            at = slice(f * pad, (f + 1) * pad)
-            ins[f, k * pad : (k + 1) * pad, :] = moved[at, :part]
-            grads[f, k * pad : (k + 1) * pad, :] = moved[at, part:]
-    hidden = down.shape[0]
-    count = blocks * pad
-    pre = [jnp.zeros((count, 2 * hidden), F32) for _ in range(2)]
-    act = [jnp.zeros((count, hidden), F32) for _ in range(2)]
-    for f in range(PARTS):
-        lanes = slice(f * part, (f + 1) * part)
-        for s, weight in enumerate((pair, pair_far)):
-            pre[s] += dot_last(ins[f], weight[:, lanes])
-        for s, weight in enumerate((down, down_far)):
-            act[s] += dot_last(grads[f], weight[:, lanes])
-    hid = []
-    for s in range(2):
-        gate, up = pre[s][:, :hidden], pre[s][:, hidden:]
+            at = f * span
+            seam = a[at + apart : at + span] + b[at : at + span - apart]
+            block = [a[at : at + apart], seam, b[at + span - apart : at + span]]
+            block = jnp.concatenate(block, axis=0).astype(BF16)
+            rows, lanes = slice(k * tall, (k + 1) * tall), slice(f % 2 * part, (f % 2 + 1) * part)
+            ins[f // 2, rows, lanes] = block[:, :part]
+            grads[f // 2, rows, lanes] = block[:, part:]
+    for copy in ready:
+        copy.wait()
+    hidden = downs.shape[0] // CORES
+    count = ins.shape[1]
+    pre = jnp.zeros((2 * CORES * hidden, count), F32)
+    act = jnp.zeros((CORES * hidden, count), F32)
+    for f in range(PARTS // 2):
+        lanes = slice(f * wide, (f + 1) * wide)
+        pre += dot_last(pairs[:, lanes], ins[f])
+        act += dot_last(downs[:, lanes], grads[f])
+    parts = []
+    for s in range(CORES):
+        gate, up = pre[2 * s * hidden :][:hidden], pre[(2 * s + 1) * hidden :][:hidden]
+        slope = act[s * hidden :][:hidden]
         sig = jax.nn.sigmoid(gate)
-        gate_grad = act[s] * up * sig * (1.0 + gate * (1.0 - sig))
-        up_grad = act[s] * gate * sig
-        hid.append(jnp.concatenate([gate_grad, up_grad], axis=1).astype(BF16))
+        parts.append(slope * up * sig * (1.0 + gate * (1.0 - sig)))
+        parts.append(slope * gate * sig)
+    hid = jnp.concatenate(parts, axis=0).T.astype(BF16)
     low = iota((count, LANES), 1) < LANES // 2
 
     def join(left, right):
@@ -181,11 +187,11 @@
     def turn(x):
         return pltpu.roll(x, LANES // 2, 1)
 
-    for f in range(pair.shape[1] // (10 * LANES)):
+    for f in range(pairs.shape[1] // (10 * LANES)):
         tiles = []
         for y in (2 * f, 2 * f + 1):
             lanes = slice(5 * LANES * y, 5 * LANES * (y + 1))
-            total = dot(hid[0], pair[:, lanes]) + dot(hid[1], pair_far[:, lanes])
+            total = dot(hid, pairs[:, lanes])
             tiles.append([total[:, t * LANES : (t + 1) * LANES] for t in range(5)])
         a, b = tiles
         at = [turn(a[t]) for t in (2, 3, 4)]
@@ -195,7 +201,7 @@
         for core, group in enumerate((first, second)):
             for t, tile in enumerate(group):
                 for k, home in enumerate(homes):
-                    write(home, core, 5 * f + t, tile[k * pad : (k + 1) * pad])
+                    write(home, core, 5 * f + t, tile[k * tall : (k + 1) * tall])
 
 
 def home_of(shift, members):
@@ -203,32 +209,42 @@
 
 
 def backward_near(members, tall, order, near, *refs):
-    parts, (pair, pair_far, down, down_far, out, ins, grads) = refs[:-7], refs[-7:]
-    middle = order.shape[2]
-    halves = [near[:middle, :], near[middle:, :]] + [p[...] for p in parts]
-
-    def write(home, core, t, rows):
-        out[home * CORES + core, t * tall : (t + 1) * tall, :] = rows[:tall].astype(BF16)
-
-    homes = [home_of(shift, members) for shift in (0, members - 1, 1)]
-    backward(homes, order, halves, pair, pair_far, down, down_far, write, ins, grads)
-
-
-def backward_opposite(members, tall, order, top, bottom, pair, pair_far, down, down_far, before_out, out, ins, grads, held, done):
-    del before_out
-
-    def write(home, core, t, rows):
-        held[core, t * tall : (t + 1) * tall, :] = rows[:tall].astype(BF16)
-
-    halves = [top[...], bottom[...]]
-    backward([None], order, halves, pair, pair_far, down, down_far, write, ins, grads)
-    home = home_of(members // 2, members)
+    parts, weights, (out, pairs, downs, ins, grads, done) = refs[:4], refs[4:8], refs[8:]
+    deep, flat = pairs.shape[0] // CORES, downs.shape[0] // CORES
+    targets = (pairs.at[:deep], pairs.at[deep:], downs.at[:flat], downs.at[flat:])
     copies = [
-        pltpu.make_async_copy(held.at[core], out.at[home * CORES + core], done.at[core])
-        for core in range(CORES)
+        pltpu.make_async_copy(source, target, done.at[n])
+        for n, (source, target) in enumerate(zip(weights, targets))
     ]
     for copy in copies:
         copy.start()
+    middle = order.shape[2]
+    halves = [near[:middle, :], near[middle:, :]] + [p[...] for p in parts]
+
+    def write(home, core, t, rows):
+        out[home * CORES + core, t * tall : (t + 1) * tall, :] = rows.astype(BF16)
+
+    homes = [home_of(shift, members) for shift in (0, members - 1, 1)]
+    backward(homes, tall, order, halves, copies, pairs, downs, write, ins, grads)
+
+
+def backward_opposite(members, tall, order, top, bottom, pairs, downs, *refs):
+    out, ins, grads, held, sent = refs[1:]
+    home = home_of(members // 2, members)
+    copies = []
+
+    def write(_, core, t, rows):
+        held[core, t * tall : (t + 1) * tall, :] = rows.astype(BF16)
+        if t % 5 == 4:
+            at = pl.ds((t - 4) * tall, 5 * tall)
+            copy = pltpu.make_async_copy(
+                held.at[core, at], out.at[home * CORES + core, at], sent.at[core, t // 5]
+            )
+            copy.start()
+            copies.append(copy)
+
+    halves = [top[...], bottom[...]]
+    backward([home], tall, order, halves, [], pairs, downs, write, ins, grads)
     for copy in copies:
         copy.wait()
 
@@ -288,7 +304,7 @@
     chunk = width // (CORES * columns)
     hidden = w_down.shape[1]
     block_rows = groups * slots // CORES
-    pad, tall = round_up(block_rows, 16), round_up(block_rows, 8)
+    tall, span = round_up(block_rows, 8), round_up(block_rows // 2, 8)
     packed_rows = block_rows * PARTS
     middle = packed_rows // 2
 
@@ -330,45 +346,52 @@
     near = exchange(sent.reshape(groups, -1, 2 * part), "group").reshape(sent.shape)
     pair_far, out_far = far(pair_late), far(out_late)
     gather, place, order = call(
-        bind(describe, groups, columns, slots, pad),
+        bind(describe, groups, columns, slots),
         (
             struct((len(ENTRIES) * tokens, groups * columns * PIECE), BF16),
             struct((groups * PIECE, len(ENTRIES) * CORES * tall), BF16),
-            struct((2, PARTS * pad, middle), BF16),
+            struct((2, PARTS * span, middle), BF16),
         ),
         ids,
     )
-    near, order, pair_far, out_far = lax.optimization_barrier((near, order, pair_far, out_far))
+    near, order = lax.optimization_barrier((near, order))
     weights = (w_pair, pair_far, w_out, out_far)
 
     top, bottom = near[:middle], near[middle:]
     below_top, above_bottom = up(top), down(bottom)
-    below_bottom, above_top = up(bottom), down(top)
+    below_bottom = up(bottom)
+    above_top = down(top)
     opposite = (up(below_top), down(above_bottom))
 
     lane_tiles = width // (CORES * LANES)
     result = struct((members * CORES, lane_tiles * tall, LANES), BF16)
 
     def rows(blocks):
-        return pltpu.VMEM((PARTS, blocks * pad, part), BF16)
-
-    partial = call(
+        return pltpu.VMEM((PARTS // 2, blocks * tall, 2 * part), BF16)
+
+    partial, pairs_all, downs_all = call(
         bind(backward_near, members, tall),
-        result,
+        (
+            result,
+            struct((CORES * 2 * hidden, width), BF16),
+            struct((CORES * hidden, width), BF16),
+        ),
         order, near, below_top, below_bottom, above_top, above_bottom, *weights,
-        flops=2 * 3 * pad * width * 10 * hidden, scratch=(rows(3), rows(3)),
+        far={6: pl.ANY, 7: pltpu.HBM, 8: pl.ANY, 9: pltpu.HBM},
+        flops=2 * 3 * tall * width * 10 * hidden,
+        scratch=(rows(3), rows(3), pltpu.SemaphoreType.DMA((4,))),
     )
     partial = call(
         bind(backward_opposite, members, tall),
         result,
-        order, *opposite, *weights, partial,
-        far={7: pl.ANY}, far_out=True, alias=7,
-        flops=2 * pad * width * 10 * hidden,
+        order, *opposite, pairs_all, downs_all, partial,
+        far={5: pl.ANY}, far_out=True, alias=5,
+        flops=2 * tall * width * 10 * hidden,
         scratch=(
             rows(1),
             rows(1),
             pltpu.VMEM((CORES,) + result.shape[1:], BF16),
-            pltpu.SemaphoreType.DMA((CORES,)),
+            pltpu.SemaphoreType.DMA((CORES, lane_tiles // 5)),
         ),
     )
     pieces = call(

time: 149 us -> 148 us (level)
  local copies, waits for them, and re-layouts: 6.25 us -> 1.25 us
  waiting for transfers between devices: 26.7 us -> 29 us
    unnamed x22 -> x10, local copies, waits for them, and re-layouts: 6.2 us -> 1.2 us
    all_to_all x1, waiting for transfers between devices: 20.1 us -> 22.4 us  [exchange(): return lax.all_to_all(x, axis, split_axis=0, concat_axis=0, tiled=True)]
  transfers between devices with their start and end apart: 9 -> 9, of which waited for: 5 -> 5; matrix products, arithmetic and copies ran while one was open for 0% -> 0% of each run, Pallas kernels for 5% -> 6%
where the time goes in v4:
time: 148 us; the launch traced here: 147 us
  blocking collectives  61 us (41%)
  starting transfers between devices  37.1 us (25%)
  waiting for transfers between devices  29 us (20%)
  Pallas kernels  18.4 us (12%)
    all_to_all x2, blocking collectives, exchange(): return lax.all_to_all(x, axis, split_axis=0, concat_axis=0, tiled=True)  61 us
    all_to_all x1, waiting for transfers between devices, exchange(): return lax.all_to_all(x, axis, split_axis=0, concat_axis=0, tiled=True)  22.4 us
    pallas_call x6, Pallas kernels, call(): pl.pallas_call(body, out_shape=out_shape, in_specs=[pl.BlockSpec(memory_s...  18.4 us
    all_to_all x1, starting transfers between devices, exchange(): return lax.all_to_all(x, axis, split_axis=0, concat_axis=0, tiled=True)  15.2 us
    ppermute x3, starting transfers between devices, up(): lax.ppermute(x, 'member', [(i, (i + 1) % members) for i in range(members)])  10.3 us
    ppermute x3, starting transfers between devices, down(): lax.ppermute(x, 'member', [(i, (i - 1) % members) for i in range(members)])  7.31 us
    ppermute x2, starting transfers between devices, far(): return lax.ppermute(x, 'core', [(0, 1), (1, 0)])  4.33 us
    ppermute x3, waiting for transfers between devices, down(): lax.ppermute(x, 'member', [(i, (i - 1) % members) for i in range(members)])  4.04 us
  transfers between devices with their start and end apart: 9, of which 5 were waited for; matrix products, arithmetic and copies ran while one was open for 0% of the time, Pallas kernels for 6%

profile of v4, /device:TPU:2, one launch (start us, length us, event | category | flops | bytes accessed | tf_op | source)
XLA Modules:
  0.0 147.0 jit_solution(7442896268406122759)
XLA Ops:
  0.0 0.0 copy-start
  0.0 0.0 copy-start.4
  0.0 3.6 %shard_map.64 = bf16[288,1280]{1,0:T(8,128)(2,1)} custom-call(s32[6,96]{1,0:T(8,128)} %bitcast.14, bf16[6,96]{1,0:T(8,128)(2,1)} %bitcast.17, bf16[96,5120]{1,0:T(8,128)(2,1)} %refs_2_.1, bf16[96,5120]{1,0:T(8,128)(2,1)} %refs_3_.1), custom_call_target="tpu_custom_call" | custom-call | bytes 1969536 | tf_op jit(solution)/shard_map/pallas_call | solution.py:27
  3.6 15.2 %all-to-all-start = ((bf16[12,24,1280]{2,1,0:T(8,128)(2,1)}), bf16[12,24,1280]{2,1,0:T(8,128)(2,1)S(1)}, u32[]{:S(2)}, u32[]{:S(2)}) async-start(bf16[12,24,1280]{2,1,0:T(8,128)(2,1)} %bitcast.16), calls=%async_computation | async-start | bytes 1474560 | tf_op jit(solution)/shard_map/all_to_all | solution.py:315
  18.7 0.0 copy-done
  18.7 1.9 %collective-permute-start.6 = (bf16[192,5120]{1,0:T(8,128)(2,1)S(1)}, bf16[192,5120]{1,0:T(8,128)(2,1)}, u32[]{:S(2)}, u32[]{:S(2)}) collective-permute-start(bf16[192,5120]{1,0:T(8,128)(2,1)S(1)} %bitcast.9), channel_id=1, source_target_pairs={{0,1},{1,0},{2,3},{3,2},{4,5},{5,4},{6,7},{7,6},{8,9},{9,8},{10,11... | collective-permute-start | bytes 5898248 | tf_op jit(solution)/shard_map/ppermute | solution.py:324
  20.7 2.4 %collective-permute-start.7 = (bf16[96,5120]{1,0:T(8,128)(2,1)}, bf16[96,5120]{1,0:T(8,128)(2,1)}, u32[]{:S(2)}, u32[]{:S(2)}) collective-permute-start(bf16[96,5120]{1,0:T(8,128)(2,1)} %bitcast.12), channel_id=1, source_target_pairs={{0,1},{1,0},{2,3},{3,2},{4,5},{5,4},{6,7},{7,6},{8,9},{9,8},{10,11... | collective-permute-start | bytes 2949128 | tf_op jit(solution)/shard_map/ppermute | solution.py:324
  23.1 0.0 copy-done.4
  23.1 1.9 %shard_map.65 = (bf16[576,1536]{1,0:T(8,128)(2,1)S(1)}, bf16[192,480]{1,0:T(8,128)(2,1)S(1)}, bf16[2,192,144]{2,1,0:T(8,128)(2,1)S(1)}) custom-call(s32[6,96]{1,0:T(8,128)S(1)} %bitcast.15), custom_call_target="tpu_custom_call" | custom-call | bytes 2304 | tf_op jit(solution)/shard_map/pallas_call | solution.py:27
  25.0 0.0 copy-start.1
  25.0 1.2 copy-done.1
  26.2 22.4 %all-to-all-done = bf16[12,24,1280]{2,1,0:T(8,128)(2,1)S(1)} async-done(((bf16[12,24,1280]{2,1,0:T(8,128)(2,1)}), bf16[12,24,1280]{2,1,0:T(8,128)(2,1)S(1)}, u32[]{:S(2)}, u32[]{:S(2)}) %all-to-all-start) | async-done | bytes 737312 | tf_op jit(solution)/shard_map/all_to_all | solution.py:315
  48.6 0.0 copy-start.3
  48.7 3.5 %collective-permute-start = (bf16[144,1280]{1,0:T(8,128)(2,1)S(1)}, bf16[144,1280]{1,0:T(8,128)(2,1)S(1)}, u32[]{:S(2)}, u32[]{:S(2)}) collective-permute-start(bf16[144,1280]{1,0:T(8,128)(2,1)S(1)} %get-tuple-element.30), channel_id=1, source_target_pairs={{0,16},{16,32},{32,48},{48,0},{1,17},{17,33},{33,49},{49,1},{2,18}... | collective-permute-start | bytes 1105928 | tf_op jit(solution)/shard_map/ppermute | solution.py:318
  52.2 2.4 %collective-permute-start.2 = (bf16[144,1280]{1,0:T(8,128)(2,1)S(1)}, bf16[144,1280]{1,0:T(8,128)(2,1)S(1)}, u32[]{:S(2)}, u32[]{:S(2)}) collective-permute-start(bf16[144,1280]{1,0:T(8,128)(2,1)S(1)} %get-tuple-element.29), channel_id=1, source_target_pairs={{0,48},{16,0},{32,16},{48,32},{1,49},{17,1},{33,17},{49,33},{2,50}... | collective-permute-start | bytes 1105928 | tf_op jit(solution)/shard_map/ppermute | solution.py:321
  54.7 3.4 %collective-permute-start.4 = (bf16[144,1280]{1,0:T(8,128)(2,1)S(1)}, bf16[144,1280]{1,0:T(8,128)(2,1)S(1)}, u32[]{:S(2)}, u32[]{:S(2)}) collective-permute-start(bf16[144,1280]{1,0:T(8,128)(2,1)S(1)} %get-tuple-element.29), channel_id=1, source_target_pairs={{0,16},{16,32},{32,48},{48,0},{1,17},{17,33},{33,49},{49,1},{2,18}... | collective-permute-start | bytes 1105928 | tf_op jit(solution)/shard_map/ppermute | solution.py:318
  58.1 0.0 collective-permute-done.7.refs_9_
  58.1 2.4 %collective-permute-start.5 = (bf16[144,1280]{1,0:T(8,128)(2,1)S(1)}, bf16[144,1280]{1,0:T(8,128)(2,1)S(1)}, u32[]{:S(2)}, u32[]{:S(2)}) collective-permute-start(bf16[144,1280]{1,0:T(8,128)(2,1)S(1)} %get-tuple-element.30), channel_id=1, source_target_pairs={{0,48},{16,0},{32,16},{48,32},{1,49},{17,1},{33,17},{49,33},{2,50}... | collective-permute-start | bytes 1105928 | tf_op jit(solution)/shard_map/ppermute | solution.py:321
  60.6 0.8 collective-permute-done.refs_2_
  61.4 3.4 %collective-permute-start.1 = (bf16[144,1280]{1,0:T(8,128)(2,1)S(1)}, bf16[144,1280]{1,0:T(8,128)(2,1)S(1)}, u32[]{:S(2)}, u32[]{:S(2)}) collective-permute-start(bf16[144,1280]{1,0:T(8,128)(2,1)S(1)} %collective-permute-done.refs_2_), channel_id=1, source_target_pairs={{0,16},{16,32},{32,48},{48,0},{1,17},{17,33},{33,49},{49,1},{2,18}... | collective-permute-start | bytes 1105928 | tf_op jit(solution)/shard_map/ppermute | solution.py:318
  64.8 0.3 collective-permute-done.2.refs_5_
  65.1 2.4 %collective-permute-start.3 = (bf16[144,1280]{1,0:T(8,128)(2,1)S(1)}, bf16[144,1280]{1,0:T(8,128)(2,1)S(1)}, u32[]{:S(2)}, u32[]{:S(2)}) collective-permute-start(bf16[144,1280]{1,0:T(8,128)(2,1)S(1)} %collective-permute-done.2.refs_5_), channel_id=1, source_target_pairs={{0,48},{16,0},{32,16},{48,32},{1,49},{17,1},{33,17},{49,33},{2,50}... | collective-permute-start | bytes 1105928 | tf_op jit(solution)/shard_map/ppermute | solution.py:321
  67.5 0.0 collective-permute-done.6.refs_7_
  67.5 1.7 %collective-permute-done.4.refs_3_ = bf16[144,1280]{1,0:T(8,128)(2,1)S(1)} collective-permute-done((bf16[144,1280]{1,0:T(8,128)(2,1)S(1)}, bf16[144,1280]{1,0:T(8,128)(2,1)S(1)}, u32[]{:S(2)}, u32[]{:S(2)}) %collective-permute-start.4) | collective-permute-done | bytes 368672 | tf_op jit(solution)/shard_map/ppermute | solution.py:318
  69.3 3.7 %collective-permute-done.5.refs_4_ = bf16[144,1280]{1,0:T(8,128)(2,1)S(1)} collective-permute-done((bf16[144,1280]{1,0:T(8,128)(2,1)S(1)}, bf16[144,1280]{1,0:T(8,128)(2,1)S(1)}, u32[]{:S(2)}, u32[]{:S(2)}) %collective-permute-start.5) | collective-permute-done | bytes 368672 | tf_op jit(solution)/shard_map/ppermute | solution.py:321
  73.0 0.0 copy-done.3
  73.0 6.2 %shard_map.66 = (bf16[8,800,128]{2,1,0:T(8,128)(2,1)S(1)}, bf16[384,5120]{1,0:T(8,128)(2,1)S(1)}, bf16[192,5120]{1,0:T(8,128)(2,1)S(1)}) custom-call(bf16[2,192,144]{2,1,0:T(8,128)(2,1)S(1)} %get-tuple-element.22.refs_0_, bf16[288,1280]{1,0:T(8,128)(2,1)S(1)} %bitcast.8, bf16[144,1280]{1,0:T(8,128)(2,1)S(1)} %collective-permute-done.refs_2_, ...), custom_call_target="tpu_custom_call" | custom-call | flops 1179648000 | bytes 8220672 | tf_op jit(solution)/shard_map/pallas_call | solution.py:27
  79.2 0.0 collective-permute-done.1.refs_1_
  79.2 0.0 collective-permute-done.3.refs_2_
  79.2 4.7 %shard_map.67 = bf16[8,800,128]{2,1,0:T(8,128)(2,1)S(1)} custom-call(bf16[2,192,144]{2,1,0:T(8,128)(2,1)S(1)} %get-tuple-element.22.refs_0_, bf16[144,1280]{1,0:T(8,128)(2,1)S(1)} %collective-permute-done.1.refs_1_, bf16[144,1280]{1,0:T(8,128)(2,1)S(1)} %collective-permute-done.3.refs_2_, ...), custom_call_target="tpu_custom_call", output_to_operand_aliasing={{}: (5, {})} | custom-call | flops 393216000 | bytes 8384512 | tf_op jit(solution)/shard_map/pallas_call | solution.py:27
  84.0 25.4 %all_to_all.15.refs_1_ = bf16[8,800,128]{2,1,0:T(8,128)(2,1)S(1)} all-to-all(bf16[8,800,128]{2,1,0:T(8,128)(2,1)S(1)} %shard_map.67), channel_id=1, replica_groups=mesh['group'=12,'member'=4,'y'=8,'core'=2] {'member','core'}, dimensions={0} | all-to-all | bytes 3276800 | tf_op jit(solution)/shard_map/all_to_all | solution.py:315
  109.4 0.0 copy-start.2
  109.4 0.6 shard_map.68
  110.0 35.6 %all_to_all.16 = bf16[96,16,128]{2,1,0:T(8,128)(2,1)S(1)} all-to-all(bf16[96,16,128]{2,1,0:T(8,128)(2,1)S(1)} %shard_map.68), channel_id=1, replica_groups=mesh['group'=12,'member'=4,'y'=8,'core'=2] {'group','y'}, dimensions={0} | all-to-all | bytes 786432 | tf_op jit(solution)/shard_map/all_to_all | solution.py:315
  145.7 0.0 copy-done.2
  145.7 1.3 shard_map.69
  (1 shorter events, 0.0 us)
Async XLA Ops:
  0.0 18.7 %copy-start = (bf16[1,2,96,5120]{3,2,1,0:T(8,128)(2,1)S(1)}, bf16[1,2,96,5120]{3,2,1,0:T(8,128)(2,1)}, u32[]{:S(2)}) copy-start(bf16[1,2,96,5120]{3,2,1,0:T(8,128)(2,1)} %param.10) | copy-start | bytes 5898244
  0.0 23.1 %copy-start.4 = (s32[96,6]{0,1:T(8,128)S(1)}, s32[96,6]{0,1:T(8,128)}, u32[]{:S(2)}) copy-start(s32[96,6]{0,1:T(8,128)} %param.9) | copy-start | bytes 6916
  3.6 45.1 %all-to-all-start = ((bf16[12,24,1280]{2,1,0:T(8,128)(2,1)}), bf16[12,24,1280]{2,1,0:T(8,128)(2,1)S(1)}, u32[]{:S(2)}, u32[]{:S(2)}) async-start(bf16[12,24,1280]{2,1,0:T(8,128)(2,1)} %bitcast.16), calls=%async_computation | async-start | bytes 1474560 | tf_op jit(solution)/shard_map/all_to_all | solution.py:315
  18.7 48.8 %collective-permute-start.6 = (bf16[192,5120]{1,0:T(8,128)(2,1)S(1)}, bf16[192,5120]{1,0:T(8,128)(2,1)}, u32[]{:S(2)}, u32[]{:S(2)}) collective-permute-start(bf16[192,5120]{1,0:T(8,128)(2,1)S(1)} %bitcast.9), channel_id=1, source_target_pairs={{0,1},{1,0},{2,3},{3,2},{4,5},{5,4},{6,7},{7,6},{8,9},{9,8},{10,11... | collective-permute-start | bytes 5898248 | tf_op jit(solution)/shard_map/ppermute | solution.py:324
  20.7 37.4 %collective-permute-start.7 = (bf16[96,5120]{1,0:T(8,128)(2,1)}, bf16[96,5120]{1,0:T(8,128)(2,1)}, u32[]{:S(2)}, u32[]{:S(2)}) collective-permute-start(bf16[96,5120]{1,0:T(8,128)(2,1)} %bitcast.12), channel_id=1, source_target_pairs={{0,1},{1,0},{2,3},{3,2},{4,5},{5,4},{6,7},{7,6},{8,9},{9,8},{10,11... | collective-permute-start | bytes 2949128 | tf_op jit(solution)/shard_map/ppermute | solution.py:324
  25.0 1.2 copy-start.1
  48.6 24.3 %copy-start.3 = (bf16[1,96,5120]{2,1,0:T(8,128)(2,1)S(1)}, bf16[1,96,5120]{2,1,0:T(8,128)(2,1)}, u32[]{:S(2)}) copy-start(bf16[1,96,5120]{2,1,0:T(8,128)(2,1)} %param.11) | copy-start | bytes 2949124
  48.7 12.7 %collective-permute-start = (bf16[144,1280]{1,0:T(8,128)(2,1)S(1)}, bf16[144,1280]{1,0:T(8,128)(2,1)S(1)}, u32[]{:S(2)}, u32[]{:S(2)}) collective-permute-start(bf16[144,1280]{1,0:T(8,128)(2,1)S(1)} %get-tuple-element.30), channel_id=1, source_target_pairs={{0,16},{16,32},{32,48},{48,0},{1,17},{17,33},{33,49},{49,1},{2,18}... | collective-permute-start | bytes 1105928 | tf_op jit(solution)/shard_map/ppermute | solution.py:318
  52.2 12.8 %collective-permute-start.2 = (bf16[144,1280]{1,0:T(8,128)(2,1)S(1)}, bf16[144,1280]{1,0:T(8,128)(2,1)S(1)}, u32[]{:S(2)}, u32[]{:S(2)}) collective-permute-start(bf16[144,1280]{1,0:T(8,128)(2,1)S(1)} %get-tuple-element.29), channel_id=1, source_target_pairs={{0,48},{16,0},{32,16},{48,32},{1,49},{17,1},{33,17},{49,33},{2,50}... | collective-permute-start | bytes 1105928 | tf_op jit(solution)/shard_map/ppermute | solution.py:321
  54.7 14.6 %collective-permute-start.4 = (bf16[144,1280]{1,0:T(8,128)(2,1)S(1)}, bf16[144,1280]{1,0:T(8,128)(2,1)S(1)}, u32[]{:S(2)}, u32[]{:S(2)}) collective-permute-start(bf16[144,1280]{1,0:T(8,128)(2,1)S(1)} %get-tuple-element.29), channel_id=1, source_target_pairs={{0,16},{16,32},{32,48},{48,0},{1,17},{17,33},{33,49},{49,1},{2,18}... | collective-permute-start | bytes 1105928 | tf_op jit(solution)/shard_map/ppermute | solution.py:318
  58.1 14.9 %collective-permute-start.5 = (bf16[144,1280]{1,0:T(8,128)(2,1)S(1)}, bf16[144,1280]{1,0:T(8,128)(2,1)S(1)}, u32[]{:S(2)}, u32[]{:S(2)}) collective-permute-start(bf16[144,1280]{1,0:T(8,128)(2,1)S(1)} %get-tuple-element.30), channel_id=1, source_target_pairs={{0,48},{16,0},{32,16},{48,32},{1,49},{17,1},{33,17},{49,33},{2,50}... | collective-permute-start | bytes 1105928 | tf_op jit(solution)/shard_map/ppermute | solution.py:321
  61.4 17.9 %collective-permute-start.1 = (bf16[144,1280]{1,0:T(8,128)(2,1)S(1)}, bf16[144,1280]{1,0:T(8,128)(2,1)S(1)}, u32[]{:S(2)}, u32[]{:S(2)}) collective-permute-start(bf16[144,1280]{1,0:T(8,128)(2,1)S(1)} %collective-permute-done.refs_2_), channel_id=1, source_target_pairs={{0,16},{16,32},{32,48},{48,0},{1,17},{17,33},{33,49},{49,1},{2,18}... | collective-permute-start | bytes 1105928 | tf_op jit(solution)/shard_map/ppermute | solution.py:318
  65.1 14.1 %collective-permute-start.3 = (bf16[144,1280]{1,0:T(8,128)(2,1)S(1)}, bf16[144,1280]{1,0:T(8,128)(2,1)S(1)}, u32[]{:S(2)}, u32[]{:S(2)}) collective-permute-start(bf16[144,1280]{1,0:T(8,128)(2,1)S(1)} %collective-permute-done.2.refs_5_), channel_id=1, source_target_pairs={{0,48},{16,0},{32,16},{48,32},{1,49},{17,1},{33,17},{49,33},{2,50}... | collective-permute-start | bytes 1105928 | tf_op jit(solution)/shard_map/ppermute | solution.py:321
  109.4 36.3 %copy-start.2 = (bf16[576,1536]{1,0:T(8,128)(2,1)S(1)}, bf16[576,1536]{1,0:T(8,128)(2,1)}, u32[]{:S(2)}) copy-start(bf16[576,1536]{1,0:T(8,128)(2,1)} %copy-done.1) | copy-start | bytes 5308420

commit v5 on v4

--- a/solution.py
+++ b/solution.py
@@ -208,7 +208,27 @@
     return lax.rem(lax.axis_index("member") + shift, members)
 
 
-def backward_near(members, tall, order, near, *refs):
+def paired(rows, store):
+    held = {}
+
+    def write(home, core, t, tile):
+        if t % 2 == 0:
+            held[id(home), core] = tile
+            return
+        first = held.pop((id(home), core))
+        extra = 2 * (tile.shape[0] - rows)
+        last = pltpu.roll(tile, tile.shape[0] - rows, 0)
+        stop = tile.shape[0] - extra
+        parts = (first[:stop], first[stop:] + last[:extra], last[extra:])
+        begin = t // 2 * 2 * rows
+        for part in parts:
+            store(home, core, begin, part.astype(BF16))
+            begin += part.shape[0]
+
+    return write
+
+
+def backward_near(members, tall, rows, order, near, *refs):
     parts, weights, (out, pairs, downs, ins, grads, done) = refs[:4], refs[4:8], refs[8:]
     deep, flat = pairs.shape[0] // CORES, downs.shape[0] // CORES
     targets = (pairs.at[:deep], pairs.at[deep:], downs.at[:flat], downs.at[flat:])
@@ -221,35 +241,38 @@
     middle = order.shape[2]
     halves = [near[:middle, :], near[middle:, :]] + [p[...] for p in parts]
 
-    def write(home, core, t, rows):
-        out[home * CORES + core, t * tall : (t + 1) * tall, :] = rows.astype(BF16)
-
-    homes = [home_of(shift, members) for shift in (0, members - 1, 1)]
-    backward(homes, tall, order, halves, copies, pairs, downs, write, ins, grads)
-
-
-def backward_opposite(members, tall, order, top, bottom, pairs, downs, *refs):
+    def store(home, core, begin, part):
+        out[home * CORES + core, begin : begin + part.shape[0], :] = part
+
+    turn = (members - 2) * lax.axis_index("core")
+    homes = [home_of(shift, members) for shift in (0, members - 1 - turn, 1 + turn)]
+    backward(homes, tall, order, halves, copies, pairs, downs, paired(rows, store), ins, grads)
+
+
+def backward_opposite(members, tall, rows, order, top, bottom, pairs, downs, *refs):
     out, ins, grads, held, sent = refs[1:]
     home = home_of(members // 2, members)
+    chunk = held.shape[1] // sent.shape[1]
     copies = []
 
-    def write(_, core, t, rows):
-        held[core, t * tall : (t + 1) * tall, :] = rows.astype(BF16)
-        if t % 5 == 4:
-            at = pl.ds((t - 4) * tall, 5 * tall)
+    def store(_, core, begin, part):
+        end = begin + part.shape[0]
+        held[core, begin:end, :] = part
+        if end % chunk == 0:
+            at = pl.ds(end - chunk, chunk)
             copy = pltpu.make_async_copy(
-                held.at[core, at], out.at[home * CORES + core, at], sent.at[core, t // 5]
+                held.at[core, at], out.at[home * CORES + core, at], sent.at[core, end // chunk - 1]
             )
             copy.start()
             copies.append(copy)
 
     halves = [top[...], bottom[...]]
-    backward([home], tall, order, halves, [], pairs, downs, write, ins, grads)
+    backward([home], tall, order, halves, [], pairs, downs, paired(rows, store), ins, grads)
     for copy in copies:
         copy.wait()
 
 
-def total_pieces(groups, columns, tall, place, x, out):
+def total_pieces(groups, columns, tall, rows, place, x, out):
     low = iota((tall, LANES), 1) < LANES // 2
     members = x.shape[0] // CORES
     for y in range(columns):
@@ -257,10 +280,13 @@
         for c in range(CORES):
             tiles, turned = [], []
             for t in range(3):
-                at = (5 * y // 2 + t) * tall
+                number = 5 * y // 2 + t
+                at = number // 2 * 2 * rows + number % 2 * (2 * rows - tall)
                 tile = x[c, at : at + tall, :].astype(F32)
                 for m in range(1, members):
                     tile += x[m * CORES + c, at : at + tall, :].astype(F32)
+                if number % 2 == 1:
+                    tile = pltpu.roll(tile, rows, 0)
                 tiles.append(tile)
                 turned.append(pltpu.roll(tile, LANES // 2, 1))
             first = [
@@ -314,11 +340,19 @@
     def exchange(x, axis):
         return lax.all_to_all(x, axis, split_axis=0, concat_axis=0, tiled=True)
 
+    def shift(x, step):
+        hops = [
+            (CORES * i + c, CORES * ((i + step * (1 - 2 * c)) % members) + c)
+            for i in range(members)
+            for c in range(CORES)
+        ]
+        return lax.ppermute(x, ("member", "core"), hops)
+
     def up(x):
-        return lax.ppermute(x, "member", [(i, (i + 1) % members) for i in range(members)])
+        return shift(x, 1)
 
     def down(x):
-        return lax.ppermute(x, "member", [(i, (i - 1) % members) for i in range(members)])
+        return shift(x, -1)
 
     def far(x):
         return lax.ppermute(x, "core", [(0, 1), (1, 0)])
@@ -364,13 +398,13 @@
     opposite = (up(below_top), down(above_bottom))
 
     lane_tiles = width // (CORES * LANES)
-    result = struct((members * CORES, lane_tiles * tall, LANES), BF16)
+    result = struct((members * CORES, lane_tiles * block_rows, LANES), BF16)
 
     def rows(blocks):
         return pltpu.VMEM((PARTS // 2, blocks * tall, 2 * part), BF16)
 
     partial, pairs_all, downs_all = call(
-        bind(backward_near, members, tall),
+        bind(backward_near, members, tall, block_rows),
         (
             result,
             struct((CORES * 2 * hidden, width), BF16),
@@ -382,7 +416,7 @@
         scratch=(rows(3), rows(3), pltpu.SemaphoreType.DMA((4,))),
     )
     partial = call(
-        bind(backward_opposite, members, tall),
+        bind(backward_opposite, members, tall, block_rows),
         result,
         order, *opposite, pairs_all, downs_all, partial,
         far={5: pl.ANY}, far_out=True, alias=5,
@@ -391,11 +425,11 @@
             rows(1),
             rows(1),
             pltpu.VMEM((CORES,) + result.shape[1:], BF16),
-            pltpu.SemaphoreType.DMA((CORES, lane_tiles // 5)),
+            pltpu.SemaphoreType.DMA((CORES, lane_tiles // 10)),
         ),
     )
     pieces = call(
-        bind(total_pieces, groups, columns, tall),
+        bind(total_pieces, groups, columns, tall, block_rows),
         struct((groups * columns, PIECE, LANES), BF16),
         place, exchange(partial, ("member", "core")),
     )

time: 148 us -> 144 us (0.973)
  waiting for transfers between devices: 29 us -> 26.9 us
    ppermute x6, waiting for transfers between devices: 6.58 us -> 4.51 us  [shift(): return lax.ppermute(x, ('member', 'core'), hops)]
  transfers between devices with their start and end apart: 9 -> 9, of which waited for: 5 -> 4; matrix products, arithmetic and copies ran while one was open for 0% -> 0% of each run, Pallas kernels for 6% -> 6%
where the time goes in v5:
time: 144 us; the launch traced here: 143 us
  blocking collectives  60.1 us (42%)
  starting transfers between devices  37.1 us (26%)
  waiting for transfers between devices  26.9 us (19%)
  Pallas kernels  17.8 us (12%)
    all_to_all x2, blocking collectives, exchange(): return lax.all_to_all(x, axis, split_axis=0, concat_axis=0, tiled=True)  60.1 us
    all_to_all x1, waiting for transfers between devices, exchange(): return lax.all_to_all(x, axis, split_axis=0, concat_axis=0, tiled=True)  22.4 us
    pallas_call x6, Pallas kernels, call(): pl.pallas_call(body, out_shape=out_shape, in_specs=[pl.BlockSpec(memory_s...  17.8 us
    ppermute x6, starting transfers between devices, shift(): return lax.ppermute(x, ('member', 'core'), hops)  17.6 us
    all_to_all x1, starting transfers between devices, exchange(): return lax.all_to_all(x, axis, split_axis=0, concat_axis=0, tiled=True)  15.2 us
    ppermute x6, waiting for transfers between devices, shift(): return lax.ppermute(x, ('member', 'core'), hops)  4.51 us
    ppermute x2, starting transfers between devices, far(): return lax.ppermute(x, 'core', [(0, 1), (1, 0)])  4.33 us
  transfers between devices with their start and end apart: 9, of which 4 were waited for; matrix products, arithmetic and copies ran while one was open for 0% of the time, Pallas kernels for 6%

profile of v5, /device:TPU:2, one launch (start us, length us, event | category | flops | bytes accessed | tf_op | source)
XLA Modules:
  0.0 143.5 jit_solution(16499365238711773259)
XLA Ops:
  0.0 0.0 copy-start
  0.0 0.0 copy-start.4
  0.0 3.6 %shard_map.64 = bf16[288,1280]{1,0:T(8,128)(2,1)} custom-call(s32[6,96]{1,0:T(8,128)} %bitcast.14, bf16[6,96]{1,0:T(8,128)(2,1)} %bitcast.17, bf16[96,5120]{1,0:T(8,128)(2,1)} %refs_2_.1, bf16[96,5120]{1,0:T(8,128)(2,1)} %refs_3_.1), custom_call_target="tpu_custom_call" | custom-call | bytes 1969536 | tf_op jit(solution)/shard_map/pallas_call | solution.py:27
  3.6 15.2 %all-to-all-start = ((bf16[12,24,1280]{2,1,0:T(8,128)(2,1)}), bf16[12,24,1280]{2,1,0:T(8,128)(2,1)S(1)}, u32[]{:S(2)}, u32[]{:S(2)}) async-start(bf16[12,24,1280]{2,1,0:T(8,128)(2,1)} %bitcast.16), calls=%async_computation | async-start | bytes 1474560 | tf_op jit(solution)/shard_map/all_to_all | solution.py:341
  18.7 0.0 copy-done
  18.7 1.9 %collective-permute-start.6 = (bf16[192,5120]{1,0:T(8,128)(2,1)S(1)}, bf16[192,5120]{1,0:T(8,128)(2,1)}, u32[]{:S(2)}, u32[]{:S(2)}) collective-permute-start(bf16[192,5120]{1,0:T(8,128)(2,1)S(1)} %bitcast.9), channel_id=1, source_target_pairs={{0,1},{1,0},{2,3},{3,2},{4,5},{5,4},{6,7},{7,6},{8,9},{9,8},{10,11... | collective-permute-start | bytes 5898248 | tf_op jit(solution)/shard_map/ppermute | solution.py:358
  20.7 2.4 %collective-permute-start.7 = (bf16[96,5120]{1,0:T(8,128)(2,1)}, bf16[96,5120]{1,0:T(8,128)(2,1)}, u32[]{:S(2)}, u32[]{:S(2)}) collective-permute-start(bf16[96,5120]{1,0:T(8,128)(2,1)} %bitcast.12), channel_id=1, source_target_pairs={{0,1},{1,0},{2,3},{3,2},{4,5},{5,4},{6,7},{7,6},{8,9},{9,8},{10,11... | collective-permute-start | bytes 2949128 | tf_op jit(solution)/shard_map/ppermute | solution.py:358
  23.1 0.0 copy-done.4
  23.1 1.9 %shard_map.65 = (bf16[576,1536]{1,0:T(8,128)(2,1)S(1)}, bf16[192,480]{1,0:T(8,128)(2,1)S(1)}, bf16[2,192,144]{2,1,0:T(8,128)(2,1)S(1)}) custom-call(s32[6,96]{1,0:T(8,128)S(1)} %bitcast.15), custom_call_target="tpu_custom_call" | custom-call | bytes 2304 | tf_op jit(solution)/shard_map/pallas_call | solution.py:27
  25.0 0.0 copy-start.1
  25.0 1.2 copy-done.1
  26.2 22.4 %all-to-all-done = bf16[12,24,1280]{2,1,0:T(8,128)(2,1)S(1)} async-done(((bf16[12,24,1280]{2,1,0:T(8,128)(2,1)}), bf16[12,24,1280]{2,1,0:T(8,128)(2,1)S(1)}, u32[]{:S(2)}, u32[]{:S(2)}) %all-to-all-start) | async-done | bytes 737312 | tf_op jit(solution)/shard_map/all_to_all | solution.py:341
  48.6 0.0 copy-start.3
  48.7 3.5 %collective-permute-start = (bf16[144,1280]{1,0:T(8,128)(2,1)S(1)}, bf16[144,1280]{1,0:T(8,128)(2,1)S(1)}, u32[]{:S(2)}, u32[]{:S(2)}) collective-permute-start(bf16[144,1280]{1,0:T(8,128)(2,1)S(1)} %get-tuple-element.30), channel_id=1, source_target_pairs={{0,16},{1,49},{16,32},{17,1},{32,48},{33,17},{48,0},{49,33},{2,18}... | collective-permute-start | bytes 1105928 | tf_op jit(solution)/shard_map/ppermute | solution.py:349
  52.2 2.4 %collective-permute-start.2 = (bf16[144,1280]{1,0:T(8,128)(2,1)S(1)}, bf16[144,1280]{1,0:T(8,128)(2,1)S(1)}, u32[]{:S(2)}, u32[]{:S(2)}) collective-permute-start(bf16[144,1280]{1,0:T(8,128)(2,1)S(1)} %get-tuple-element.29), channel_id=1, source_target_pairs={{0,48},{1,17},{16,0},{17,33},{32,16},{33,49},{48,32},{49,1},{2,50}... | collective-permute-start | bytes 1105928 | tf_op jit(solution)/shard_map/ppermute | solution.py:349
  54.7 3.4 %collective-permute-start.4 = (bf16[144,1280]{1,0:T(8,128)(2,1)S(1)}, bf16[144,1280]{1,0:T(8,128)(2,1)S(1)}, u32[]{:S(2)}, u32[]{:S(2)}) collective-permute-start(bf16[144,1280]{1,0:T(8,128)(2,1)S(1)} %get-tuple-element.29), channel_id=1, source_target_pairs={{0,16},{1,49},{16,32},{17,1},{32,48},{33,17},{48,0},{49,33},{2,18}... | collective-permute-start | bytes 1105928 | tf_op jit(solution)/shard_map/ppermute | solution.py:349
  58.1 0.0 collective-permute-done.7.refs_9_
  58.1 2.4 %collective-permute-start.5 = (bf16[144,1280]{1,0:T(8,128)(2,1)S(1)}, bf16[144,1280]{1,0:T(8,128)(2,1)S(1)}, u32[]{:S(2)}, u32[]{:S(2)}) collective-permute-start(bf16[144,1280]{1,0:T(8,128)(2,1)S(1)} %get-tuple-element.30), channel_id=1, source_target_pairs={{0,48},{1,17},{16,0},{17,33},{32,16},{33,49},{48,32},{49,1},{2,50}... | collective-permute-start | bytes 1105928 | tf_op jit(solution)/shard_map/ppermute | solution.py:349
  60.6 1.7 %collective-permute-done.refs_2_ = bf16[144,1280]{1,0:T(8,128)(2,1)S(1)} collective-permute-done((bf16[144,1280]{1,0:T(8,128)(2,1)S(1)}, bf16[144,1280]{1,0:T(8,128)(2,1)S(1)}, u32[]{:S(2)}, u32[]{:S(2)}) %collective-permute-start) | collective-permute-done | bytes 368672 | tf_op jit(solution)/shard_map/ppermute | solution.py:349
  62.2 3.4 %collective-permute-start.1 = (bf16[144,1280]{1,0:T(8,128)(2,1)S(1)}, bf16[144,1280]{1,0:T(8,128)(2,1)S(1)}, u32[]{:S(2)}, u32[]{:S(2)}) collective-permute-start(bf16[144,1280]{1,0:T(8,128)(2,1)S(1)} %collective-permute-done.refs_2_), channel_id=1, source_target_pairs={{0,16},{1,49},{16,32},{17,1},{32,48},{33,17},{48,0},{49,33},{2,18}... | collective-permute-start | bytes 1105928 | tf_op jit(solution)/shard_map/ppermute | solution.py:349
  65.6 0.0 collective-permute-done.2.refs_5_
  65.7 2.4 %collective-permute-start.3 = (bf16[144,1280]{1,0:T(8,128)(2,1)S(1)}, bf16[144,1280]{1,0:T(8,128)(2,1)S(1)}, u32[]{:S(2)}, u32[]{:S(2)}) collective-permute-start(bf16[144,1280]{1,0:T(8,128)(2,1)S(1)} %collective-permute-done.2.refs_5_), channel_id=1, source_target_pairs={{0,48},{1,17},{16,0},{17,33},{32,16},{33,49},{48,32},{49,1},{2,50}... | collective-permute-start | bytes 1105928 | tf_op jit(solution)/shard_map/ppermute | solution.py:349
  68.1 0.0 collective-permute-done.6.refs_7_
  68.1 2.0 %collective-permute-done.4.refs_3_ = bf16[144,1280]{1,0:T(8,128)(2,1)S(1)} collective-permute-done((bf16[144,1280]{1,0:T(8,128)(2,1)S(1)}, bf16[144,1280]{1,0:T(8,128)(2,1)S(1)}, u32[]{:S(2)}, u32[]{:S(2)}) %collective-permute-start.4) | collective-permute-done | bytes 368672 | tf_op jit(solution)/shard_map/ppermute | solution.py:349
  70.1 0.8 collective-permute-done.5.refs_4_
  70.9 0.0 copy-done.3
  70.9 6.0 %shard_map.66 = (bf16[8,720,128]{2,1,0:T(8,128)(2,1)S(1)}, bf16[384,5120]{1,0:T(8,128)(2,1)S(1)}, bf16[192,5120]{1,0:T(8,128)(2,1)S(1)}) custom-call(bf16[2,192,144]{2,1,0:T(8,128)(2,1)S(1)} %get-tuple-element.22.refs_0_, bf16[288,1280]{1,0:T(8,128)(2,1)S(1)} %bitcast.8, bf16[144,1280]{1,0:T(8,128)(2,1)S(1)} %collective-permute-done.refs_2_, ...), custom_call_target="tpu_custom_call" | custom-call | flops 1179648000 | bytes 8220672 | tf_op jit(solution)/shard_map/pallas_call | solution.py:27
  76.9 0.0 collective-permute-done.1.refs_1_
  76.9 0.0 collective-permute-done.3.refs_2_
  76.9 4.4 %shard_map.67 = bf16[8,720,128]{2,1,0:T(8,128)(2,1)S(1)} custom-call(bf16[2,192,144]{2,1,0:T(8,128)(2,1)S(1)} %get-tuple-element.22.refs_0_, bf16[144,1280]{1,0:T(8,128)(2,1)S(1)} %collective-permute-done.1.refs_1_, bf16[144,1280]{1,0:T(8,128)(2,1)S(1)} %collective-permute-done.3.refs_2_, ...), custom_call_target="tpu_custom_call", output_to_operand_aliasing={{}: (5, {})} | custom-call | flops 393216000 | bytes 8220672 | tf_op jit(solution)/shard_map/pallas_call | solution.py:27
  81.3 26.0 %all_to_all.15.refs_1_ = bf16[8,720,128]{2,1,0:T(8,128)(2,1)S(1)} all-to-all(bf16[8,720,128]{2,1,0:T(8,128)(2,1)S(1)} %shard_map.67), channel_id=1, replica_groups=mesh['group'=12,'member'=4,'y'=8,'core'=2] {'member','core'}, dimensions={0} | all-to-all | bytes 2949120 | tf_op jit(solution)/shard_map/all_to_all | solution.py:341
  107.4 0.0 copy-start.2
  107.4 0.6 shard_map.68
  108.0 34.1 %all_to_all.16 = bf16[96,16,128]{2,1,0:T(8,128)(2,1)S(1)} all-to-all(bf16[96,16,128]{2,1,0:T(8,128)(2,1)S(1)} %shard_map.68), channel_id=1, replica_groups=mesh['group'=12,'member'=4,'y'=8,'core'=2] {'group','y'}, dimensions={0} | all-to-all | bytes 786432 | tf_op jit(solution)/shard_map/all_to_all | solution.py:341
  142.1 0.0 copy-done.2
  142.1 1.3 shard_map.69
  (1 shorter events, 0.0 us)
Async XLA Ops:
  0.0 18.7 %copy-start = (bf16[1,2,96,5120]{3,2,1,0:T(8,128)(2,1)S(1)}, bf16[1,2,96,5120]{3,2,1,0:T(8,128)(2,1)}, u32[]{:S(2)}) copy-start(bf16[1,2,96,5120]{3,2,1,0:T(8,128)(2,1)} %param.10) | copy-start | bytes 5898244
  0.0 23.1 %copy-start.4 = (s32[96,6]{0,1:T(8,128)S(1)}, s32[96,6]{0,1:T(8,128)}, u32[]{:S(2)}) copy-start(s32[96,6]{0,1:T(8,128)} %param.9) | copy-start | bytes 6916
  3.6 45.1 %all-to-all-start = ((bf16[12,24,1280]{2,1,0:T(8,128)(2,1)}), bf16[12,24,1280]{2,1,0:T(8,128)(2,1)S(1)}, u32[]{:S(2)}, u32[]{:S(2)}) async-start(bf16[12,24,1280]{2,1,0:T(8,128)(2,1)} %bitcast.16), calls=%async_computation | async-start | bytes 1474560 | tf_op jit(solution)/shard_map/all_to_all | solution.py:341
  18.7 49.3 %collective-permute-start.6 = (bf16[192,5120]{1,0:T(8,128)(2,1)S(1)}, bf16[192,5120]{1,0:T(8,128)(2,1)}, u32[]{:S(2)}, u32[]{:S(2)}) collective-permute-start(bf16[192,5120]{1,0:T(8,128)(2,1)S(1)} %bitcast.9), channel_id=1, source_target_pairs={{0,1},{1,0},{2,3},{3,2},{4,5},{5,4},{6,7},{7,6},{8,9},{9,8},{10,11... | collective-permute-start | bytes 5898248 | tf_op jit(solution)/shard_map/ppermute | solution.py:358
  20.7 37.4 %collective-permute-start.7 = (bf16[96,5120]{1,0:T(8,128)(2,1)}, bf16[96,5120]{1,0:T(8,128)(2,1)}, u32[]{:S(2)}, u32[]{:S(2)}) collective-permute-start(bf16[96,5120]{1,0:T(8,128)(2,1)} %bitcast.12), channel_id=1, source_target_pairs={{0,1},{1,0},{2,3},{3,2},{4,5},{5,4},{6,7},{7,6},{8,9},{9,8},{10,11... | collective-permute-start | bytes 2949128 | tf_op jit(solution)/shard_map/ppermute | solution.py:358
  25.0 1.2 copy-start.1
  48.6 22.3 %copy-start.3 = (bf16[1,96,5120]{2,1,0:T(8,128)(2,1)S(1)}, bf16[1,96,5120]{2,1,0:T(8,128)(2,1)}, u32[]{:S(2)}) copy-start(bf16[1,96,5120]{2,1,0:T(8,128)(2,1)} %param.11) | copy-start | bytes 2949124
  48.7 13.5 %collective-permute-start = (bf16[144,1280]{1,0:T(8,128)(2,1)S(1)}, bf16[144,1280]{1,0:T(8,128)(2,1)S(1)}, u32[]{:S(2)}, u32[]{:S(2)}) collective-permute-start(bf16[144,1280]{1,0:T(8,128)(2,1)S(1)} %get-tuple-element.30), channel_id=1, source_target_pairs={{0,16},{1,49},{16,32},{17,1},{32,48},{33,17},{48,0},{49,33},{2,18}... | collective-permute-start | bytes 1105928 | tf_op jit(solution)/shard_map/ppermute | solution.py:349
  52.2 13.4 %collective-permute-start.2 = (bf16[144,1280]{1,0:T(8,128)(2,1)S(1)}, bf16[144,1280]{1,0:T(8,128)(2,1)S(1)}, u32[]{:S(2)}, u32[]{:S(2)}) collective-permute-start(bf16[144,1280]{1,0:T(8,128)(2,1)S(1)} %get-tuple-element.29), channel_id=1, source_target_pairs={{0,48},{1,17},{16,0},{17,33},{32,16},{33,49},{48,32},{49,1},{2,50}... | collective-permute-start | bytes 1105928 | tf_op jit(solution)/shard_map/ppermute | solution.py:349
  54.7 15.4 %collective-permute-start.4 = (bf16[144,1280]{1,0:T(8,128)(2,1)S(1)}, bf16[144,1280]{1,0:T(8,128)(2,1)S(1)}, u32[]{:S(2)}, u32[]{:S(2)}) collective-permute-start(bf16[144,1280]{1,0:T(8,128)(2,1)S(1)} %get-tuple-element.29), channel_id=1, source_target_pairs={{0,16},{1,49},{16,32},{17,1},{32,48},{33,17},{48,0},{49,33},{2,18}... | collective-permute-start | bytes 1105928 | tf_op jit(solution)/shard_map/ppermute | solution.py:349
  58.1 12.8 %collective-permute-start.5 = (bf16[144,1280]{1,0:T(8,128)(2,1)S(1)}, bf16[144,1280]{1,0:T(8,128)(2,1)S(1)}, u32[]{:S(2)}, u32[]{:S(2)}) collective-permute-start(bf16[144,1280]{1,0:T(8,128)(2,1)S(1)} %get-tuple-element.30), channel_id=1, source_target_pairs={{0,48},{1,17},{16,0},{17,33},{32,16},{33,49},{48,32},{49,1},{2,50}... | collective-permute-start | bytes 1105928 | tf_op jit(solution)/shard_map/ppermute | solution.py:349
  62.2 14.7 %collective-permute-start.1 = (bf16[144,1280]{1,0:T(8,128)(2,1)S(1)}, bf16[144,1280]{1,0:T(8,128)(2,1)S(1)}, u32[]{:S(2)}, u32[]{:S(2)}) collective-permute-start(bf16[144,1280]{1,0:T(8,128)(2,1)S(1)} %collective-permute-done.refs_2_), channel_id=1, source_target_pairs={{0,16},{1,49},{16,32},{17,1},{32,48},{33,17},{48,0},{49,33},{2,18}... | collective-permute-start | bytes 1105928 | tf_op jit(solution)/shard_map/ppermute | solution.py:349
  65.7 11.3 %collective-permute-start.3 = (bf16[144,1280]{1,0:T(8,128)(2,1)S(1)}, bf16[144,1280]{1,0:T(8,128)(2,1)S(1)}, u32[]{:S(2)}, u32[]{:S(2)}) collective-permute-start(bf16[144,1280]{1,0:T(8,128)(2,1)S(1)} %collective-permute-done.2.refs_5_), channel_id=1, source_target_pairs={{0,48},{1,17},{16,0},{17,33},{32,16},{33,49},{48,32},{49,1},{2,50}... | collective-permute-start | bytes 1105928 | tf_op jit(solution)/shard_map/ppermute | solution.py:349
  107.4 34.8 %copy-start.2 = (bf16[576,1536]{1,0:T(8,128)(2,1)S(1)}, bf16[576,1536]{1,0:T(8,128)(2,1)}, u32[]{:S(2)}) copy-start(bf16[576,1536]{1,0:T(8,128)(2,1)} %copy-done.1) | copy-start | bytes 5308420

commit v6 on v5

--- a/solution.py
+++ b/solution.py
@@ -116,7 +116,9 @@
     rank = dot(hit.astype(BF16), before(tokens, tokens))
     code = jnp.where(hit, rank, -1.0).astype(BF16)
     lanes = experts * PIECE
-    widen = (iota((experts, lanes), 1) // PIECE == iota((experts, lanes), 0)).astype(BF16)
+    piece = iota((experts, lanes), 1) // PIECE
+    expert = piece % groups * per_group + piece // groups
+    widen = (expert == iota((experts, lanes), 0)).astype(BF16)
     spread = dot_first(code, widen).astype(jnp.int32)
     row = iota((tokens, lanes), 1) % PIECE
     for n, (odd, part) in enumerate(ENTRIES):
@@ -304,7 +306,7 @@
         stack = jnp.concatenate([e for pair in sorted_entries for e in pair], axis=0)
         moved = dot(place[...], stack.astype(BF16)).astype(BF16)
         for g in range(groups):
-            out[g * columns + y] = moved[g * PIECE : (g + 1) * PIECE]
+            out[y * groups + g] = moved[g * PIECE : (g + 1) * PIECE]
 
 
 def finish(gather, x, out):
@@ -433,7 +435,7 @@
         struct((groups * columns, PIECE, LANES), BF16),
         place, exchange(partial, ("member", "core")),
     )
-    arrived = exchange(pieces, ("group", "y")).reshape(-1, LANES)
+    arrived = exchange(pieces, ("y", "group")).reshape(-1, LANES)
     return call(finish, struct((tokens, chunk), BF16), gather, arrived)
 
 

time: 144 us -> 144 us (level)
  the two profiles are of different devices: /device:TPU:2 before, /device:TPU:8 now
where the time goes in v6:
time: 144 us; the launch traced here: 143 us
  blocking collectives  57.6 us (40%)
  starting transfers between devices  40.8 us (28%)
  waiting for transfers between devices  25.4 us (18%)
  Pallas kernels  17.9 us (12%)
    all_to_all x2, blocking collectives, exchange(): return lax.all_to_all(x, axis, split_axis=0, concat_axis=0, tiled=True)  57.6 us
    all_to_all x1, waiting for transfers between devices, exchange(): return lax.all_to_all(x, axis, split_axis=0, concat_axis=0, tiled=True)  22.3 us
    ppermute x6, starting transfers between devices, shift(): return lax.ppermute(x, ('member', 'core'), hops)  21.3 us
    pallas_call x6, Pallas kernels, call(): pl.pallas_call(body, out_shape=out_shape, in_specs=[pl.BlockSpec(memory_s...  17.9 us
    all_to_all x1, starting transfers between devices, exchange(): return lax.all_to_all(x, axis, split_axis=0, concat_axis=0, tiled=True)  15.2 us
    ppermute x2, starting transfers between devices, far(): return lax.ppermute(x, 'core', [(0, 1), (1, 0)])  4.33 us
    ppermute x6, waiting for transfers between devices, shift(): return lax.ppermute(x, ('member', 'core'), hops)  3.08 us
  transfers between devices with their start and end apart: 9, of which 5 were waited for; matrix products, arithmetic and copies ran while one was open for 0% of the time, Pallas kernels for 6%

profile of v6, /device:TPU:8, one launch (start us, length us, event | category | flops | bytes accessed | tf_op | source)
XLA Modules:
  0.0 143.1 jit_solution(2510750073408242502)
XLA Ops:
  0.0 0.0 copy-start
  0.0 0.0 copy-start.4
  0.0 3.6 %shard_map.64 = bf16[288,1280]{1,0:T(8,128)(2,1)} custom-call(s32[6,96]{1,0:T(8,128)} %bitcast.14, bf16[6,96]{1,0:T(8,128)(2,1)} %bitcast.17, bf16[96,5120]{1,0:T(8,128)(2,1)} %refs_2_.1, bf16[96,5120]{1,0:T(8,128)(2,1)} %refs_3_.1), custom_call_target="tpu_custom_call" | custom-call | bytes 1969536 | tf_op jit(solution)/shard_map/pallas_call | solution.py:27
  3.6 15.2 %all-to-all-start = ((bf16[12,24,1280]{2,1,0:T(8,128)(2,1)}), bf16[12,24,1280]{2,1,0:T(8,128)(2,1)S(1)}, u32[]{:S(2)}, u32[]{:S(2)}) async-start(bf16[12,24,1280]{2,1,0:T(8,128)(2,1)} %bitcast.16), calls=%async_computation | async-start | bytes 1474560 | tf_op jit(solution)/shard_map/all_to_all | solution.py:343
  18.7 0.0 copy-done
  18.8 1.9 %collective-permute-start.6 = (bf16[192,5120]{1,0:T(8,128)(2,1)S(1)}, bf16[192,5120]{1,0:T(8,128)(2,1)}, u32[]{:S(2)}, u32[]{:S(2)}) collective-permute-start(bf16[192,5120]{1,0:T(8,128)(2,1)S(1)} %bitcast.9), channel_id=1, source_target_pairs={{0,1},{1,0},{2,3},{3,2},{4,5},{5,4},{6,7},{7,6},{8,9},{9,8},{10,11... | collective-permute-start | bytes 5898248 | tf_op jit(solution)/shard_map/ppermute | solution.py:360
  20.7 2.4 %collective-permute-start.7 = (bf16[96,5120]{1,0:T(8,128)(2,1)}, bf16[96,5120]{1,0:T(8,128)(2,1)}, u32[]{:S(2)}, u32[]{:S(2)}) collective-permute-start(bf16[96,5120]{1,0:T(8,128)(2,1)} %bitcast.12), channel_id=1, source_target_pairs={{0,1},{1,0},{2,3},{3,2},{4,5},{5,4},{6,7},{7,6},{8,9},{9,8},{10,11... | collective-permute-start | bytes 2949128 | tf_op jit(solution)/shard_map/ppermute | solution.py:360
  23.1 0.0 copy-done.4
  23.1 2.0 %shard_map.65 = (bf16[576,1536]{1,0:T(8,128)(2,1)S(1)}, bf16[192,480]{1,0:T(8,128)(2,1)S(1)}, bf16[2,192,144]{2,1,0:T(8,128)(2,1)S(1)}) custom-call(s32[6,96]{1,0:T(8,128)S(1)} %bitcast.15), custom_call_target="tpu_custom_call" | custom-call | bytes 2304 | tf_op jit(solution)/shard_map/pallas_call | solution.py:27
  25.1 0.0 copy-start.1
  25.1 1.2 copy-done.1
  26.3 22.3 %all-to-all-done = bf16[12,24,1280]{2,1,0:T(8,128)(2,1)S(1)} async-done(((bf16[12,24,1280]{2,1,0:T(8,128)(2,1)}), bf16[12,24,1280]{2,1,0:T(8,128)(2,1)S(1)}, u32[]{:S(2)}, u32[]{:S(2)}) %all-to-all-start) | async-done | bytes 737312 | tf_op jit(solution)/shard_map/all_to_all | solution.py:343
  48.7 0.0 copy-start.3
  48.7 3.5 %collective-permute-start = (bf16[144,1280]{1,0:T(8,128)(2,1)S(1)}, bf16[144,1280]{1,0:T(8,128)(2,1)S(1)}, u32[]{:S(2)}, u32[]{:S(2)}) collective-permute-start(bf16[144,1280]{1,0:T(8,128)(2,1)S(1)} %get-tuple-element.30), channel_id=1, source_target_pairs={{0,16},{1,49},{16,32},{17,1},{32,48},{33,17},{48,0},{49,33},{2,18}... | collective-permute-start | bytes 1105928 | tf_op jit(solution)/shard_map/ppermute | solution.py:351
  52.2 3.7 %collective-permute-start.2 = (bf16[144,1280]{1,0:T(8,128)(2,1)S(1)}, bf16[144,1280]{1,0:T(8,128)(2,1)S(1)}, u32[]{:S(2)}, u32[]{:S(2)}) collective-permute-start(bf16[144,1280]{1,0:T(8,128)(2,1)S(1)} %get-tuple-element.29), channel_id=1, source_target_pairs={{0,48},{1,17},{16,0},{17,33},{32,16},{33,49},{48,32},{49,1},{2,50}... | collective-permute-start | bytes 1105928 | tf_op jit(solution)/shard_map/ppermute | solution.py:351
  55.9 2.2 %collective-permute-start.4 = (bf16[144,1280]{1,0:T(8,128)(2,1)S(1)}, bf16[144,1280]{1,0:T(8,128)(2,1)S(1)}, u32[]{:S(2)}, u32[]{:S(2)}) collective-permute-start(bf16[144,1280]{1,0:T(8,128)(2,1)S(1)} %get-tuple-element.29), channel_id=1, source_target_pairs={{0,16},{1,49},{16,32},{17,1},{32,48},{33,17},{48,0},{49,33},{2,18}... | collective-permute-start | bytes 1105928 | tf_op jit(solution)/shard_map/ppermute | solution.py:351
  58.1 0.0 collective-permute-done.7.refs_9_
  58.1 4.9 %collective-permute-start.5 = (bf16[144,1280]{1,0:T(8,128)(2,1)S(1)}, bf16[144,1280]{1,0:T(8,128)(2,1)S(1)}, u32[]{:S(2)}, u32[]{:S(2)}) collective-permute-start(bf16[144,1280]{1,0:T(8,128)(2,1)S(1)} %get-tuple-element.30), channel_id=1, source_target_pairs={{0,48},{1,17},{16,0},{17,33},{32,16},{33,49},{48,32},{49,1},{2,50}... | collective-permute-start | bytes 1105928 | tf_op jit(solution)/shard_map/ppermute | solution.py:351
  63.0 0.4 collective-permute-done.refs_2_
  63.4 2.2 %collective-permute-start.1 = (bf16[144,1280]{1,0:T(8,128)(2,1)S(1)}, bf16[144,1280]{1,0:T(8,128)(2,1)S(1)}, u32[]{:S(2)}, u32[]{:S(2)}) collective-permute-start(bf16[144,1280]{1,0:T(8,128)(2,1)S(1)} %collective-permute-done.refs_2_), channel_id=1, source_target_pairs={{0,16},{1,49},{16,32},{17,1},{32,48},{33,17},{48,0},{49,33},{2,18}... | collective-permute-start | bytes 1105928 | tf_op jit(solution)/shard_map/ppermute | solution.py:351
  65.6 0.0 collective-permute-done.2.refs_5_
  65.6 4.8 %collective-permute-start.3 = (bf16[144,1280]{1,0:T(8,128)(2,1)S(1)}, bf16[144,1280]{1,0:T(8,128)(2,1)S(1)}, u32[]{:S(2)}, u32[]{:S(2)}) collective-permute-start(bf16[144,1280]{1,0:T(8,128)(2,1)S(1)} %collective-permute-done.2.refs_5_), channel_id=1, source_target_pairs={{0,48},{1,17},{16,0},{17,33},{32,16},{33,49},{48,32},{49,1},{2,50}... | collective-permute-start | bytes 1105928 | tf_op jit(solution)/shard_map/ppermute | solution.py:351
  70.5 0.0 collective-permute-done.6.refs_7_
  70.5 0.8 collective-permute-done.4.refs_3_
  71.3 1.1 collective-permute-done.5.refs_4_
  72.4 0.0 copy-done.3
  72.4 6.0 %shard_map.66 = (bf16[8,720,128]{2,1,0:T(8,128)(2,1)S(1)}, bf16[384,5120]{1,0:T(8,128)(2,1)S(1)}, bf16[192,5120]{1,0:T(8,128)(2,1)S(1)}) custom-call(bf16[2,192,144]{2,1,0:T(8,128)(2,1)S(1)} %get-tuple-element.22.refs_0_, bf16[288,1280]{1,0:T(8,128)(2,1)S(1)} %bitcast.8, bf16[144,1280]{1,0:T(8,128)(2,1)S(1)} %collective-permute-done.refs_2_, ...), custom_call_target="tpu_custom_call" | custom-call | flops 1179648000 | bytes 8220672 | tf_op jit(solution)/shard_map/pallas_call | solution.py:27
  78.4 0.7 collective-permute-done.1.refs_1_
  79.1 0.0 collective-permute-done.3.refs_2_
  79.1 4.4 %shard_map.67 = bf16[8,720,128]{2,1,0:T(8,128)(2,1)S(1)} custom-call(bf16[2,192,144]{2,1,0:T(8,128)(2,1)S(1)} %get-tuple-element.22.refs_0_, bf16[144,1280]{1,0:T(8,128)(2,1)S(1)} %collective-permute-done.1.refs_1_, bf16[144,1280]{1,0:T(8,128)(2,1)S(1)} %collective-permute-done.3.refs_2_, ...), custom_call_target="tpu_custom_call", output_to_operand_aliasing={{}: (5, {})} | custom-call | flops 393216000 | bytes 8220672 | tf_op jit(solution)/shard_map/pallas_call | solution.py:27
  83.5 24.8 %all_to_all.15.refs_1_ = bf16[8,720,128]{2,1,0:T(8,128)(2,1)S(1)} all-to-all(bf16[8,720,128]{2,1,0:T(8,128)(2,1)S(1)} %shard_map.67), channel_id=1, replica_groups=mesh['group'=12,'member'=4,'y'=8,'core'=2] {'member','core'}, dimensions={0} | all-to-all | bytes 2949120 | tf_op jit(solution)/shard_map/all_to_all | solution.py:343
  108.3 0.0 copy-start.2
  108.3 0.6 shard_map.68
  108.9 32.9 %all_to_all.16 = bf16[96,16,128]{2,1,0:T(8,128)(2,1)S(1)} all-to-all(bf16[96,16,128]{2,1,0:T(8,128)(2,1)S(1)} %shard_map.68), channel_id=1, replica_groups=mesh['group'=12,'member'=4,'y'=8,'core'=2] {'y','group'}, dimensions={0} | all-to-all | bytes 786432 | tf_op jit(solution)/shard_map/all_to_all | solution.py:343
  141.8 0.0 copy-done.2
  141.8 1.3 shard_map.69
  (1 shorter events, 0.0 us)
Async XLA Ops:
  0.0 18.7 %copy-start = (bf16[1,2,96,5120]{3,2,1,0:T(8,128)(2,1)S(1)}, bf16[1,2,96,5120]{3,2,1,0:T(8,128)(2,1)}, u32[]{:S(2)}) copy-start(bf16[1,2,96,5120]{3,2,1,0:T(8,128)(2,1)} %param.10) | copy-start | bytes 5898244
  0.0 23.1 %copy-start.4 = (s32[96,6]{0,1:T(8,128)S(1)}, s32[96,6]{0,1:T(8,128)}, u32[]{:S(2)}) copy-start(s32[96,6]{0,1:T(8,128)} %param.9) | copy-start | bytes 6916
  3.6 45.1 %all-to-all-start = ((bf16[12,24,1280]{2,1,0:T(8,128)(2,1)}), bf16[12,24,1280]{2,1,0:T(8,128)(2,1)S(1)}, u32[]{:S(2)}, u32[]{:S(2)}) async-start(bf16[12,24,1280]{2,1,0:T(8,128)(2,1)} %bitcast.16), calls=%async_computation | async-start | bytes 1474560 | tf_op jit(solution)/shard_map/all_to_all | solution.py:343
  18.8 51.7 %collective-permute-start.6 = (bf16[192,5120]{1,0:T(8,128)(2,1)S(1)}, bf16[192,5120]{1,0:T(8,128)(2,1)}, u32[]{:S(2)}, u32[]{:S(2)}) collective-permute-start(bf16[192,5120]{1,0:T(8,128)(2,1)S(1)} %bitcast.9), channel_id=1, source_target_pairs={{0,1},{1,0},{2,3},{3,2},{4,5},{5,4},{6,7},{7,6},{8,9},{9,8},{10,11... | collective-permute-start | bytes 5898248 | tf_op jit(solution)/shard_map/ppermute | solution.py:360
  20.7 37.4 %collective-permute-start.7 = (bf16[96,5120]{1,0:T(8,128)(2,1)}, bf16[96,5120]{1,0:T(8,128)(2,1)}, u32[]{:S(2)}, u32[]{:S(2)}) collective-permute-start(bf16[96,5120]{1,0:T(8,128)(2,1)} %bitcast.12), channel_id=1, source_target_pairs={{0,1},{1,0},{2,3},{3,2},{4,5},{5,4},{6,7},{7,6},{8,9},{9,8},{10,11... | collective-permute-start | bytes 2949128 | tf_op jit(solution)/shard_map/ppermute | solution.py:360
  25.1 1.2 copy-start.1
  48.7 23.8 %copy-start.3 = (bf16[1,96,5120]{2,1,0:T(8,128)(2,1)S(1)}, bf16[1,96,5120]{2,1,0:T(8,128)(2,1)}, u32[]{:S(2)}) copy-start(bf16[1,96,5120]{2,1,0:T(8,128)(2,1)} %param.11) | copy-start | bytes 2949124
  48.7 14.7 %collective-permute-start = (bf16[144,1280]{1,0:T(8,128)(2,1)S(1)}, bf16[144,1280]{1,0:T(8,128)(2,1)S(1)}, u32[]{:S(2)}, u32[]{:S(2)}) collective-permute-start(bf16[144,1280]{1,0:T(8,128)(2,1)S(1)} %get-tuple-element.30), channel_id=1, source_target_pairs={{0,16},{1,49},{16,32},{17,1},{32,48},{33,17},{48,0},{49,33},{2,18}... | collective-permute-start | bytes 1105928 | tf_op jit(solution)/shard_map/ppermute | solution.py:351
  52.2 13.4 %collective-permute-start.2 = (bf16[144,1280]{1,0:T(8,128)(2,1)S(1)}, bf16[144,1280]{1,0:T(8,128)(2,1)S(1)}, u32[]{:S(2)}, u32[]{:S(2)}) collective-permute-start(bf16[144,1280]{1,0:T(8,128)(2,1)S(1)} %get-tuple-element.29), channel_id=1, source_target_pairs={{0,48},{1,17},{16,0},{17,33},{32,16},{33,49},{48,32},{49,1},{2,50}... | collective-permute-start | bytes 1105928 | tf_op jit(solution)/shard_map/ppermute | solution.py:351
  55.9 15.4 %collective-permute-start.4 = (bf16[144,1280]{1,0:T(8,128)(2,1)S(1)}, bf16[144,1280]{1,0:T(8,128)(2,1)S(1)}, u32[]{:S(2)}, u32[]{:S(2)}) collective-permute-start(bf16[144,1280]{1,0:T(8,128)(2,1)S(1)} %get-tuple-element.29), channel_id=1, source_target_pairs={{0,16},{1,49},{16,32},{17,1},{32,48},{33,17},{48,0},{49,33},{2,18}... | collective-permute-start | bytes 1105928 | tf_op jit(solution)/shard_map/ppermute | solution.py:351
  58.1 14.3 %collective-permute-start.5 = (bf16[144,1280]{1,0:T(8,128)(2,1)S(1)}, bf16[144,1280]{1,0:T(8,128)(2,1)S(1)}, u32[]{:S(2)}, u32[]{:S(2)}) collective-permute-start(bf16[144,1280]{1,0:T(8,128)(2,1)S(1)} %get-tuple-element.30), channel_id=1, source_target_pairs={{0,48},{1,17},{16,0},{17,33},{32,16},{33,49},{48,32},{49,1},{2,50}... | collective-permute-start | bytes 1105928 | tf_op jit(solution)/shard_map/ppermute | solution.py:351
  63.4 15.7 %collective-permute-start.1 = (bf16[144,1280]{1,0:T(8,128)(2,1)S(1)}, bf16[144,1280]{1,0:T(8,128)(2,1)S(1)}, u32[]{:S(2)}, u32[]{:S(2)}) collective-permute-start(bf16[144,1280]{1,0:T(8,128)(2,1)S(1)} %collective-permute-done.refs_2_), channel_id=1, source_target_pairs={{0,16},{1,49},{16,32},{17,1},{32,48},{33,17},{48,0},{49,33},{2,18}... | collective-permute-start | bytes 1105928 | tf_op jit(solution)/shard_map/ppermute | solution.py:351
  65.6 13.5 %collective-permute-start.3 = (bf16[144,1280]{1,0:T(8,128)(2,1)S(1)}, bf16[144,1280]{1,0:T(8,128)(2,1)S(1)}, u32[]{:S(2)}, u32[]{:S(2)}) collective-permute-start(bf16[144,1280]{1,0:T(8,128)(2,1)S(1)} %collective-permute-done.2.refs_5_), channel_id=1, source_target_pairs={{0,48},{1,17},{16,0},{17,33},{32,16},{33,49},{48,32},{49,1},{2,50}... | collective-permute-start | bytes 1105928 | tf_op jit(solution)/shard_map/ppermute | solution.py:351
  108.3 33.5 %copy-start.2 = (bf16[576,1536]{1,0:T(8,128)(2,1)S(1)}, bf16[576,1536]{1,0:T(8,128)(2,1)}, u32[]{:S(2)}) copy-start(bf16[576,1536]{1,0:T(8,128)(2,1)} %copy-done.1) | copy-start | bytes 5308420
